TPU v7x, 256 devices: a whole 4x4x8 slice. The times are simulated.
256 devices in a mesh: row: 16 (over x, y_hi, core), col: 16 (over z, y_lo).
Axes of the slice: x: 4, y: 4 (y_hi: 2, y_lo: 2; y = y_hi * 2 + y_lo), z: 8, core: 2. Of those that a mesh axis runs over, the one named last changes fastest.
Arguments:
- forward_fields: bfloat16 [4, 512, 512, 256], P(None, 'row', 'col'), may hold values from -6 to 6
- adjoint_now: float32 [512, 512, 256], P('row', 'col'), may hold values from -6 to 6
- adjoint_prev: float32 [512, 512, 256], P('row', 'col'), may hold values from -6 to 6
- courant_sq: float32 [512, 512, 256], P('row', 'col'), may hold values from 0.04 to 0.2
- receiver_cells: int32 [16, 16, 512], P('row', 'col'), may hold values from 0 to 262143
- traces: float32 [16, 16, 4, 512], P('row', 'col'), may hold values from -6 to 6
Outputs:
- smoothed: float32 [512, 512, 256], P('row', 'col')
- final_now: float32 [512, 512, 256], P('row', 'col')
- final_prev: float32 [512, 512, 256], P('row', 'col')
All inputs are finite; a program needn't handle non-finite values.
Results may differ from a plain program's by a relative error of at most 0.0003.
Values sent between devices are 32-bit elements; how exact they have to be, the bound alone decides.
No kernel may reach another device: no remote copies, remote signals or barrier semaphores. Data moves between devices by JAX's collectives and lax.ppermute only.
A program may use at most 64 MiB of HBM per device.

v0:
```python
import jax
import jax.numpy as jnp
from jax import lax
from jax.sharding import PartitionSpec as P

STEPS = 4
KX = 128
KY = 128
KZ = 64


def with_halo(cells, sides, width):
    for axis, dim in sides:
        count = lax.axis_size(axis)
        ends = count - 1
        head = lax.slice_in_dim(cells, 0, width, axis=dim)
        tail = lax.slice_in_dim(cells, cells.shape[dim] - width, cells.shape[dim], axis=dim)
        cells = jnp.concatenate(
            [
                lax.ppermute(tail, axis, [(i, (i + 1) % count) for i in range(ends)]),
                cells,
                lax.ppermute(head, axis, [((i + 1) % count, i) for i in range(ends)]),
            ],
            axis=dim,
        )
    return cells


def laplace(padded):
    center = padded[2:-2, 2:-2, 2:-2]
    total = -7.5 * center
    total = total + 4.0 / 3.0 * (padded[3:-1, 2:-2, 2:-2] + padded[1:-3, 2:-2, 2:-2])
    total = total - 1.0 / 12.0 * (padded[4:, 2:-2, 2:-2] + padded[:-4, 2:-2, 2:-2])
    total = total + 4.0 / 3.0 * (padded[2:-2, 3:-1, 2:-2] + padded[2:-2, 1:-3, 2:-2])
    total = total - 1.0 / 12.0 * (padded[2:-2, 4:, 2:-2] + padded[2:-2, :-4, 2:-2])
    total = total + 4.0 / 3.0 * (padded[2:-2, 2:-2, 3:-1] + padded[2:-2, 2:-2, 1:-3])
    total = total - 1.0 / 12.0 * (padded[2:-2, 2:-2, 4:] + padded[2:-2, 2:-2, :-4])
    return total


def basis_table(count, length, offset, span):
    cells = offset + jnp.arange(span, dtype=jnp.int32)[None, :]
    modes = jnp.arange(count, dtype=jnp.int32)[:, None]
    half = count // 2
    freq = jnp.where(modes < half, modes, modes - half + 1)
    phase = (freq * cells % length).astype(jnp.float32) * (2.0 * jnp.pi / length)
    scale = jnp.sqrt(2.0 / length)
    values = jnp.where(modes < half, scale * jnp.cos(phase), scale * jnp.sin(phase))
    values = jnp.where(modes == 0, jnp.sqrt(1.0 / length), values)
    values = jnp.where(modes == count - 1, 0.0, values)
    return values


def contract(form, left, right):
    return jnp.einsum(
        form, left, right, precision=lax.Precision.HIGHEST, preferred_element_type=jnp.float32
    )


def per_device(forward_fields, adjoint_now, adjoint_prev, courant_sq, receiver_cells, traces):
    cells_x, cells_y, depth = adjoint_now.shape
    full_x = cells_x * lax.axis_size("row")
    full_y = cells_y * lax.axis_size("col")
    shape = adjoint_now.shape
    flat_cells = receiver_cells.reshape(-1)
    gradient = jnp.zeros(shape, jnp.float32)
    now, prev = (adjoint_now, adjoint_prev)
    for step in range(STEPS):
        rimmed = with_halo(now, (("row", 0), ("col", 1)), 2)
        padded = jnp.pad(rimmed, ((0, 0), (0, 0), (2, 2)))
        lap = laplace(padded)
        gradient = gradient + forward_fields[step].astype(jnp.float32) * lap
        nxt = 2.0 * now - prev + courant_sq * lap
        nxt = nxt.reshape(-1).at[flat_cells].add(traces[0, 0, step, :]).reshape(shape)
        prev, now = (now, nxt)
    table_z = basis_table(KZ, depth, 0, depth)
    coef = contract("xyn,kn->kxy", gradient, table_z)
    table_y = basis_table(KY, full_y, lax.axis_index("col") * cells_y, cells_y)
    partial_y = contract("zxy,ky->zkx", coef, table_y)
    shared_y = lax.psum_scatter(partial_y, "col", scatter_dimension=1, tiled=True)
    table_x = basis_table(KX, full_x, lax.axis_index("row") * cells_x, cells_x)
    partial_x = contract("zkx,jx->zkj", shared_y, table_x)
    shared_x = lax.psum_scatter(partial_x, "row", scatter_dimension=2, tiled=True)
    all_x = lax.all_gather(shared_x, "row", axis=2, tiled=True)
    xback = contract("zkj,jx->zkx", all_x, table_x)
    all_y = lax.all_gather(xback, "col", axis=1, tiled=True)
    coef_back = contract("zkx,ky->zxy", all_y, table_y)
    smoothed = contract("kxy,kn->xyn", coef_back, table_z)
    return (smoothed, now, prev)


def solution(mesh):
    in_specs = (
        P(None, "row", "col", None),
        P("row", "col", None),
        P("row", "col", None),
        P("row", "col", None),
        P("row", "col", None),
        P("row", "col", None, None),
    )
    out_specs = (P("row", "col", None), P("row", "col", None), P("row", "col", None))
    return jax.shard_map(
        per_device, mesh=mesh, in_specs=in_specs, out_specs=out_specs, check_vma=False
    )
```

profile of v0, /device:TPU:16, one launch (start us, length us, event | category | flops | bytes accessed | tf_op | source)
XLA Modules:
  0.0 443.7 jit_solution(3990539196682417912)
XLA Ops:
  8.1 1.9 collective-permute-start.1
  10.0 5.1 %collective-permute-start = (f32[2,32,256]{2,1,0:T(8,128)S(1)}, f32[2,32,256]{2,1,0:T(8,128)S(1)}, u32[]{:S(2)}, u32[]{:S(2)}) collective-permute-start(f32[2,32,256]{2,1,0:T(8,128)S(1)} %get-tuple-element.37), channel_id=1, source_target_pairs={{16,0},{32,16},{48,32},{64,48},{80,64},{96,80},{112,96},{128,112},... | collective-permute-start | bytes 196616 | tf_op jit(solution)/shard_map/ppermute | solution.py:22
  16.7 1.6 constant_dynamic-update-slice_fusion.1
  18.4 1.3 collective-permute-start.2
  19.7 4.5 %collective-permute-start.3 = (f32[36,2,256]{2,1,0:T(2,128)S(1)}, f32[36,2,256]{2,1,0:T(2,128)S(1)}, u32[]{:S(2)}, u32[]{:S(2)}) collective-permute-start(f32[36,2,256]{2,1,0:T(2,128)S(1)} %get-tuple-element.17), channel_id=1, source_target_pairs={{0,1},{1,2},{2,3},{3,4},{4,5},{5,6},{6,7},{7,8},{8,9},{9,10},{10,1... | collective-permute-start | bytes 221192 | tf_op jit(solution)/shard_map/ppermute | solution.py:20
  25.1 1.7 collective-permute-done.3
  26.7 1.0 select_maximum_fusion.6
  27.7 3.3 multiply_add_fusion.3
  31.6 3.7 scatter_fusion
  35.4 2.2 collective-permute-start.5
  38.0 4.8 %collective-permute-start.4 = (f32[2,32,256]{2,1,0:T(8,128)S(1)}, f32[2,32,256]{2,1,0:T(8,128)S(1)}, u32[]{:S(2)}, u32[]{:S(2)}) collective-permute-start(f32[2,32,256]{2,1,0:T(8,128)S(1)} %slice.394), channel_id=1, source_target_pairs={{16,0},{32,16},{48,32},{64,48},{80,64},{96,80},{112,96},{128,112},... | collective-permute-start | bytes 196616 | tf_op jit(solution)/shard_map/ppermute | solution.py:22
  43.2 1.5 collective-permute-done.4
  44.8 1.3 collective-permute-start.6
  46.1 5.0 %collective-permute-start.7 = (f32[36,2,256]{2,1,0:T(2,128)S(1)}, f32[36,2,256]{2,1,0:T(2,128)S(1)}, u32[]{:S(2)}, u32[]{:S(2)}) collective-permute-start(f32[36,2,256]{2,1,0:T(2,128)S(1)} %get-tuple-element.15), channel_id=1, source_target_pairs={{0,1},{1,2},{2,3},{3,4},{4,5},{5,6},{6,7},{7,8},{8,9},{9,10},{10,1... | collective-permute-start | bytes 221192 | tf_op jit(solution)/shard_map/ppermute | solution.py:20
  51.5 1.6 collective-permute-done.7
  53.1 1.0 select_maximum_fusion.4
  54.1 3.3 multiply_add_fusion.2
  57.9 3.7 scatter_fusion.1
  61.7 5.1 %collective-permute-start.9 = (f32[2,32,256]{2,1,0:T(8,128)S(1)}, f32[2,32,256]{2,1,0:T(8,128)S(1)}, u32[]{:S(2)}, u32[]{:S(2)}) collective-permute-start(f32[2,32,256]{2,1,0:T(8,128)S(1)} %slice.417), channel_id=1, source_target_pairs={{0,16},{16,32},{32,48},{48,64},{64,80},{80,96},{96,112},{112,128},... | collective-permute-start | bytes 196616 | tf_op jit(solution)/shard_map/ppermute | solution.py:20
  67.2 2.0 collective-permute-start.8
  69.6 1.6 collective-permute-done.8
  71.2 1.3 collective-permute-start.10
  72.5 5.8 %collective-permute-start.11 = (f32[36,2,256]{2,1,0:T(2,128)S(1)}, f32[36,2,256]{2,1,0:T(2,128)S(1)}, u32[]{:S(2)}, u32[]{:S(2)}) collective-permute-start(f32[36,2,256]{2,1,0:T(2,128)S(1)} %get-tuple-element.13), channel_id=1, source_target_pairs={{0,1},{1,2},{2,3},{3,4},{4,5},{5,6},{6,7},{7,8},{8,9},{9,10},{10,1... | collective-permute-start | bytes 221192 | tf_op jit(solution)/shard_map/ppermute | solution.py:20
  78.5 1.6 collective-permute-done.11
  81.1 3.3 multiply_add_fusion.1
  85.0 3.7 scatter_fusion.2
  88.8 6.4 %collective-permute-start.13 = (f32[2,32,256]{2,1,0:T(8,128)S(1)}, f32[2,32,256]{2,1,0:T(8,128)S(1)}, u32[]{:S(2)}, u32[]{:S(2)}) collective-permute-start(f32[2,32,256]{2,1,0:T(8,128)S(1)} %slice.437), channel_id=1, source_target_pairs={{0,16},{16,32},{32,48},{48,64},{64,80},{80,96},{96,112},{112,128},... | collective-permute-start | bytes 196616 | tf_op jit(solution)/shard_map/ppermute | solution.py:20
  95.2 1.3 reshape.189
  96.5 1.9 collective-permute-start.12
  98.4 1.6 constant_dynamic-update-slice_fusion.22
  100.4 1.3 collective-permute-start.14
  101.7 5.2 %collective-permute-start.15 = (f32[36,2,256]{2,1,0:T(2,128)S(1)}, f32[36,2,256]{2,1,0:T(2,128)S(1)}, u32[]{:S(2)}, u32[]{:S(2)}) collective-permute-start(f32[36,2,256]{2,1,0:T(2,128)S(1)} %get-tuple-element.11), channel_id=1, source_target_pairs={{0,1},{1,2},{2,3},{3,4},{4,5},{5,6},{6,7},{7,8},{8,9},{9,10},{10,1... | collective-permute-start | bytes 221192 | tf_op jit(solution)/shard_map/ppermute | solution.py:20
  107.3 1.6 collective-permute-done.15
  109.9 2.5 multiply_add_fusion
  112.5 3.2 fusion.66
  115.6 1.9 convolution_bitcast_fusion
  117.5 2.9 copy.13
  120.7 88.4 %reduce-scatter.3.cloned.1.call-done = f32[64,8,32]{0,2,1:T(8,128)} async-done(((f32[64,128,32]{0,2,1:T(8,128)}), f32[64,8,32]{0,2,1:T(8,128)}) %reduce-scatter.3.cloned.1.call-update) | async-done | bytes 65552 | tf_op jit(solution)/shard_map/reduce_scatter | solution.py:80
  209.1 1.5 fusion.98
  210.6 1.0 copy.15
  211.7 74.0 %reduce-scatter.5.cloned.1.call-done = f32[64,8,8]{0,1,2:T(8,128)} async-done(((f32[64,8,128]{0,1,2:T(8,128)}), f32[64,8,8]{0,1,2:T(8,128)}) %reduce-scatter.5.cloned.1.call-update) | async-done | bytes 16400 | tf_op jit(solution)/shard_map/reduce_scatter | solution.py:83
  285.7 21.7 %all_gather.6 = f32[64,8,128]{0,1,2:T(8,128)S(1)} all-gather(f32[64,8,8]{0,1,2:T(8,128)} %reduce-scatter.5.cloned.1.call-done), channel_id=1, replica_groups=mesh['row'=16,'col'=16] {'row'}, dimensions={2}, use_global_device_ids=true | all-gather | bytes 278528 | tf_op jit(solution)/shard_map/all_gather | solution.py:84
  307.7 1.2 fusion.96
  309.4 3.7 scatter_fusion.3
  313.2 1.3 reshape.191
  314.4 110.9 %all-gather.2.cloned.1.call-done = f32[64,128,32]{2,1,0:T(8,128)} async-done(((f32[64,8,32]{2,1,0:T(8,128)}), f32[64,128,32]{2,1,0:T(8,128)}) %all-gather.2.cloned.1.call-update) | async-done | bytes 1048592 | tf_op jit(solution)/shard_map/all_gather | solution.py:86
  425.4 8.5 %fusion.100 = f32[64,32,32]{2,1,0:T(8,128)S(1)} fusion(f32[64,128,32]{2,1,0:T(8,128)} %all-gather.2.cloned.1.call-done, s32[32]{0:T(128)S(1)} %iota_add_fusion.1, s32[128]{0:T(128)S(1)} %add_select_fusion.4, pred[128]{0:T(512)(128)(4,1)S(1)} %get-tuple-element.61, pred[128]{0:T(512)(128)(4,1)S(1)} %get-tuple-element.62, ...), kind=kOutput, calls=%fused_computation.202 | convolution fusion | flops 100741120 | bytes 1311744 | tf_op jit(solution)/shard_map/zkx,ky->zxy/dot_general | solution.py:55
  433.8 3.4 fusion.72
  (79 shorter events, 10.9 us)
Async XLA Ops:
  7.2 201.9 %reduce-scatter.3.cloned.1.call-start = ((), (), s32[]{:S(2)}) async-start(), calls=%async_computation.2 | async-start | bytes 2228224 | tf_op jit(solution)/shard_map/reduce_scatter | solution.py:80
  8.1 8.6 %collective-permute-start.1 = (f32[2,32,256]{2,1,0:T(8,128)S(1)}, f32[2,32,256]{2,1,0:T(8,128)S(1)}, u32[]{:S(2)}, u32[]{:S(2)}) collective-permute-start(f32[2,32,256]{2,1,0:T(8,128)S(1)} %get-tuple-element.38), channel_id=1, source_target_pairs={{0,16},{16,32},{32,48},{48,64},{64,80},{80,96},{96,112},{112,128},... | collective-permute-start | bytes 196616 | tf_op jit(solution)/shard_map/ppermute | solution.py:20
  10.0 8.3 %collective-permute-start = (f32[2,32,256]{2,1,0:T(8,128)S(1)}, f32[2,32,256]{2,1,0:T(8,128)S(1)}, u32[]{:S(2)}, u32[]{:S(2)}) collective-permute-start(f32[2,32,256]{2,1,0:T(8,128)S(1)} %get-tuple-element.37), channel_id=1, source_target_pairs={{16,0},{32,16},{48,32},{64,48},{80,64},{96,80},{112,96},{128,112},... | collective-permute-start | bytes 196616 | tf_op jit(solution)/shard_map/ppermute | solution.py:22
  18.4 6.6 %collective-permute-start.2 = (f32[36,2,256]{2,1,0:T(2,128)S(1)}, f32[36,2,256]{2,1,0:T(2,128)S(1)}, u32[]{:S(2)}, u32[]{:S(2)}) collective-permute-start(f32[36,2,256]{2,1,0:T(2,128)S(1)} %get-tuple-element.18), channel_id=1, source_target_pairs={{1,0},{2,1},{3,2},{4,3},{5,4},{6,5},{7,6},{8,7},{9,8},{10,9},{11,1... | collective-permute-start | bytes 221192 | tf_op jit(solution)/shard_map/ppermute | solution.py:22
  19.7 7.0 %collective-permute-start.3 = (f32[36,2,256]{2,1,0:T(2,128)S(1)}, f32[36,2,256]{2,1,0:T(2,128)S(1)}, u32[]{:S(2)}, u32[]{:S(2)}) collective-permute-start(f32[36,2,256]{2,1,0:T(2,128)S(1)} %get-tuple-element.17), channel_id=1, source_target_pairs={{0,1},{1,2},{2,3},{3,4},{4,5},{5,6},{6,7},{7,8},{8,9},{9,10},{10,1... | collective-permute-start | bytes 221192 | tf_op jit(solution)/shard_map/ppermute | solution.py:20
  24.3 3.4 copy-start
  24.3 3.4 copy-start.3
  24.3 3.4 copy-start.9
  35.4 7.4 %collective-permute-start.5 = (f32[2,32,256]{2,1,0:T(8,128)S(1)}, f32[2,32,256]{2,1,0:T(8,128)S(1)}, u32[]{:S(2)}, u32[]{:S(2)}) collective-permute-start(f32[2,32,256]{2,1,0:T(8,128)S(1)} %slice.397), channel_id=1, source_target_pairs={{0,16},{16,32},{32,48},{48,64},{64,80},{80,96},{96,112},{112,128},... | collective-permute-start | bytes 196616 | tf_op jit(solution)/shard_map/ppermute | solution.py:20
  38.0 16.1 %copy-start.1 = (f32[32,32,256]{2,1,0:T(8,128)}, f32[32,32,256]{2,1,0:T(8,128)S(1)}, u32[]{:S(2)}) copy-start(f32[32,32,256]{2,1,0:T(8,128)S(1)} %reshape.185) | copy-start | bytes 3145732
  38.0 6.7 %collective-permute-start.4 = (f32[2,32,256]{2,1,0:T(8,128)S(1)}, f32[2,32,256]{2,1,0:T(8,128)S(1)}, u32[]{:S(2)}, u32[]{:S(2)}) collective-permute-start(f32[2,32,256]{2,1,0:T(8,128)S(1)} %slice.394), channel_id=1, source_target_pairs={{16,0},{32,16},{48,32},{64,48},{80,64},{96,80},{112,96},{128,112},... | collective-permute-start | bytes 196616 | tf_op jit(solution)/shard_map/ppermute | solution.py:22
  44.8 6.7 %collective-permute-start.6 = (f32[36,2,256]{2,1,0:T(2,128)S(1)}, f32[36,2,256]{2,1,0:T(2,128)S(1)}, u32[]{:S(2)}, u32[]{:S(2)}) collective-permute-start(f32[36,2,256]{2,1,0:T(2,128)S(1)} %get-tuple-element.16), channel_id=1, source_target_pairs={{1,0},{2,1},{3,2},{4,3},{5,4},{6,5},{7,6},{8,7},{9,8},{10,9},{11,1... | collective-permute-start | bytes 221192 | tf_op jit(solution)/shard_map/ppermute | solution.py:22
  46.1 7.0 %collective-permute-start.7 = (f32[36,2,256]{2,1,0:T(2,128)S(1)}, f32[36,2,256]{2,1,0:T(2,128)S(1)}, u32[]{:S(2)}, u32[]{:S(2)}) collective-permute-start(f32[36,2,256]{2,1,0:T(2,128)S(1)} %get-tuple-element.15), channel_id=1, source_target_pairs={{0,1},{1,2},{2,3},{3,4},{4,5},{5,6},{6,7},{7,8},{8,9},{9,10},{10,1... | collective-permute-start | bytes 221192 | tf_op jit(solution)/shard_map/ppermute | solution.py:20
  51.1 2.9 copy-start.4
  61.7 7.4 %collective-permute-start.9 = (f32[2,32,256]{2,1,0:T(8,128)S(1)}, f32[2,32,256]{2,1,0:T(8,128)S(1)}, u32[]{:S(2)}, u32[]{:S(2)}) collective-permute-start(f32[2,32,256]{2,1,0:T(8,128)S(1)} %slice.417), channel_id=1, source_target_pairs={{0,16},{16,32},{32,48},{48,64},{64,80},{80,96},{96,112},{112,128},... | collective-permute-start | bytes 196616 | tf_op jit(solution)/shard_map/ppermute | solution.py:20
  67.2 4.0 collective-permute-start.8
  71.2 7.3 %collective-permute-start.10 = (f32[36,2,256]{2,1,0:T(2,128)S(1)}, f32[36,2,256]{2,1,0:T(2,128)S(1)}, u32[]{:S(2)}, u32[]{:S(2)}) collective-permute-start(f32[36,2,256]{2,1,0:T(2,128)S(1)} %get-tuple-element.14), channel_id=1, source_target_pairs={{1,0},{2,1},{3,2},{4,3},{5,4},{6,5},{7,6},{8,7},{9,8},{10,9},{11,1... | collective-permute-start | bytes 221192 | tf_op jit(solution)/shard_map/ppermute | solution.py:22
  72.5 7.6 %collective-permute-start.11 = (f32[36,2,256]{2,1,0:T(2,128)S(1)}, f32[36,2,256]{2,1,0:T(2,128)S(1)}, u32[]{:S(2)}, u32[]{:S(2)}) collective-permute-start(f32[36,2,256]{2,1,0:T(2,128)S(1)} %get-tuple-element.13), channel_id=1, source_target_pairs={{0,1},{1,2},{2,3},{3,4},{4,5},{5,6},{6,7},{7,8},{8,9},{9,10},{10,1... | collective-permute-start | bytes 221192 | tf_op jit(solution)/shard_map/ppermute | solution.py:20
  78.3 2.8 copy-start.2
  88.8 9.6 %collective-permute-start.13 = (f32[2,32,256]{2,1,0:T(8,128)S(1)}, f32[2,32,256]{2,1,0:T(8,128)S(1)}, u32[]{:S(2)}, u32[]{:S(2)}) collective-permute-start(f32[2,32,256]{2,1,0:T(8,128)S(1)} %slice.437), channel_id=1, source_target_pairs={{0,16},{16,32},{32,48},{48,64},{64,80},{80,96},{96,112},{112,128},... | collective-permute-start | bytes 196616 | tf_op jit(solution)/shard_map/ppermute | solution.py:20
  96.5 3.8 collective-permute-start.12
  100.4 6.9 %collective-permute-start.14 = (f32[36,2,256]{2,1,0:T(2,128)S(1)}, f32[36,2,256]{2,1,0:T(2,128)S(1)}, u32[]{:S(2)}, u32[]{:S(2)}) collective-permute-start(f32[36,2,256]{2,1,0:T(2,128)S(1)} %get-tuple-element.12), channel_id=1, source_target_pairs={{1,0},{2,1},{3,2},{4,3},{5,4},{6,5},{7,6},{8,7},{9,8},{10,9},{11,1... | collective-permute-start | bytes 221192 | tf_op jit(solution)/shard_map/ppermute | solution.py:22
  101.7 7.2 %collective-permute-start.15 = (f32[36,2,256]{2,1,0:T(2,128)S(1)}, f32[36,2,256]{2,1,0:T(2,128)S(1)}, u32[]{:S(2)}, u32[]{:S(2)}) collective-permute-start(f32[36,2,256]{2,1,0:T(2,128)S(1)} %get-tuple-element.11), channel_id=1, source_target_pairs={{0,1},{1,2},{2,3},{3,4},{4,5},{5,6},{6,7},{7,8},{8,9},{9,10},{10,1... | collective-permute-start | bytes 221192 | tf_op jit(solution)/shard_map/ppermute | solution.py:20
  106.9 2.9 copy-start.5
  109.8 2.6 copy-start.6
  109.8 2.6 copy-start.7
  109.9 2.6 copy-start.8
  120.4 165.3 %reduce-scatter.5.cloned.1.call-start = ((), (), s32[]{:S(2)}) async-start(), calls=%async_computation.3 | async-start | bytes 557056 | tf_op jit(solution)/shard_map/reduce_scatter | solution.py:83
  211.6 213.7 %all-gather.2.cloned.1.call-start = ((), (), s32[]{:S(2)}) async-start(), calls=%async_computation.4 | async-start | bytes 4456448 | tf_op jit(solution)/shard_map/all_gather | solution.py:86
Sparse Core Ops, SparseCore 0:
  120.5 88.5 reduce-scatter.2
  213.7 72.0 reduce-scatter.4
  309.0 116.3 all-gather.1
where the time goes:
time: 448 us; the launch traced here: 444 us
  waiting for transfers between devices  285 us (64%)
  starting transfers between devices  55.6 us (12%)
  other arithmetic  32.1 us (7%)
  blocking collectives  21.7 us (5%)
  matrix products  19.6 us (4%)
  local copies, waits for them, and re-layouts  15.6 us (3%)
  between operations  14.4 us (3%)
    all_gather x1, waiting for transfers between devices, per_device(): all_y = lax.all_gather(xback, 'col', axis=1, tiled=True)  111 us
    reduce_scatter x1, waiting for transfers between devices, per_device(): lax.psum_scatter(partial_y, 'col', scatter_dimension=1, tiled=True)  88.4 us
    reduce_scatter x1, waiting for transfers between devices, per_device(): lax.psum_scatter(partial_x, 'row', scatter_dimension=2, tiled=True)  74 us
    ppermute x8, starting transfers between devices, with_halo(): lax.ppermute(tail, axis, [(i, (i + 1) % count) for i in range(ends)])  36.2 us
    all_gather x1, blocking collectives, per_device(): all_x = lax.all_gather(shared_x, 'row', axis=2, tiled=True)  21.7 us
    dot_general x6, matrix products, contract(): jnp.einsum(form, left, right, precision=lax.Precision.HIGHEST, preferred_...  19.6 us
    ppermute x8, starting transfers between devices, with_halo(): lax.ppermute(head, axis, [((i + 1) % count, i) for i in range(ends)])  19 us
    scatter-add x4, other arithmetic, per_device(): nxt.reshape(-1).at[flat_cells].add(traces[0, 0, step, :]).reshape(shape)  14.9 us
  transfers between devices with their start and end apart: 19, of which 14 were waited for; matrix products, arithmetic and copies ran while one was open for 3% of the time, Pallas kernels for 0%

commit v1 on v0

v1 whole, which is shorter than its diff:
```python
import functools

import jax
import jax.numpy as jnp
import numpy as np
from jax import lax
from jax.experimental import pallas as pl
from jax.experimental.pallas import tpu as pltpu
from jax.sharding import PartitionSpec as P

STEPS = 4
KX = 128
KY = 128
KZ = 64
GROUP = 4
ROWS = 256
TWELFTH = 1.0 / 12.0

HBM = pl.BlockSpec(memory_space=pltpu.HBM)
VMEM = pl.BlockSpec(memory_space=pltpu.VMEM)
SMEM = pl.BlockSpec(memory_space=pltpu.SMEM)
DMA = pltpu.SemaphoreType.DMA
NT = (((1,), (1,)), ((), ()))
NN = (((1,), (0,)), ((), ()))
TN = (((0,), (0,)), ((), ()))


def split(value):
    high = value.astype(jnp.bfloat16)
    low = (value - high.astype(jnp.float32)).astype(jnp.bfloat16)
    return high, low


def dot(left, right, dims):
    return lax.dot_general(left, right, dims, preferred_element_type=jnp.float32)


def dot3(left, right, dims):
    return (
        dot(left[0], right[0], dims)
        + dot(left[1], right[0], dims)
        + dot(left[0], right[1], dims)
    )


def basis(count, length):
    half = count // 2
    cells = np.arange(length, dtype=np.int64)[None, :]
    modes = np.arange(count, dtype=np.int64)[:, None]
    freq = np.where(modes < half, modes, modes - half + 1)
    phase = (freq * cells % length) * (2.0 * np.pi / length)
    values = np.sqrt(2.0 / length) * np.where(modes < half, np.cos(phase), np.sin(phase))
    values[0] = np.sqrt(1.0 / length)
    values[count - 1] = 0.0
    return values


def bands(size_y, size_z):
    def far(size):
        one = lax.broadcasted_iota(jnp.int32, (size, size), 0)
        two = lax.broadcasted_iota(jnp.int32, (size, size), 1)
        return jnp.abs(one - two), one // size_y == two // size_y

    gap, _ = far(size_z)
    band_z = jnp.where(gap == 0, -90.0, jnp.where(gap == 1, 16.0, jnp.where(gap == 2, -1.0, 0.0)))
    gap, same = far(ROWS)
    band_y = jnp.where(gap == 1, 16.0, jnp.where(gap == 2, -1.0, 0.0))
    band_y = jnp.where(same, band_y, 0.0)
    return band_z.astype(jnp.bfloat16), band_y.astype(jnp.bfloat16)


def pack(now, x_low, x_high, y_low, y_high, first, last, sems):
    size_x, size_y, _ = now.shape
    copies = [
        pltpu.make_async_copy(now.at[0:2], x_low, sems.at[0]),
        pltpu.make_async_copy(now.at[size_x - 2 : size_x], x_high, sems.at[1]),
        pltpu.make_async_copy(now.at[:, 0:8], first, sems.at[2]),
        pltpu.make_async_copy(now.at[:, size_y - 8 : size_y], last, sems.at[3]),
    ]
    for copy in copies:
        copy.start()
    for copy in copies:
        copy.wait()
    y_low[...] = first[:, 0:2, :]
    y_high[...] = last[:, 6:8, :]


def x_changes(inside, x_low, x_high, size_x):
    before = [jnp.where(inside[0] > 0, x_low[i], 0.0) for i in range(2)]
    after = [jnp.where(inside[1] > 0, x_high[i], 0.0) for i in range(2)]
    return {
        0: 16.0 * before[1] - before[0],
        1: -before[1],
        size_x - 2: -after[0],
        size_x - 1: 16.0 * after[0] - after[1],
    }


def y_tiles(inside, y_low, y_high, x):
    size_z = y_low.shape[2]
    line = lax.broadcasted_iota(jnp.int32, (8, size_z), 0)
    low = jnp.where(inside[2] > 0, y_low[x], 0.0)
    near = jnp.broadcast_to(low[1:2], (8, size_z))
    far = jnp.broadcast_to(low[0:1], (8, size_z))
    first = jnp.where(line == 0, 16.0 * near - far, jnp.where(line == 1, -near, 0.0))
    high = jnp.where(inside[3] > 0, y_high[x], 0.0)
    near = jnp.broadcast_to(high[0:1], (8, size_z))
    far = jnp.broadcast_to(high[1:2], (8, size_z))
    last = jnp.where(line == 7, 16.0 * near - far, jnp.where(line == 6, -near, 0.0))
    return first, last


def with_change(value, x, x_change, tiles):
    size_y = value.shape[0]
    parts = [value[0:8] + tiles[0], value[8 : size_y - 8], value[size_y - 8 : size_y] + tiles[1]]
    value = jnp.concatenate(parts, axis=0)
    return value + x_change[x] if x in x_change else value


def faces_after(inside, x_low, x_high, y_low, y_high, courant, base, lap, out_x_low, out_x_high, out_y_low, out_y_high):
    size_x, size_y, _ = base.shape
    x_change = x_changes(inside, x_low, x_high, size_x)
    for x in range(size_x):
        tiles = y_tiles(inside, y_low, y_high, x)
        if x in x_change:
            value = with_change(lap[x], x, x_change, tiles)
            value = base[x] + (courant[x] * TWELFTH) * value
            out = out_x_low if x < 2 else out_x_high
            out[x % 2] = value
            first, last = value[0:8], value[size_y - 8 : size_y]
        else:
            first = base[x, 0:8] + (courant[x, 0:8] * TWELFTH) * (lap[x, 0:8] + tiles[0])
            end = slice(size_y - 8, size_y)
            last = base[x, end] + (courant[x, end] * TWELFTH) * (lap[x, end] + tiles[1])
        out_y_low[x] = first[0:2]
        out_y_high[x] = last[6:8]


def injection(step, cells, traces, size_z):
    spots = cells[...]
    value = traces[pl.ds(step, 1), :]
    top = value.astype(jnp.bfloat16)
    rest = value - top.astype(jnp.float32)
    mid = rest.astype(jnp.bfloat16)
    low = (rest - mid.astype(jnp.float32)).astype(jnp.bfloat16)
    depth = lax.broadcasted_iota(jnp.int32, (size_z, spots.shape[1]), 0)
    here = depth == spots % size_z
    parts = [
        jnp.where(here, part.astype(jnp.float32), 0.0).astype(jnp.bfloat16)
        for part in (top, mid, low)
    ]
    line = lax.broadcasted_iota(jnp.int32, (ROWS, spots.shape[1]), 0)

    def block(first_row):
        hits = jnp.where(line == spots // size_z - first_row, 1.0, 0.0).astype(jnp.bfloat16)
        return sum(dot(hits, part, NT) for part in parts)

    return block


def laplace_block(now, first, layers, band_z, band_y):
    size_x, size_y, size_z = now.shape
    center = now[first : first + layers].reshape(ROWS, size_z)
    high, low = split(center)
    lap = dot(high, band_z, NN) + dot(low, band_z, NN)
    lap = lap + dot(band_y, high, NN) + dot(band_y, low, NN)
    lap = lap.reshape(layers, size_y, size_z)
    out = []
    for layer in range(layers):
        x = first + layer
        near = [now[x + d] for d in (-1, 1) if 0 <= x + d < size_x]
        far = [now[x + d] for d in (-2, 2) if 0 <= x + d < size_x]
        value = lap[layer] + 16.0 * functools.reduce(jnp.add, near)
        out.append(value - functools.reduce(jnp.add, far))
    return out


def first_step(now_hbm, prev_hbm, courant_hbm, forward_hbm, cells, traces, now, courant, forward, base, lap, prev, sems):
    size_x, size_y, size_z = now.shape
    layers = ROWS // size_y
    blocks = size_x // layers
    copies = []
    for source, target, row in ((now_hbm, now, 0), (prev_hbm, prev, 1)):
        for b in range(blocks):
            part = pl.ds(b * layers, layers)
            copies.append(pltpu.make_async_copy(source.at[part], target.at[part], sems.at[row, b]))
    others = [
        pltpu.make_async_copy(courant_hbm, courant, sems.at[2, 0]),
        pltpu.make_async_copy(forward_hbm.at[0], forward, sems.at[2, 1]),
    ]
    for b in range(blocks):
        copies[b].start()
        copies[blocks + b].start()
    for copy in others:
        copy.start()
    band_z, band_y = bands(size_y, size_z)
    added = injection(0, cells, traces, size_z)
    copies[0].wait()
    for b in range(blocks):
        if b + 1 < blocks:
            copies[b + 1].wait()
        copies[blocks + b].wait()
        inject = added(b * ROWS).reshape(layers, size_y, size_z)
        for i, value in enumerate(laplace_block(now, b * layers, layers, band_z, band_y)):
            x = b * layers + i
            lap[x] = value
            base[x] = (2.0 * now[x] - prev[x]) + inject[i]
    for copy in others:
        copy.wait()


def later_step(step, has_gradient, *refs):
    inside, x_low, x_high, y_low, y_high, base_in, lap_in, prev, courant, forward_in, forward_hbm, cells, traces, *refs = refs
    gradient_in = refs.pop(0) if has_gradient else None
    last = step == STEPS - 1
    if last:
        now, lap, gradient, forward, sem = refs
    else:
        now, lap, gradient, forward, base, sem = refs
    size_x, size_y, size_z = now.shape
    layers = ROWS // size_y
    copy = pltpu.make_async_copy(forward_hbm.at[step], forward, sem)
    copy.start()
    band_z, band_y = bands(size_y, size_z)
    x_change = x_changes(inside, x_low, x_high, size_x)
    for x in range(size_x):
        value = with_change(lap_in[x], x, x_change, y_tiles(inside, y_low, y_high, x))
        now[x] = base_in[x] + (courant[x] * TWELFTH) * value
        value = forward_in[x].astype(jnp.float32) * value
        gradient[x] = gradient_in[x] + value if has_gradient else value
    added = None if last else injection(step, cells, traces, size_z)
    if last:
        copy.wait()
    for b in range(size_x // layers):
        inject = None if last else added(b * ROWS).reshape(layers, size_y, size_z)
        for i, value in enumerate(laplace_block(now, b * layers, layers, band_z, band_y)):
            x = b * layers + i
            lap[x] = value
            if last:
                gradient[x] += forward[x].astype(jnp.float32) * value
            else:
                base[x] = (2.0 * now[x] - prev[x]) + inject[i]
    if not last:
        copy.wait()


def finish(inside, x_low, x_high, y_low, y_high, now, lap, prev, courant, cells, traces, next_hbm, now_hbm, nxt, sems):
    size_x, size_y, size_z = now.shape
    layers = ROWS // size_y
    keep = pltpu.make_async_copy(now, now_hbm, sems.at[0])
    keep.start()
    added = injection(STEPS - 1, cells, traces, size_z)
    x_change = x_changes(inside, x_low, x_high, size_x)
    copies = []
    for b in range(size_x // layers):
        inject = added(b * ROWS).reshape(layers, size_y, size_z)
        for i in range(layers):
            x = b * layers + i
            value = with_change(lap[x], x, x_change, y_tiles(inside, y_low, y_high, x))
            base = (2.0 * now[x] - prev[x]) + inject[i]
            nxt[x] = base + (courant[x] * TWELFTH) * value
        part = pl.ds(b * layers, layers)
        copies.append(pltpu.make_async_copy(nxt.at[part], next_hbm.at[part], sems.at[1 + b]))
        copies[-1].start()
    for copy in copies:
        copy.wait()
    keep.wait()


def project_z(inside, x_low, x_high, y_low, y_high, forward, gradient, table_z, coef):
    size_x, size_y, _ = gradient.shape
    table = split(table_z[...])
    x_change = x_changes(inside, x_low, x_high, size_x)
    for s in range(8):
        lines = []
        for x in range(s, size_x, 8):
            first, last = y_tiles(inside, y_low, y_high, x)
            scale = forward[x].astype(jnp.float32)
            tiles = (scale[0:8] * first, scale[size_y - 8 : size_y] * last)
            value = with_change(gradient[x], x, {}, tiles)
            lines.append(value + scale * x_change[x] if x in x_change else value)
        coef[:, s, :] = dot3(table, split(jnp.concatenate(lines, axis=0)), NT)


def project_y(chunks, table_y, out, plane):
    count = chunks.shape[0] // GROUP
    for r in range(GROUP):
        for q in range(4):
            pieces = [chunks[r * count + c][:, q * 32 : (q + 1) * 32] for c in range(count)]
            plane[pl.ds((r * 4 + q) * 8, 8), :] = jnp.concatenate(pieces, axis=1)
    out[...] = dot3(split(plane[...]), split(table_y[...]), NT)


def smooth_plane(own, one, two, three, table_x, table_y, chunks, plane):
    total = None
    for k, part in enumerate((own, one, two, three)):
        term = dot3(split(table_x[k]), split(part[...]), NN)
        total = term if total is None else total + term
    plane[...] = dot3(split(total), split(table_y[...]), NN)
    count = chunks.shape[0] // GROUP
    for r in range(GROUP):
        for c in range(count):
            pieces = [plane[pl.ds((r * 4 + q) * 8, 8), c * 32 : (c + 1) * 32] for q in range(4)]
            chunks[r * count + c] = jnp.concatenate(pieces, axis=1)


def expand_z(coef, table_z, out, lines, sems):
    _, size_y, size_z = out.shape
    high, low = split(table_z[...])
    table = jnp.concatenate([high, high, low], axis=0)
    copies = []
    for s in range(8):
        high, low = split(coef[:, s, :])
        value = dot(jnp.concatenate([high, low, high], axis=0), table, TN)
        lines[s] = value.reshape(4, size_y, size_z)
        for q in range(4):
            copies.append(pltpu.make_async_copy(lines.at[s, q], out.at[q * 8 + s], sems.at[s, q]))
            copies[-1].start()
    for copy in copies:
        copy.wait()


def call(kernel, out_shape, specs, out_specs=None, scratch=(), room=24, **cost):
    return pl.pallas_call(
        kernel,
        out_shape=out_shape,
        in_specs=specs,
        out_specs=out_specs or jax.tree.map(lambda _: VMEM, out_shape),
        scratch_shapes=scratch,
        compiler_params=pltpu.CompilerParams(vmem_limit_bytes=int(room * 2**20)),
        cost_estimate=pl.CostEstimate(transcendentals=0, **cost),
    )


def per_device(forward_fields, adjoint_now, adjoint_prev, courant_sq, receiver_cells, traces):
    shape = adjoint_now.shape
    size_x, size_y, size_z = shape
    rows, cols = lax.axis_size("row"), lax.axis_size("col")
    row, col = lax.axis_index("row"), lax.axis_index("col")
    inside = jnp.stack([row > 0, row < rows - 1, col > 0, col < cols - 1]).astype(jnp.int32)
    spots = receiver_cells.reshape(1, -1)
    values = traces.reshape(STEPS, -1)
    basis_z = basis(KZ, size_z)
    table_z = jnp.asarray(basis_z, jnp.float32)
    table_z_scaled = jnp.asarray(basis_z * TWELFTH, jnp.float32)
    table_y = jnp.asarray(basis(KY, cols * size_y), jnp.float32)
    basis_x = basis(KX, rows * size_x)
    low_pass = basis_x.T @ basis_x
    own = GROUP * size_x
    parts = rows // GROUP
    table_x = jnp.asarray(
        np.stack([low_pass[:own, k * own : (k + 1) * own] for k in range(parts)]), jnp.float32
    )

    field = jax.ShapeDtypeStruct(shape, jnp.float32)
    half_field = jax.ShapeDtypeStruct(shape, jnp.bfloat16)
    x_face = jax.ShapeDtypeStruct((2, size_y, size_z), jnp.float32)
    y_face = jax.ShapeDtypeStruct((size_x, 2, size_z), jnp.float32)
    chunks = jax.ShapeDtypeStruct((KZ, 8, 128), jnp.float32)
    ring = [[(i, (i + 1) % n) for i in range(n)] for n in (rows, cols)]
    back = [[(b, a) for a, b in pairs] for pairs in ring]
    heavy = dict(flops=2 * 10**9, bytes_accessed=7 * 2**20)
    light = dict(flops=10**6, bytes_accessed=2**18)
    strip = pltpu.VMEM((size_x, 8, size_z), jnp.float32)
    whole = pltpu.VMEM(shape, jnp.float32)
    blocks = size_x * size_y // ROWS

    faces = call(
        pack, (x_face, x_face, y_face, y_face), [HBM], scratch=[strip, strip, DMA((4,))], room=57, **light
    )(adjoint_now)
    halo = gradient = prev = None
    for step in range(STEPS):
        sent = (
            lax.ppermute(faces[1], "row", ring[0]),
            lax.ppermute(faces[0], "row", back[0]),
            lax.ppermute(faces[3], "col", ring[1]),
            lax.ppermute(faces[2], "col", back[1]),
        )
        if step == 0:
            now, courant, forward, base, lap = call(
                first_step,
                (field, field, half_field, field, field),
                [HBM] * 4 + [VMEM] * 2,
                scratch=[whole, DMA((3, blocks))],
                room=49,
                **heavy,
            )(adjoint_now, adjoint_prev, courant_sq, forward_fields, spots, values)
        else:
            last = step == STEPS - 1
            operands = (inside, *halo, base, lap, now, courant, forward, forward_fields, spots, values)
            specs = [SMEM] + [VMEM] * 9 + [HBM] + [VMEM] * 2
            if step > 1:
                operands, specs = operands + (gradient,), specs + [VMEM]
            prev = now
            results = call(
                functools.partial(later_step, step, step > 1),
                (field, field, field, half_field) + (() if last else (field,)),
                specs,
                scratch=[DMA(())],
                **heavy,
            )(*operands)
            now, lap, gradient, forward = results[:4]
            base = None if last else results[4]
        halo = sent
        if step < STEPS - 1:
            faces = call(
                faces_after, (x_face, x_face, y_face, y_face), [SMEM] + [VMEM] * 7, **light
            )(inside, *halo, courant, base, lap)
    coef = call(project_z, chunks, [SMEM] + [VMEM] * 7, **light)(
        inside, *halo, forward, gradient, table_z_scaled
    )
    final_now, final_prev = call(
        finish,
        (field, field),
        [SMEM] + [VMEM] * 10,
        out_specs=(HBM, HBM),
        scratch=[whole, DMA((1 + blocks,))],
        **heavy,
    )(inside, *halo, now, lap, prev, courant, spots, values)

    groups = [
        [(g * GROUP + r) * cols + c for r in range(GROUP) for c in range(cols)] for g in range(parts)
    ]
    both = ("row", "col")
    coef = lax.all_to_all(coef, both, 0, 0, axis_index_groups=groups, tiled=True)
    plane = jax.ShapeDtypeStruct((own, KY), jnp.float32)
    wide = pltpu.VMEM((own, cols * size_y), jnp.float32)
    mine = call(project_y, plane, [VMEM] * 2, scratch=[wide], **light)(coef, table_y)
    others = [
        lax.ppermute(mine, "row", [((i + k * GROUP) % rows, i) for i in range(rows)])
        for k in range(1, parts)
    ]
    coef = call(smooth_plane, chunks, [VMEM] * 6, scratch=[wide], **light)(
        mine, *others, table_x, table_y
    )
    coef = lax.all_to_all(coef, both, 0, 0, axis_index_groups=groups, tiled=True)
    smoothed = call(
        expand_z,
        field,
        [VMEM] * 2,
        out_specs=HBM,
        scratch=[pltpu.VMEM((8, 4, size_y, size_z), jnp.float32), DMA((8, 4))],
        **light,
    )(coef, table_z)
    return (smoothed, final_now, final_prev)


def solution(mesh):
    in_specs = (
        P(None, "row", "col", None),
        P("row", "col", None),
        P("row", "col", None),
        P("row", "col", None),
        P("row", "col", None),
        P("row", "col", None, None),
    )
    out_specs = (P("row", "col", None), P("row", "col", None), P("row", "col", None))
    return jax.shard_map(
        per_device, mesh=mesh, in_specs=in_specs, out_specs=out_specs, check_vma=False
    )
```

time: 448 us -> 111 us (0.25)
  waiting for transfers between devices: 285 us -> 12.6 us
  other arithmetic: 32.1 us -> 0.08 us
  Pallas kernels: 0 us -> 23 us
  matrix products: 19.6 us -> 0 us
  starting transfers between devices: 55.6 us -> 41.1 us
  between operations: 14.4 us -> 1.12 us
  local copies, waits for them, and re-layouts: 15.6 us -> 3.87 us
  blocking collectives: 21.7 us -> 27.6 us
    reduce_scatter x2 -> x0, waiting for transfers between devices: 162 us -> none  [the longest x1 88.4 us: per_device(): lax.psum_scatter(partial_y, 'col', scatter_dimension=1, tiled=True)]
    all_gather x1 -> x0, waiting for transfers between devices: 111 us -> none  [per_device(): all_y = lax.all_gather(xback, 'col', axis=1, tiled=True)]
    all_to_all x0 -> x1, blocking collectives: none -> 27.6 us  [per_device(): lax.all_to_all(coef, both, 0, 0, axis_index_groups=groups, tiled=True)]
    pallas_call x0 -> x13, Pallas kernels: none -> 23 us  [the longest x3 7.04 us: per_device(): call(functools.partial(later_step, step, step > 1), (field, field, field,...]
    all_gather x1 -> x0, blocking collectives: 21.7 us -> none  [per_device(): all_x = lax.all_gather(shared_x, 'row', axis=2, tiled=True)]
    ppermute x16 -> x19, starting transfers between devices: 55.3 us -> 34.9 us  [the longest x4 17.7 us: per_device(): lax.ppermute(faces[2], 'col', back[1])]
    dot_general x6 -> x0, matrix products: 19.6 us -> none  [contract(): jnp.einsum(form, left, right, precision=lax.Precision.HIGHEST, preferred_...]
    scatter-add x4 -> x0, other arithmetic: 14.9 us -> none  [per_device(): nxt.reshape(-1).at[flat_cells].add(traces[0, 0, step, :]).reshape(shape)]
  transfers between devices with their start and end apart: 19 -> 20, of which waited for: 14 -> 5; matrix products, arithmetic and copies ran while one was open for 3% -> 0% of each run, Pallas kernels for 0% -> 12%
where the time goes in v1:
time: 111 us; the launch traced here: 109 us
  starting transfers between devices  41.1 us (37%)
  blocking collectives  27.6 us (25%)
  Pallas kernels  23 us (21%)
  waiting for transfers between devices  12.6 us (11%)
  local copies, waits for them, and re-layouts  3.87 us (3%)
  between operations  1.12 us (1%)
    all_to_all x1, blocking collectives, per_device(): lax.all_to_all(coef, both, 0, 0, axis_index_groups=groups, tiled=True)  27.6 us
    ppermute x4, starting transfers between devices, per_device(): lax.ppermute(faces[2], 'col', back[1])  17.7 us
    ppermute x4, starting transfers between devices, per_device(): lax.ppermute(faces[0], 'row', back[0])  9.72 us
    pallas_call x3, Pallas kernels, per_device(): call(functools.partial(later_step, step, step > 1), (field, field, field,...  7.04 us
    all_to_all x1, waiting for transfers between devices, per_device(): lax.all_to_all(coef, both, 0, 0, axis_index_groups=groups, tiled=True)  6.73 us
    all_to_all x1, starting transfers between devices, per_device(): lax.all_to_all(coef, both, 0, 0, axis_index_groups=groups, tiled=True)  6.21 us
    ppermute x3, waiting for transfers between devices, per_device(): lax.ppermute(mine, 'row', [((i + k * GROUP) % rows, i) for i in range(row...  5.08 us
    ppermute x4, starting transfers between devices, per_device(): lax.ppermute(faces[1], 'row', ring[0])  3.99 us
  transfers between devices with their start and end apart: 20, of which 5 were waited for; matrix products, arithmetic and copies ran while one was open for 0% of the time, Pallas kernels for 12%

profile of v1, /device:TPU:16, one launch (start us, length us, event | category | flops | bytes accessed | tf_op | source)
XLA Modules:
  0.0 109.4 jit_solution(2502820430437965672)
XLA Ops:
  0.6 1.8 %shard_map.121 = (f32[2,32,256]{2,1,0:T(8,128)}, f32[2,32,256]{2,1,0:T(8,128)}, f32[32,2,256]{2,1,0:T(2,128)}, f32[32,2,256]{2,1,0:T(2,128)}) custom-call(f32[32,32,256]{2,1,0:T(8,128)} %now_hbm.1), custom_call_target="tpu_custom_call" | custom-call | flops 1000000 | bytes 262144 | tf_op jit(solution)/shard_map/pallas_call | solution.py:368
  2.5 0.1 collective-permute-start
  2.6 3.2 %collective-permute-start.1 = (f32[2,32,256]{2,1,0:T(8,128)}, f32[2,32,256]{2,1,0:T(8,128)S(1)}, u32[]{:S(2)}, u32[]{:S(2)}) collective-permute-start(f32[2,32,256]{2,1,0:T(8,128)} %get-tuple-element.41), channel_id=1, source_target_pairs={{16,0},{32,16},{48,32},{64,48},{80,64},{96,80},{112,96},{128,112},... | collective-permute-start | bytes 196616 | tf_op jit(solution)/shard_map/ppermute | solution.py:375
  5.8 1.3 %collective-permute-start.2 = (f32[32,2,256]{2,1,0:T(2,128)}, f32[32,2,256]{2,1,0:T(2,128)S(1)}, u32[]{:S(2)}, u32[]{:S(2)}) collective-permute-start(f32[32,2,256]{2,1,0:T(2,128)} %get-tuple-element.42), channel_id=1, source_target_pairs={{0,1},{1,2},{2,3},{3,4},{4,5},{5,6},{6,7},{7,8},{8,9},{9,10},{10,1... | collective-permute-start | bytes 196616 | tf_op jit(solution)/shard_map/ppermute | solution.py:376
  7.1 5.3 %collective-permute-start.3 = (f32[32,2,256]{2,1,0:T(2,128)}, f32[32,2,256]{2,1,0:T(2,128)S(1)}, u32[]{:S(2)}, u32[]{:S(2)}) collective-permute-start(f32[32,2,256]{2,1,0:T(2,128)} %get-tuple-element.43), channel_id=1, source_target_pairs={{1,0},{2,1},{3,2},{4,3},{5,4},{6,5},{7,6},{8,7},{9,8},{10,9},{11,1... | collective-permute-start | bytes 196616 | tf_op jit(solution)/shard_map/ppermute | solution.py:377
  12.4 0.7 copy-done.5
  13.1 0.7 copy-done.7
  13.8 3.7 %shard_map.122 = (f32[32,32,256]{2,1,0:T(8,128)S(1)}, f32[32,32,256]{2,1,0:T(8,128)S(1)}, bf16[32,32,256]{2,1,0:T(8,128)(2,1)S(1)}, f32[32,32,256]{2,1,0:T(8,128)S(1)}, f32[32,32,256]{2,1,0:T(8,128)S(1)}) custom-call(f32[32,32,256]{2,1,0:T(8,128)} %now_hbm.1, f32[32,32,256]{2,1,0:T(8,128)} %prev_hbm.1, f32[32,32,256]{2,1,0:T(8,128)} %courant_hbm.1, ...), custom_call_target="tpu_custom_call" | custom-call | flops 2000000000 | bytes 7340032 | tf_op jit(solution)/shard_map/pallas_call | solution.py:380
  17.4 0.0 copy-start
  17.4 0.1 add_convert_fusion.inside.refs_0_
  17.6 0.8 shard_map.123
  18.4 0.1 collective-permute-start.4
  18.5 3.2 %collective-permute-start.5 = (f32[2,32,256]{2,1,0:T(8,128)S(1)}, f32[2,32,256]{2,1,0:T(8,128)S(1)}, u32[]{:S(2)}, u32[]{:S(2)}) collective-permute-start(f32[2,32,256]{2,1,0:T(8,128)S(1)} %get-tuple-element.48), channel_id=1, source_target_pairs={{16,0},{32,16},{48,32},{64,48},{80,64},{96,80},{112,96},{128,112},... | collective-permute-start | bytes 196616 | tf_op jit(solution)/shard_map/ppermute | solution.py:375
  21.7 4.1 %collective-permute-start.7 = (f32[32,2,256]{2,1,0:T(2,128)S(1)}, f32[32,2,256]{2,1,0:T(2,128)S(1)}, u32[]{:S(2)}, u32[]{:S(2)}) collective-permute-start(f32[32,2,256]{2,1,0:T(2,128)S(1)} %get-tuple-element.50), channel_id=1, source_target_pairs={{1,0},{2,1},{3,2},{4,3},{5,4},{6,5},{7,6},{8,7},{9,8},{10,9},{11,1... | collective-permute-start | bytes 196616 | tf_op jit(solution)/shard_map/ppermute | solution.py:377
  25.9 2.5 %shard_map.124 = (f32[32,32,256]{2,1,0:T(8,128)S(1)}, f32[32,32,256]{2,1,0:T(8,128)S(1)}, f32[32,32,256]{2,1,0:T(8,128)S(1)}, bf16[32,32,256]{2,1,0:T(8,128)(2,1)S(1)}, f32[32,32,256]{2,1,0:T(8,128)S(1)}) custom-call(s32[4]{0:T(128)S(1)} %add_convert_fusion.inside.refs_0_, f32[2,32,256]{2,1,0:T(8,128)S(1)} %collective-permute-done.x_low.refs_1_, ...), custom_call_target="tpu_custom_call" | custom-call | flops 2000000000 | bytes 7340032 | tf_op jit(solution)/shard_map/pallas_call | solution.py:395
  28.5 0.8 shard_map.125
  29.3 0.1 collective-permute-start.10
  29.4 4.1 %collective-permute-start.11 = (f32[32,2,256]{2,1,0:T(2,128)S(1)}, f32[32,2,256]{2,1,0:T(2,128)S(1)}, u32[]{:S(2)}, u32[]{:S(2)}) collective-permute-start(f32[32,2,256]{2,1,0:T(2,128)S(1)} %get-tuple-element.58), channel_id=1, source_target_pairs={{1,0},{2,1},{3,2},{4,3},{5,4},{6,5},{7,6},{8,7},{9,8},{10,9},{11,1... | collective-permute-start | bytes 196616 | tf_op jit(solution)/shard_map/ppermute | solution.py:377
  33.5 0.0 collective-permute-start.8
  33.5 3.2 %collective-permute-start.9 = (f32[2,32,256]{2,1,0:T(8,128)S(1)}, f32[2,32,256]{2,1,0:T(8,128)S(1)}, u32[]{:S(2)}, u32[]{:S(2)}) collective-permute-start(f32[2,32,256]{2,1,0:T(8,128)S(1)} %get-tuple-element.56), channel_id=1, source_target_pairs={{16,0},{32,16},{48,32},{64,48},{80,64},{96,80},{112,96},{128,112},... | collective-permute-start | bytes 196616 | tf_op jit(solution)/shard_map/ppermute | solution.py:375
  36.8 2.5 %shard_map.126 = (f32[32,32,256]{2,1,0:T(8,128)S(1)}, f32[32,32,256]{2,1,0:T(8,128)S(1)}, f32[32,32,256]{2,1,0:T(8,128)S(1)}, bf16[32,32,256]{2,1,0:T(8,128)(2,1)S(1)}, f32[32,32,256]{2,1,0:T(8,128)S(1)}) custom-call(s32[4]{0:T(128)S(1)} %add_convert_fusion.inside.refs_0_, f32[2,32,256]{2,1,0:T(8,128)S(1)} %collective-permute-done.4.x_low.refs_1_, ...), custom_call_target="tpu_custom_call" | custom-call | flops 2000000000 | bytes 7340032 | tf_op jit(solution)/shard_map/pallas_call | solution.py:395
  39.3 0.8 shard_map.127
  40.2 3.8 %collective-permute-start.12 = (f32[2,32,256]{2,1,0:T(8,128)S(1)}, f32[2,32,256]{2,1,0:T(8,128)S(1)}, u32[]{:S(2)}, u32[]{:S(2)}) collective-permute-start(f32[2,32,256]{2,1,0:T(8,128)S(1)} %get-tuple-element.64), channel_id=1, source_target_pairs={{0,16},{16,32},{32,48},{48,64},{64,80},{80,96},{96,112},{112,128},... | collective-permute-start | bytes 196616 | tf_op jit(solution)/shard_map/ppermute | solution.py:374
  44.0 4.1 %collective-permute-start.15 = (f32[32,2,256]{2,1,0:T(2,128)S(1)}, f32[32,2,256]{2,1,0:T(2,128)S(1)}, u32[]{:S(2)}, u32[]{:S(2)}) collective-permute-start(f32[32,2,256]{2,1,0:T(2,128)S(1)} %get-tuple-element.67), channel_id=1, source_target_pairs={{1,0},{2,1},{3,2},{4,3},{5,4},{6,5},{7,6},{8,7},{9,8},{10,9},{11,1... | collective-permute-start | bytes 196616 | tf_op jit(solution)/shard_map/ppermute | solution.py:377
  48.1 2.0 %shard_map.128 = (f32[32,32,256]{2,1,0:T(8,128)S(1)}, f32[32,32,256]{2,1,0:T(8,128)S(1)}, f32[32,32,256]{2,1,0:T(8,128)S(1)}, bf16[32,32,256]{2,1,0:T(8,128)(2,1)S(1)}) custom-call(s32[4]{0:T(128)S(1)} %add_convert_fusion.inside.refs_0_, f32[2,32,256]{2,1,0:T(8,128)S(1)} %collective-permute-done.8.x_low.refs_1_, ...), custom_call_target="tpu_custom_call" | custom-call | flops 2000000000 | bytes 7340032 | tf_op jit(solution)/shard_map/pallas_call | solution.py:395
  50.1 0.0 copy-start.9
  50.1 0.0 copy-start.11
  50.2 0.0 copy-start.1
  50.2 0.0 copy-start.2
  50.2 0.8 collective-permute-done.14.y_low
  51.0 0.0 copy-start.8
  51.0 1.3 %shard_map.129 = f32[64,8,128]{2,1,0:T(8,128)S(1)} custom-call(s32[4]{0:T(128)S(1)} %add_convert_fusion.inside.refs_0_, f32[2,32,256]{2,1,0:T(8,128)S(1)} %collective-permute-done.12.x_low, f32[2,32,256]{2,1,0:T(8,128)S(1)} %collective-permute-done.13.x_high, f32[32,2,256]{2,1,0:T(2,128)S(1)} %collective-permute-done.14.y_low, ...), custom_call_target="tpu_custom_call" | custom-call | flops 1000000 | bytes 262144 | tf_op jit(solution)/shard_map/pallas_call | solution.py:409
  52.3 27.6 %all_to_all.10.chunks = f32[64,8,128]{2,1,0:T(8,128)S(1)} all-to-all(f32[64,8,128]{2,1,0:T(8,128)S(1)} %shard_map.129), channel_id=1, replica_groups={{0,1,2,3,4,5,6,7,8,9,10,11,12,13,14,15,16,17,18,19,20,21,22,23,24,25,26..., dimensions={0} | all-to-all | bytes 524288 | tf_op jit(solution)/shard_map/all_to_all | solution.py:425
  80.0 0.5 shard_map.130.own
  80.5 0.1 collective-permute-start.16
  80.5 0.1 collective-permute-start.17
  80.6 1.9 %collective-permute-start.18 = (f32[128,128]{1,0:T(8,128)S(1)}, f32[128,128]{1,0:T(8,128)S(1)}, u32[]{:S(2)}, u32[]{:S(2)}) collective-permute-start(f32[128,128]{1,0:T(8,128)S(1)} %shard_map.130.own), channel_id=1, source_target_pairs={{192,0},{208,16},{224,32},{240,48},{0,64},{16,80},{32,96},{48,112}... | collective-permute-start | bytes 196616 | tf_op jit(solution)/shard_map/ppermute | solution.py:430
  82.6 2.2 %collective-permute-done.16.one = f32[128,128]{1,0:T(8,128)S(1)} collective-permute-done((f32[128,128]{1,0:T(8,128)S(1)}, f32[128,128]{1,0:T(8,128)S(1)}, u32[]{:S(2)}, u32[]{:S(2)}) %collective-permute-start.16) | collective-permute-done | bytes 65568 | tf_op jit(solution)/shard_map/ppermute | solution.py:430
  84.8 2.3 %collective-permute-done.17.two = f32[128,128]{1,0:T(8,128)S(1)} collective-permute-done((f32[128,128]{1,0:T(8,128)S(1)}, f32[128,128]{1,0:T(8,128)S(1)}, u32[]{:S(2)}, u32[]{:S(2)}) %collective-permute-start.17) | collective-permute-done | bytes 65568 | tf_op jit(solution)/shard_map/ppermute | solution.py:430
  87.1 0.5 collective-permute-done.18.three
  87.7 1.6 %shard_map.131 = f32[64,8,128]{2,1,0:T(8,128)} custom-call(f32[128,128]{1,0:T(8,128)S(1)} %shard_map.130.own, f32[128,128]{1,0:T(8,128)S(1)} %collective-permute-done.16.one, f32[128,128]{1,0:T(8,128)S(1)} %collective-permute-done.17.two, f32[128,128]{1,0:T(8,128)S(1)} %collective-permute-done.18.three, f32[4,128,128]{2,1,0:T(8,128)S(1)} %copy-done.2, ...), custom_call_target="tpu_custom_call" | custom-call | flops 1000000 | bytes 262144 | tf_op jit(solution)/shard_map/pallas_call | solution.py:433
  89.2 6.2 %all-to-all-start.1 = ((f32[64,8,128]{2,1,0:T(8,128)}), f32[64,8,128]{2,1,0:T(8,128)S(1)}, u32[]{:S(2)}, u32[]{:S(2)}) async-start(f32[64,8,128]{2,1,0:T(8,128)} %shard_map.131), calls=%async_computation.1 | async-start | bytes 524288 | tf_op jit(solution)/shard_map/all_to_all | solution.py:436
  95.4 0.0 copy-start.10
  95.5 1.2 %copy-done.10 = f32[32,32,256]{2,1,0:T(8,128)S(1)} copy-done((f32[32,32,256]{2,1,0:T(8,128)S(1)}, f32[32,32,256]{2,1,0:T(8,128)}, u32[]{:S(2)}) %copy-start.10) | copy-done | bytes 1048600
  96.7 1.2 %copy-done.12 = f32[32,32,256]{2,1,0:T(8,128)S(1)} copy-done((f32[32,32,256]{2,1,0:T(8,128)S(1)}, f32[32,32,256]{2,1,0:T(8,128)}, u32[]{:S(2)}) %copy-start.12) | copy-done | bytes 1048600
  97.9 2.7 %shard_map.133 = (f32[32,32,256]{2,1,0:T(8,128)}, f32[32,32,256]{2,1,0:T(8,128)}) custom-call(s32[4]{0:T(128)S(1)} %add_convert_fusion.inside.refs_0_, f32[2,32,256]{2,1,0:T(8,128)S(1)} %collective-permute-done.12.x_low, f32[2,32,256]{2,1,0:T(8,128)S(1)} %collective-permute-done.13.x_high, f32[32,2,256]{2,1,0:T(2,128)S(1)} %collective-permute-done.14.y_low, ...), custom_call_target="tpu_custom_call" | custom-call | flops 2000000000 | bytes 7340032 | tf_op jit(solution)/shard_map/pallas_call | solution.py:412
  100.6 6.7 %all-to-all-done.1.coef = f32[64,8,128]{2,1,0:T(8,128)S(1)} async-done(((f32[64,8,128]{2,1,0:T(8,128)}), f32[64,8,128]{2,1,0:T(8,128)S(1)}, u32[]{:S(2)}, u32[]{:S(2)}) %all-to-all-start.1) | async-done | bytes 262176 | tf_op jit(solution)/shard_map/all_to_all | solution.py:436
  107.3 1.9 %shard_map.132 = f32[32,32,256]{2,1,0:T(8,128)} custom-call(f32[64,8,128]{2,1,0:T(8,128)S(1)} %all-to-all-done.1.coef, f32[64,256]{1,0:T(8,128)S(1)} %copy-done.4), custom_call_target="tpu_custom_call" | custom-call | flops 1000000 | bytes 262144 | tf_op jit(solution)/shard_map/pallas_call | solution.py:437
  (33 shorter events, 0.1 us)
Async XLA Ops:
  2.5 15.1 %collective-permute-start = (f32[2,32,256]{2,1,0:T(8,128)}, f32[2,32,256]{2,1,0:T(8,128)S(1)}, u32[]{:S(2)}, u32[]{:S(2)}) collective-permute-start(f32[2,32,256]{2,1,0:T(8,128)} %get-tuple-element.40), channel_id=1, source_target_pairs={{0,16},{16,32},{32,48},{48,64},{64,80},{80,96},{96,112},{112,128},... | collective-permute-start | bytes 196616 | tf_op jit(solution)/shard_map/ppermute | solution.py:374
  2.6 15.0 %collective-permute-start.1 = (f32[2,32,256]{2,1,0:T(8,128)}, f32[2,32,256]{2,1,0:T(8,128)S(1)}, u32[]{:S(2)}, u32[]{:S(2)}) collective-permute-start(f32[2,32,256]{2,1,0:T(8,128)} %get-tuple-element.41), channel_id=1, source_target_pairs={{16,0},{32,16},{48,32},{64,48},{80,64},{96,80},{112,96},{128,112},... | collective-permute-start | bytes 196616 | tf_op jit(solution)/shard_map/ppermute | solution.py:375
  5.8 11.7 %collective-permute-start.2 = (f32[32,2,256]{2,1,0:T(2,128)}, f32[32,2,256]{2,1,0:T(2,128)S(1)}, u32[]{:S(2)}, u32[]{:S(2)}) collective-permute-start(f32[32,2,256]{2,1,0:T(2,128)} %get-tuple-element.42), channel_id=1, source_target_pairs={{0,1},{1,2},{2,3},{3,4},{4,5},{5,6},{6,7},{7,8},{8,9},{9,10},{10,1... | collective-permute-start | bytes 196616 | tf_op jit(solution)/shard_map/ppermute | solution.py:376
  7.1 10.5 %collective-permute-start.3 = (f32[32,2,256]{2,1,0:T(2,128)}, f32[32,2,256]{2,1,0:T(2,128)S(1)}, u32[]{:S(2)}, u32[]{:S(2)}) collective-permute-start(f32[32,2,256]{2,1,0:T(2,128)} %get-tuple-element.43), channel_id=1, source_target_pairs={{1,0},{2,1},{3,2},{4,3},{5,4},{6,5},{7,6},{8,7},{9,8},{10,9},{11,1... | collective-permute-start | bytes 196616 | tf_op jit(solution)/shard_map/ppermute | solution.py:377
  12.4 0.7 copy-start.5
  13.1 0.7 copy-start.7
  17.4 8.4 %copy-start = (bf16[4,32,32,256]{3,2,1,0:T(8,128)(2,1)S(1)}, bf16[4,32,32,256]{3,2,1,0:T(8,128)(2,1)}, u32[]{:S(2)}) copy-start(bf16[4,32,32,256]{3,2,1,0:T(8,128)(2,1)} %refs_10_.5) | copy-start | bytes 6291460
  18.4 10.0 %collective-permute-start.4 = (f32[2,32,256]{2,1,0:T(8,128)S(1)}, f32[2,32,256]{2,1,0:T(8,128)S(1)}, u32[]{:S(2)}, u32[]{:S(2)}) collective-permute-start(f32[2,32,256]{2,1,0:T(8,128)S(1)} %get-tuple-element.47), channel_id=1, source_target_pairs={{0,16},{16,32},{32,48},{48,64},{64,80},{80,96},{96,112},{112,128},... | collective-permute-start | bytes 196616 | tf_op jit(solution)/shard_map/ppermute | solution.py:374
  18.5 9.9 %collective-permute-start.5 = (f32[2,32,256]{2,1,0:T(8,128)S(1)}, f32[2,32,256]{2,1,0:T(8,128)S(1)}, u32[]{:S(2)}, u32[]{:S(2)}) collective-permute-start(f32[2,32,256]{2,1,0:T(8,128)S(1)} %get-tuple-element.48), channel_id=1, source_target_pairs={{16,0},{32,16},{48,32},{64,48},{80,64},{96,80},{112,96},{128,112},... | collective-permute-start | bytes 196616 | tf_op jit(solution)/shard_map/ppermute | solution.py:375
  21.7 6.7 %collective-permute-start.6 = (f32[32,2,256]{2,1,0:T(2,128)S(1)}, f32[32,2,256]{2,1,0:T(2,128)S(1)}, u32[]{:S(2)}, u32[]{:S(2)}) collective-permute-start(f32[32,2,256]{2,1,0:T(2,128)S(1)} %get-tuple-element.49), channel_id=1, source_target_pairs={{0,1},{1,2},{2,3},{3,4},{4,5},{5,6},{6,7},{7,8},{8,9},{9,10},{10,1... | collective-permute-start | bytes 196616 | tf_op jit(solution)/shard_map/ppermute | solution.py:376
  21.7 6.7 %collective-permute-start.7 = (f32[32,2,256]{2,1,0:T(2,128)S(1)}, f32[32,2,256]{2,1,0:T(2,128)S(1)}, u32[]{:S(2)}, u32[]{:S(2)}) collective-permute-start(f32[32,2,256]{2,1,0:T(2,128)S(1)} %get-tuple-element.50), channel_id=1, source_target_pairs={{1,0},{2,1},{3,2},{4,3},{5,4},{6,5},{7,6},{8,7},{9,8},{10,9},{11,1... | collective-permute-start | bytes 196616 | tf_op jit(solution)/shard_map/ppermute | solution.py:377
  29.3 10.0 %collective-permute-start.10 = (f32[32,2,256]{2,1,0:T(2,128)S(1)}, f32[32,2,256]{2,1,0:T(2,128)S(1)}, u32[]{:S(2)}, u32[]{:S(2)}) collective-permute-start(f32[32,2,256]{2,1,0:T(2,128)S(1)} %get-tuple-element.57), channel_id=1, source_target_pairs={{0,1},{1,2},{2,3},{3,4},{4,5},{5,6},{6,7},{7,8},{8,9},{9,10},{10,1... | collective-permute-start | bytes 196616 | tf_op jit(solution)/shard_map/ppermute | solution.py:376
  29.4 9.9 %collective-permute-start.11 = (f32[32,2,256]{2,1,0:T(2,128)S(1)}, f32[32,2,256]{2,1,0:T(2,128)S(1)}, u32[]{:S(2)}, u32[]{:S(2)}) collective-permute-start(f32[32,2,256]{2,1,0:T(2,128)S(1)} %get-tuple-element.58), channel_id=1, source_target_pairs={{1,0},{2,1},{3,2},{4,3},{5,4},{6,5},{7,6},{8,7},{9,8},{10,9},{11,1... | collective-permute-start | bytes 196616 | tf_op jit(solution)/shard_map/ppermute | solution.py:377
  33.5 5.8 %collective-permute-start.8 = (f32[2,32,256]{2,1,0:T(8,128)S(1)}, f32[2,32,256]{2,1,0:T(8,128)S(1)}, u32[]{:S(2)}, u32[]{:S(2)}) collective-permute-start(f32[2,32,256]{2,1,0:T(8,128)S(1)} %get-tuple-element.55), channel_id=1, source_target_pairs={{0,16},{16,32},{32,48},{48,64},{64,80},{80,96},{96,112},{112,128},... | collective-permute-start | bytes 196616 | tf_op jit(solution)/shard_map/ppermute | solution.py:374
  33.5 5.8 %collective-permute-start.9 = (f32[2,32,256]{2,1,0:T(8,128)S(1)}, f32[2,32,256]{2,1,0:T(8,128)S(1)}, u32[]{:S(2)}, u32[]{:S(2)}) collective-permute-start(f32[2,32,256]{2,1,0:T(8,128)S(1)} %get-tuple-element.56), channel_id=1, source_target_pairs={{16,0},{32,16},{48,32},{64,48},{80,64},{96,80},{112,96},{128,112},... | collective-permute-start | bytes 196616 | tf_op jit(solution)/shard_map/ppermute | solution.py:375
  40.2 10.0 %collective-permute-start.12 = (f32[2,32,256]{2,1,0:T(8,128)S(1)}, f32[2,32,256]{2,1,0:T(8,128)S(1)}, u32[]{:S(2)}, u32[]{:S(2)}) collective-permute-start(f32[2,32,256]{2,1,0:T(8,128)S(1)} %get-tuple-element.64), channel_id=1, source_target_pairs={{0,16},{16,32},{32,48},{48,64},{64,80},{80,96},{96,112},{112,128},... | collective-permute-start | bytes 196616 | tf_op jit(solution)/shard_map/ppermute | solution.py:374
  44.0 6.2 %collective-permute-start.13 = (f32[2,32,256]{2,1,0:T(8,128)S(1)}, f32[2,32,256]{2,1,0:T(8,128)S(1)}, u32[]{:S(2)}, u32[]{:S(2)}) collective-permute-start(f32[2,32,256]{2,1,0:T(8,128)S(1)} %get-tuple-element.65), channel_id=1, source_target_pairs={{16,0},{32,16},{48,32},{64,48},{80,64},{96,80},{112,96},{128,112},... | collective-permute-start | bytes 196616 | tf_op jit(solution)/shard_map/ppermute | solution.py:375
  44.0 7.0 %collective-permute-start.14 = (f32[32,2,256]{2,1,0:T(2,128)S(1)}, f32[32,2,256]{2,1,0:T(2,128)S(1)}, u32[]{:S(2)}, u32[]{:S(2)}) collective-permute-start(f32[32,2,256]{2,1,0:T(2,128)S(1)} %get-tuple-element.66), channel_id=1, source_target_pairs={{0,1},{1,2},{2,3},{3,4},{4,5},{5,6},{6,7},{7,8},{8,9},{9,10},{10,1... | collective-permute-start | bytes 196616 | tf_op jit(solution)/shard_map/ppermute | solution.py:376
  44.0 7.0 %collective-permute-start.15 = (f32[32,2,256]{2,1,0:T(2,128)S(1)}, f32[32,2,256]{2,1,0:T(2,128)S(1)}, u32[]{:S(2)}, u32[]{:S(2)}) collective-permute-start(f32[32,2,256]{2,1,0:T(2,128)S(1)} %get-tuple-element.67), channel_id=1, source_target_pairs={{1,0},{2,1},{3,2},{4,3},{5,4},{6,5},{7,6},{8,7},{9,8},{10,9},{11,1... | collective-permute-start | bytes 196616 | tf_op jit(solution)/shard_map/ppermute | solution.py:377
  48.1 2.8 %copy-start.3 = (f32[64,256]{1,0:T(8,128)S(1)}, f32[64,256]{1,0:T(8,128)}, u32[]{:S(2)}) copy-start(f32[64,256]{1,0:T(8,128)} %constant.20.clone.table_z) | copy-start | bytes 196612
  50.1 37.5 %copy-start.9 = (f32[32,32,256]{2,1,0:T(8,128)}, f32[32,32,256]{2,1,0:T(8,128)S(1)}, u32[]{:S(2)}) copy-start(f32[32,32,256]{2,1,0:T(8,128)S(1)} %get-tuple-element.73.now) | copy-start | bytes 3145732
  50.1 37.5 %copy-start.11 = (f32[32,32,256]{2,1,0:T(8,128)}, f32[32,32,256]{2,1,0:T(8,128)S(1)}, u32[]{:S(2)}) copy-start(f32[32,32,256]{2,1,0:T(8,128)S(1)} %get-tuple-element.74.lap) | copy-start | bytes 3145732
  50.2 29.8 %copy-start.1 = (f32[128,512]{1,0:T(8,128)S(1)}, f32[128,512]{1,0:T(8,128)}, u32[]{:S(2)}) copy-start(f32[128,512]{1,0:T(8,128)} %constant.21.clone.table_y) | copy-start | bytes 786436
  50.2 37.5 %copy-start.2 = (f32[4,128,128]{2,1,0:T(8,128)S(1)}, f32[4,128,128]{2,1,0:T(8,128)}, u32[]{:S(2)}) copy-start(f32[4,128,128]{2,1,0:T(8,128)} %constant.22.clone.table_x) | copy-start | bytes 786436
  51.0 44.4 %copy-start.6 = (f32[1,1,4,512]{3,2,1,0:T(4,128)S(1)}, f32[1,1,4,512]{3,2,1,0:T(4,128)}, u32[]{:S(2)}) copy-start(f32[1,1,4,512]{3,2,1,0:T(4,128)} %param.15) | copy-start | bytes 24580
  51.0 44.4 %copy-start.8 = (s32[1,1,512]{2,1,0:T(1,128)S(1)}, s32[1,1,512]{2,1,0:T(1,128)}, u32[]{:S(2)}) copy-start(s32[1,1,512]{2,1,0:T(1,128)} %param.14) | copy-start | bytes 6148
  80.5 4.3 %collective-permute-start.16 = (f32[128,128]{1,0:T(8,128)S(1)}, f32[128,128]{1,0:T(8,128)S(1)}, u32[]{:S(2)}, u32[]{:S(2)}) collective-permute-start(f32[128,128]{1,0:T(8,128)S(1)} %shard_map.130.own), channel_id=1, source_target_pairs={{64,0},{80,16},{96,32},{112,48},{128,64},{144,80},{160,96},{176,11... | collective-permute-start | bytes 196616 | tf_op jit(solution)/shard_map/ppermute | solution.py:430
  80.5 6.6 %collective-permute-start.17 = (f32[128,128]{1,0:T(8,128)S(1)}, f32[128,128]{1,0:T(8,128)S(1)}, u32[]{:S(2)}, u32[]{:S(2)}) collective-permute-start(f32[128,128]{1,0:T(8,128)S(1)} %shard_map.130.own), channel_id=1, source_target_pairs={{128,0},{144,16},{160,32},{176,48},{192,64},{208,80},{224,96},{240... | collective-permute-start | bytes 196616 | tf_op jit(solution)/shard_map/ppermute | solution.py:430
  80.6 7.0 %collective-permute-start.18 = (f32[128,128]{1,0:T(8,128)S(1)}, f32[128,128]{1,0:T(8,128)S(1)}, u32[]{:S(2)}, u32[]{:S(2)}) collective-permute-start(f32[128,128]{1,0:T(8,128)S(1)} %shard_map.130.own), channel_id=1, source_target_pairs={{192,0},{208,16},{224,32},{240,48},{0,64},{16,80},{32,96},{48,112}... | collective-permute-start | bytes 196616 | tf_op jit(solution)/shard_map/ppermute | solution.py:430
  89.2 18.1 %all-to-all-start.1 = ((f32[64,8,128]{2,1,0:T(8,128)}), f32[64,8,128]{2,1,0:T(8,128)S(1)}, u32[]{:S(2)}, u32[]{:S(2)}) async-start(f32[64,8,128]{2,1,0:T(8,128)} %shard_map.131), calls=%async_computation.1 | async-start | bytes 524288 | tf_op jit(solution)/shard_map/all_to_all | solution.py:436
  95.4 1.2 %copy-start.10 = (f32[32,32,256]{2,1,0:T(8,128)S(1)}, f32[32,32,256]{2,1,0:T(8,128)}, u32[]{:S(2)}) copy-start(f32[32,32,256]{2,1,0:T(8,128)} %copy-done.9) | copy-start | bytes 3145732
  96.7 1.2 %copy-start.12 = (f32[32,32,256]{2,1,0:T(8,128)S(1)}, f32[32,32,256]{2,1,0:T(8,128)}, u32[]{:S(2)}) copy-start(f32[32,32,256]{2,1,0:T(8,128)} %copy-done.11) | copy-start | bytes 3145732
  97.9 9.4 %copy-start.4 = (f32[64,256]{1,0:T(8,128)S(1)}, f32[64,256]{1,0:T(8,128)}, u32[]{:S(2)}) copy-start(f32[64,256]{1,0:T(8,128)} %constant.19.clone.table_z) | copy-start | bytes 196612

commit v2 on v1

v2 whole, which is shorter than its diff:
```python
import functools

import jax
import jax.numpy as jnp
import numpy as np
from jax import lax
from jax.experimental import pallas as pl
from jax.experimental.pallas import tpu as pltpu
from jax.sharding import PartitionSpec as P

STEPS = 4
KX = 128
KY = 128
KZ = 64
GROUP = 4
ROWS = 256
TWELFTH = 1.0 / 12.0
PACK_ROOM = 52
FIRST_ROOM = 50

HBM = pl.BlockSpec(memory_space=pltpu.HBM)
VMEM = pl.BlockSpec(memory_space=pltpu.VMEM)
SMEM = pl.BlockSpec(memory_space=pltpu.SMEM)
DMA = pltpu.SemaphoreType.DMA
NT = (((1,), (1,)), ((), ()))
NN = (((1,), (0,)), ((), ()))
TN = (((0,), (0,)), ((), ()))


def split(value):
    high = value.astype(jnp.bfloat16)
    low = (value - high.astype(jnp.float32)).astype(jnp.bfloat16)
    return high, low


def dot(left, right, dims):
    return lax.dot_general(left, right, dims, preferred_element_type=jnp.float32)


def dot3(left, right, dims):
    return (
        dot(left[0], right[0], dims)
        + dot(left[1], right[0], dims)
        + dot(left[0], right[1], dims)
    )


def basis(count, length):
    half = count // 2
    cells = np.arange(length, dtype=np.int64)[None, :]
    modes = np.arange(count, dtype=np.int64)[:, None]
    freq = np.where(modes < half, modes, modes - half + 1)
    phase = (freq * cells % length) * (2.0 * np.pi / length)
    values = np.sqrt(2.0 / length) * np.where(modes < half, np.cos(phase), np.sin(phase))
    values[0] = np.sqrt(1.0 / length)
    values[count - 1] = 0.0
    return values


def bands(size_y, size_z):
    def far(size):
        one = lax.broadcasted_iota(jnp.int32, (size, size), 0)
        two = lax.broadcasted_iota(jnp.int32, (size, size), 1)
        return jnp.abs(one - two), one // size_y == two // size_y

    gap, _ = far(size_z)
    band_z = jnp.where(gap == 0, -90.0, jnp.where(gap == 1, 16.0, jnp.where(gap == 2, -1.0, 0.0)))
    gap, same = far(ROWS)
    band_y = jnp.where(gap == 1, 16.0, jnp.where(gap == 2, -1.0, 0.0))
    band_y = jnp.where(same, band_y, 0.0)
    return band_z.astype(jnp.bfloat16), band_y.astype(jnp.bfloat16)


def with_flags(rows, cols, kernel, spot, *refs):
    row, col = spot[0] >> (cols.bit_length() - 1), spot[0] & (cols - 1)
    turn = row & (GROUP - 1)
    flags = [row, rows - 1 - row, col, cols - 1 - col, row & 1, col & 1]
    flags += [turn - (turn ^ k) + GROUP - 1 for k in range(GROUP)]
    kernel(flags, *refs)


def pack(flags, now_hbm, now, x_even, x_odd, y_even, y_odd, sems):
    size_x, size_y, _ = now.shape
    step = size_x // 4
    copies = []
    for b in range(4):
        part = pl.ds(b * step, step)
        copies.append(pltpu.make_async_copy(now_hbm.at[part], now.at[part], sems.at[b]))
        copies[-1].start()
    for b in range(4):
        copies[b].wait()
        part = pl.ds(b * step, step)
        low, high = now[part, 0:2, :], now[part, size_y - 2 : size_y, :]
        y_even[part] = jnp.where(flags[5] > 0, low, high)
        y_odd[part] = jnp.where(flags[5] > 0, high, low)
    low, high = now[0:2], now[size_x - 2 : size_x]
    x_even[...] = jnp.where(flags[4] > 0, low, high)
    x_odd[...] = jnp.where(flags[4] > 0, high, low)


def x_changes(flags, x_even, x_odd, size_x):
    odd = flags[4] > 0
    before = [jnp.where(odd, x_even[i], x_odd[i]) for i in range(2)]
    after = [jnp.where(odd, x_odd[i], x_even[i]) for i in range(2)]
    before = [jnp.where(flags[0] > 0, value, 0.0) for value in before]
    after = [jnp.where(flags[1] > 0, value, 0.0) for value in after]
    return {
        0: 16.0 * before[1] - before[0],
        1: -before[1],
        size_x - 2: -after[0],
        size_x - 1: 16.0 * after[0] - after[1],
    }


def y_tiles(flags, y_even, y_odd, x):
    size_z = y_even.shape[2]
    line = lax.broadcasted_iota(jnp.int32, (8, size_z), 0)
    odd = flags[5] > 0
    low = jnp.where(flags[2] > 0, jnp.where(odd, y_even[x], y_odd[x]), 0.0)
    near = jnp.broadcast_to(low[1:2], (8, size_z))
    far = jnp.broadcast_to(low[0:1], (8, size_z))
    first = jnp.where(line == 0, 16.0 * near - far, jnp.where(line == 1, -near, 0.0))
    high = jnp.where(flags[3] > 0, jnp.where(odd, y_odd[x], y_even[x]), 0.0)
    near = jnp.broadcast_to(high[0:1], (8, size_z))
    far = jnp.broadcast_to(high[1:2], (8, size_z))
    last = jnp.where(line == 7, 16.0 * near - far, jnp.where(line == 6, -near, 0.0))
    return first, last


def with_change(value, x, x_change, tiles):
    size_y = value.shape[0]
    parts = [value[0:8] + tiles[0], value[8 : size_y - 8], value[size_y - 8 : size_y] + tiles[1]]
    value = jnp.concatenate(parts, axis=0)
    return value + x_change[x] if x in x_change else value


def faces_after(flags, x_even, x_odd, y_even, y_odd, courant, base, lap, out_x_even, out_x_odd, out_y_even, out_y_odd):
    size_x, size_y, _ = base.shape
    x_change = x_changes(flags, x_even, x_odd, size_x)
    layers = {}
    for x in range(size_x):
        tiles = y_tiles(flags, y_even, y_odd, x)
        if x in x_change:
            value = with_change(lap[x], x, x_change, tiles)
            layers[x] = value = base[x] + (courant[x] * TWELFTH) * value
            first, last = value[0:8], value[size_y - 8 : size_y]
        else:
            first = base[x, 0:8] + (courant[x, 0:8] * TWELFTH) * (lap[x, 0:8] + tiles[0])
            end = slice(size_y - 8, size_y)
            last = base[x, end] + (courant[x, end] * TWELFTH) * (lap[x, end] + tiles[1])
        low, high = first[0:2], last[6:8]
        out_y_even[x] = jnp.where(flags[5] > 0, low, high)
        out_y_odd[x] = jnp.where(flags[5] > 0, high, low)
    for i in range(2):
        low, high = layers[i], layers[size_x - 2 + i]
        out_x_even[i] = jnp.where(flags[4] > 0, low, high)
        out_x_odd[i] = jnp.where(flags[4] > 0, high, low)


def injection(step, cells, traces, size_z):
    spots = cells[...]
    value = traces[pl.ds(step, 1), :]
    top = value.astype(jnp.bfloat16)
    rest = value - top.astype(jnp.float32)
    mid = rest.astype(jnp.bfloat16)
    depth = lax.broadcasted_iota(jnp.int32, (size_z, spots.shape[1]), 0)
    here = depth == spots % size_z
    parts = [
        jnp.where(here, part.astype(jnp.float32), 0.0).astype(jnp.bfloat16)
        for part in (top, mid)
    ]
    line = lax.broadcasted_iota(jnp.int32, (ROWS, spots.shape[1]), 0)

    def block(first_row):
        hits = jnp.where(line == spots // size_z - first_row, 1.0, 0.0).astype(jnp.bfloat16)
        return sum(dot(hits, part, NT) for part in parts)

    return block


def laplace_block(now, first, layers, band_z, band_y):
    size_x, size_y, size_z = now.shape
    center = now[first : first + layers].reshape(ROWS, size_z)
    high, low = split(center)
    lap = dot(high, band_z, NN) + dot(low, band_z, NN)
    lap = lap + dot(band_y, high, NN) + dot(band_y, low, NN)
    lap = lap.reshape(layers, size_y, size_z)
    out = []
    for layer in range(layers):
        x = first + layer
        near = [now[x + d] for d in (-1, 1) if 0 <= x + d < size_x]
        far = [now[x + d] for d in (-2, 2) if 0 <= x + d < size_x]
        value = lap[layer] + 16.0 * functools.reduce(jnp.add, near)
        out.append(value - functools.reduce(jnp.add, far))
    return out


def first_step(now, prev_hbm, cells, traces, base, lap, prev, sems):
    size_x, size_y, size_z = now.shape
    layers = ROWS // size_y
    blocks = size_x // layers
    copies = []
    for b in range(blocks):
        part = pl.ds(b * layers, layers)
        copies.append(pltpu.make_async_copy(prev_hbm.at[part], prev.at[part], sems.at[b]))
        copies[-1].start()
    band_z, band_y = bands(size_y, size_z)
    added = injection(0, cells, traces, size_z)
    for b in range(blocks):
        inject = added(b * ROWS).reshape(layers, size_y, size_z)
        for i, value in enumerate(laplace_block(now, b * layers, layers, band_z, band_y)):
            x = b * layers + i
            lap[x] = value
            base[x] = 2.0 * now[x] + inject[i]
    for b in range(blocks):
        copies[b].wait()
        part = slice(b * layers, (b + 1) * layers)
        base[part] = base[part] - prev[part]


def later_step(step, flags, *refs):
    x_even, x_odd, y_even, y_odd, base_in, lap_in, prev, courant, forward, cells, traces, *refs = refs
    gradient_in = refs.pop(0) if step > 1 else None
    last = step == STEPS - 1
    now, lap, gradient = refs[:3]
    base = None if last else refs[3]
    size_x, size_y, size_z = now.shape
    layers = ROWS // size_y
    band_z, band_y = bands(size_y, size_z)
    x_change = x_changes(flags, x_even, x_odd, size_x)
    for x in range(size_x):
        value = with_change(lap_in[x], x, x_change, y_tiles(flags, y_even, y_odd, x))
        now[x] = base_in[x] + (courant[x] * TWELFTH) * value
        value = forward[step - 1, x].astype(jnp.float32) * value
        gradient[x] = gradient_in[x] + value if step > 1 else value
    added = None if last else injection(step, cells, traces, size_z)
    for b in range(size_x // layers):
        inject = None if last else added(b * ROWS).reshape(layers, size_y, size_z)
        for i, value in enumerate(laplace_block(now, b * layers, layers, band_z, band_y)):
            x = b * layers + i
            lap[x] = value
            if last:
                gradient[x] += forward[step, x].astype(jnp.float32) * value
            else:
                base[x] = (2.0 * now[x] - prev[x]) + inject[i]


def finish(flags, x_even, x_odd, y_even, y_odd, now, lap, prev, courant, cells, traces, next_hbm, now_hbm, nxt, sems):
    size_x, size_y, size_z = now.shape
    layers = ROWS // size_y
    keep = pltpu.make_async_copy(now, now_hbm, sems.at[0])
    keep.start()
    added = injection(STEPS - 1, cells, traces, size_z)
    x_change = x_changes(flags, x_even, x_odd, size_x)
    copies = []
    for b in range(size_x // layers):
        inject = added(b * ROWS).reshape(layers, size_y, size_z)
        for i in range(layers):
            x = b * layers + i
            value = with_change(lap[x], x, x_change, y_tiles(flags, y_even, y_odd, x))
            base = (2.0 * now[x] - prev[x]) + inject[i]
            nxt[x] = base + (courant[x] * TWELFTH) * value
        part = pl.ds(b * layers, layers)
        copies.append(pltpu.make_async_copy(nxt.at[part], next_hbm.at[part], sems.at[1 + b]))
        copies[-1].start()
    for copy in copies:
        copy.wait()
    keep.wait()


def project_z(flags, x_even, x_odd, y_even, y_odd, forward, gradient, table_z, coef):
    size_x, size_y, _ = gradient.shape
    table = split(table_z[...])
    x_change = x_changes(flags, x_even, x_odd, size_x)
    for s in range(8):
        lines = []
        for x in range(s, size_x, 8):
            first, last = y_tiles(flags, y_even, y_odd, x)
            scale = forward[STEPS - 1, x].astype(jnp.float32)
            tiles = (scale[0:8] * first, scale[size_y - 8 : size_y] * last)
            value = with_change(gradient[x], x, {}, tiles)
            lines.append(value + scale * x_change[x] if x in x_change else value)
        coef[:, s, :] = dot3(table, split(jnp.concatenate(lines, axis=0)), NT)


def project_y(chunks, table_y, out, plane):
    count = chunks.shape[0] // GROUP
    for r in range(GROUP):
        for q in range(4):
            pieces = [chunks[r * count + c][:, q * 32 : (q + 1) * 32] for c in range(count)]
            plane[pl.ds((r * 4 + q) * 8, 8), :] = jnp.concatenate(pieces, axis=1)
    out[...] = dot3(split(plane[...]), split(table_y[...]), NT)


def smooth_plane(flags, own, one, two, three, table_x, table_y, chunks_hbm, plane, chunks, sems):
    high, low = split(jnp.concatenate([own[...], one[...], two[...], three[...]], axis=0))
    tables = [split(table_x[flags[6 + k]]) for k in range(GROUP)]
    left_high = jnp.concatenate([table[0] for table in tables], axis=1)
    left_low = jnp.concatenate([table[1] for table in tables], axis=1)
    total = dot3((left_high, left_low), (high, low), NN)
    plane[...] = dot3(split(total), split(table_y[...]), NN)
    count = chunks.shape[0] // GROUP
    copies = []
    for r in range(GROUP):
        for c in range(count):
            pieces = [plane[pl.ds((r * 4 + q) * 8, 8), c * 32 : (c + 1) * 32] for q in range(4)]
            chunks[r * count + c] = jnp.concatenate(pieces, axis=1)
        part = pl.ds(r * count, count)
        copies.append(pltpu.make_async_copy(chunks.at[part], chunks_hbm.at[part], sems.at[r]))
        copies[-1].start()
    for copy in copies:
        copy.wait()


def expand_z(coef, table_z, out, lines, sems):
    _, size_y, size_z = out.shape
    high, low = split(table_z[...])
    table = jnp.concatenate([high, high, low], axis=0)
    copies = []
    for s in range(8):
        high, low = split(coef[:, s, :])
        value = dot(jnp.concatenate([high, low, high], axis=0), table, TN)
        lines[s] = value.reshape(4, size_y, size_z)
        for q in range(4):
            copies.append(pltpu.make_async_copy(lines.at[s, q], out.at[q * 8 + s], sems.at[s, q]))
            copies[-1].start()
    for copy in copies:
        copy.wait()


def call(kernel, out_shape, specs, out_specs=None, scratch=(), room=24, **cost):
    return pl.pallas_call(
        kernel,
        out_shape=out_shape,
        in_specs=specs,
        out_specs=out_specs or jax.tree.map(lambda _: VMEM, out_shape),
        scratch_shapes=scratch,
        compiler_params=pltpu.CompilerParams(vmem_limit_bytes=int(room * 2**20)),
        cost_estimate=pl.CostEstimate(transcendentals=0, **cost),
    )


def per_device(forward_fields, adjoint_now, adjoint_prev, courant_sq, receiver_cells, traces):
    shape = adjoint_now.shape
    size_x, size_y, size_z = shape
    rows, cols = lax.axis_size("row"), lax.axis_size("col")
    both = ("row", "col")
    spot = lax.axis_index(both).reshape(1)
    placed = functools.partial(functools.partial, with_flags, rows, cols)
    spots = receiver_cells.reshape(1, -1)
    values = traces.reshape(STEPS, -1)
    basis_z = basis(KZ, size_z)
    table_z = jnp.asarray(basis_z, jnp.float32)
    table_z_scaled = jnp.asarray(basis_z * TWELFTH, jnp.float32)
    table_y = jnp.asarray(basis(KY, cols * size_y), jnp.float32)
    basis_x = basis(KX, rows * size_x)
    low_pass = (basis_x.T @ basis_x)[0]
    span = rows // GROUP
    own = span * size_x
    place = (np.arange(span)[:, None] * GROUP * size_x + np.arange(size_x)[None, :]).reshape(-1)
    gap = place[:, None] - place[None, :]
    table_x = jnp.asarray(
        np.stack([low_pass[(gap + k * size_x) % low_pass.size] for k in range(1 - GROUP, GROUP)]),
        jnp.float32,
    )

    field = jax.ShapeDtypeStruct(shape, jnp.float32)
    x_face = jax.ShapeDtypeStruct((2, size_y, size_z), jnp.float32)
    y_face = jax.ShapeDtypeStruct((size_x, 2, size_z), jnp.float32)
    chunks = jax.ShapeDtypeStruct((KZ, 8, 128), jnp.float32)
    swaps = [[], [], [], []]
    for r in range(rows):
        for c in range(cols):
            up, right = r + 2 * (r % 2) - 1, c + 2 * (c % 2) - 1
            targets = (
                (r ^ 1, c),
                (up, c) if 0 <= up < rows else (r, c ^ 1),
                (r, c ^ 1),
                (r, right) if 0 <= right < cols else (r ^ 1, c),
            )
            for pairs, (to_row, to_col) in zip(swaps, targets):
                pairs.append((r * cols + c, to_row * cols + to_col))
    heavy = dict(flops=2 * 10**9, bytes_accessed=7 * 2**20)
    light = dict(flops=10**6, bytes_accessed=2**18)
    whole = pltpu.VMEM(shape, jnp.float32)
    blocks = size_x * size_y // ROWS

    now, *faces = call(
        placed(pack),
        (field, x_face, x_face, y_face, y_face),
        [SMEM, HBM],
        scratch=[DMA((4,))],
        room=PACK_ROOM,
        **light,
    )(spot, adjoint_now)
    halo = gradient = prev = None
    for step in range(STEPS):
        sent = [lax.ppermute(face, both, pairs) for face, pairs in zip(faces, swaps)]
        if step == 0:
            base, lap = call(
                first_step,
                (field, field),
                [VMEM, HBM, VMEM, VMEM],
                scratch=[whole, DMA((blocks,))],
                room=FIRST_ROOM,
                **heavy,
            )(now, adjoint_prev, spots, values)
        else:
            last = step == STEPS - 1
            operands = (spot, *halo, base, lap, now, courant_sq, forward_fields, spots, values)
            if step > 1:
                operands += (gradient,)
            prev = now
            results = call(
                placed(functools.partial(later_step, step)),
                (field,) * (3 if last else 4),
                [SMEM] + [VMEM] * (len(operands) - 1),
                **heavy,
            )(*operands)
            now, lap, gradient = results[:3]
            base = None if last else results[3]
        halo = sent
        if step < STEPS - 1:
            faces = call(
                placed(faces_after), (x_face, x_face, y_face, y_face), [SMEM] + [VMEM] * 7, **light
            )(spot, *halo, courant_sq, base, lap)
    coef = call(placed(project_z), chunks, [SMEM] + [VMEM] * 7, **light)(
        spot, *halo, forward_fields, gradient, table_z_scaled
    )
    final_now, final_prev = call(
        placed(finish),
        (field, field),
        [SMEM] + [VMEM] * 10,
        out_specs=(HBM, HBM),
        scratch=[whole, DMA((1 + blocks,))],
        **heavy,
    )(spot, *halo, now, lap, prev, courant_sq, spots, values)

    groups = [
        [(m * GROUP + g) * cols + c for m in range(span) for c in range(cols)] for g in range(GROUP)
    ]
    coef = lax.all_to_all(coef, both, 0, 0, axis_index_groups=groups, tiled=True)
    plane = jax.ShapeDtypeStruct((own, KY), jnp.float32)
    wide = pltpu.VMEM((own, cols * size_y), jnp.float32)
    mine = call(project_y, plane, [VMEM] * 2, scratch=[wide], **light)(coef, table_y)
    others = [
        lax.ppermute(mine, "row", [(i, i ^ k) for i in range(rows)]) for k in range(1, GROUP)
    ]
    coef = call(
        placed(smooth_plane),
        chunks,
        [SMEM] + [VMEM] * 6,
        out_specs=HBM,
        scratch=[wide, pltpu.VMEM(chunks.shape, jnp.float32), DMA((GROUP,))],
        **light,
    )(
        spot, mine, *others, table_x, table_y
    )
    coef = lax.all_to_all(coef, both, 0, 0, axis_index_groups=groups, tiled=True)
    smoothed = call(
        expand_z,
        field,
        [VMEM] * 2,
        out_specs=HBM,
        scratch=[pltpu.VMEM((8, 4, size_y, size_z), jnp.float32), DMA((8, 4))],
        **light,
    )(coef, table_z)
    return (smoothed, final_now, final_prev)


def solution(mesh):
    in_specs = (
        P(None, "row", "col", None),
        P("row", "col", None),
        P("row", "col", None),
        P("row", "col", None),
        P("row", "col", None),
        P("row", "col", None, None),
    )
    out_specs = (P("row", "col", None), P("row", "col", None), P("row", "col", None))
    return jax.shard_map(
        per_device, mesh=mesh, in_specs=in_specs, out_specs=out_specs, check_vma=False
    )
```

time: 111 us -> 95 us (0.86)
  starting transfers between devices: 41.1 us -> 29.5 us
  Pallas kernels: 23 us -> 15.3 us
  waiting for transfers between devices: 12.6 us -> 15.9 us
    ppermute x19, starting transfers between devices: 34.9 us -> 23.1 us  [the longest x16 19.6 us: per_device(): lax.ppermute(face, both, pairs)]
    pallas_call x11, Pallas kernels: 20.6 us -> 12.9 us  [the longest x3 4.79 us: per_device(): call(placed(functools.partial(later_step, step)), (field,) * (3 if last e...]
    ppermute x19, waiting for transfers between devices: 5.9 us -> 8 us  [the longest x16 4.37 us: per_device(): lax.ppermute(face, both, pairs)]
    all_to_all x1, waiting for transfers between devices: 6.73 us -> 7.91 us  [per_device(): lax.all_to_all(coef, both, 0, 0, axis_index_groups=groups, tiled=True)]
    unnamed x26 -> x28, local copies, waits for them, and re-layouts: 3.87 us -> 3.88 us
  transfers between devices with their start and end apart: 20 -> 20, of which waited for: 5 -> 6; matrix products, arithmetic and copies ran while one was open for 0% -> 0% of each run, Pallas kernels for 12% -> 9%
where the time goes in v2:
time: 95 us; the launch traced here: 93.8 us
  starting transfers between devices  29.5 us (31%)
  blocking collectives  28.2 us (30%)
  waiting for transfers between devices  15.9 us (17%)
  Pallas kernels  15.3 us (16%)
  local copies, waits for them, and re-layouts  3.88 us (4%)
  between operations  1.09 us (1%)
    all_to_all x1, blocking collectives, per_device(): lax.all_to_all(coef, both, 0, 0, axis_index_groups=groups, tiled=True)  28.2 us
    ppermute x16, starting transfers between devices, per_device(): lax.ppermute(face, both, pairs)  19.6 us
    all_to_all x1, waiting for transfers between devices, per_device(): lax.all_to_all(coef, both, 0, 0, axis_index_groups=groups, tiled=True)  7.91 us
    all_to_all x1, starting transfers between devices, per_device(): lax.all_to_all(coef, both, 0, 0, axis_index_groups=groups, tiled=True)  6.39 us
    pallas_call x3, Pallas kernels, per_device(): call(placed(functools.partial(later_step, step)), (field,) * (3 if last e...  4.79 us
    ppermute x16, waiting for transfers between devices, per_device(): lax.ppermute(face, both, pairs)  4.37 us
    unnamed x28, local copies, waits for them, and re-layouts  3.88 us
    ppermute x3, waiting for transfers between devices, per_device(): lax.ppermute(mine, 'row', [(i, i ^ k) for i in range(rows)])  3.63 us
  transfers between devices with their start and end apart: 20, of which 6 were waited for; matrix products, arithmetic and copies ran while one was open for 0% of the time, Pallas kernels for 9%

profile of v2, /device:TPU:16, one launch (start us, length us, event | category | flops | bytes accessed | tf_op | source)
XLA Modules:
  0.0 93.8 jit_solution(3818093368466348888)
XLA Ops:
  0.6 1.3 %shard_map.121 = (f32[32,32,256]{2,1,0:T(8,128)S(1)}, f32[2,32,256]{2,1,0:T(8,128)S(1)}, f32[2,32,256]{2,1,0:T(8,128)S(1)}, f32[32,2,256]{2,1,0:T(2,128)S(1)}, f32[32,2,256]{2,1,0:T(2,128)S(1)}) custom-call(s32[1]{0:T(128)} %bitcast.spot, f32[32,32,256]{2,1,0:T(8,128)} %refs_0_.1), custom_call_target="tpu_custom_call" | custom-call | flops 1000000 | bytes 262144 | tf_op jit(solution)/shard_map/pallas_call | solution.py:388
  1.9 0.1 collective-permute-start
  2.0 2.2 %collective-permute-start.1 = (f32[2,32,256]{2,1,0:T(8,128)S(1)}, f32[2,32,256]{2,1,0:T(8,128)S(1)}, u32[]{:S(2)}, u32[]{:S(2)}) collective-permute-start(f32[2,32,256]{2,1,0:T(8,128)S(1)} %get-tuple-element.36), channel_id=1, source_target_pairs={{0,1},{1,0},{2,3},{3,2},{4,5},{5,4},{6,7},{7,6},{8,9},{9,8},{10,11... | collective-permute-start | bytes 196616 | tf_op jit(solution)/shard_map/ppermute | solution.py:398
  4.2 0.4 collective-permute-start.2
  4.6 0.7 collective-permute-start.3
  5.4 0.7 copy-done.6
  6.1 0.7 copy-done.8
  6.8 1.6 %shard_map.122 = (f32[32,32,256]{2,1,0:T(8,128)S(1)}, f32[32,32,256]{2,1,0:T(8,128)S(1)}) custom-call(f32[32,32,256]{2,1,0:T(8,128)S(1)} %get-tuple-element.39.now.refs_6_, f32[32,32,256]{2,1,0:T(8,128)} %prev_hbm.1, s32[1,512]{1,0:T(1,128)S(1)} %bitcast.8, f32[4,512]{1,0:T(4,128)S(1)} %bitcast.3), custom_call_target="tpu_custom_call" | custom-call | flops 2000000000 | bytes 7340032 | tf_op jit(solution)/shard_map/pallas_call | solution.py:400
  8.4 0.0 collective-permute-done.2.refs_2_
  8.5 0.3 shard_map.123
  8.8 0.4 collective-permute-start.4
  9.2 2.1 %collective-permute-start.5 = (f32[2,32,256]{2,1,0:T(8,128)S(1)}, f32[2,32,256]{2,1,0:T(8,128)S(1)}, u32[]{:S(2)}, u32[]{:S(2)}) collective-permute-start(f32[2,32,256]{2,1,0:T(8,128)S(1)} %get-tuple-element.43), channel_id=1, source_target_pairs={{0,1},{1,0},{2,3},{3,2},{4,5},{5,4},{6,7},{7,6},{8,9},{9,8},{10,11... | collective-permute-start | bytes 196616 | tf_op jit(solution)/shard_map/ppermute | solution.py:398
  11.3 2.7 %collective-permute-start.6 = (f32[32,2,256]{2,1,0:T(2,128)S(1)}, f32[32,2,256]{2,1,0:T(2,128)S(1)}, u32[]{:S(2)}, u32[]{:S(2)}) collective-permute-start(f32[32,2,256]{2,1,0:T(2,128)S(1)} %get-tuple-element.44), channel_id=1, source_target_pairs={{0,1},{1,0},{2,3},{3,2},{4,5},{5,4},{6,7},{7,6},{8,9},{9,8},{10,11... | collective-permute-start | bytes 196616 | tf_op jit(solution)/shard_map/ppermute | solution.py:398
  14.0 0.7 collective-permute-start.7
  14.7 1.8 %shard_map.124 = (f32[32,32,256]{2,1,0:T(8,128)S(1)}, f32[32,32,256]{2,1,0:T(8,128)S(1)}, f32[32,32,256]{2,1,0:T(8,128)S(1)}, f32[32,32,256]{2,1,0:T(8,128)S(1)}) custom-call(s32[1]{0:T(128)} %bitcast.spot, f32[2,32,256]{2,1,0:T(8,128)S(1)} %collective-permute-done.refs_0_, f32[2,32,256]{2,1,0:T(8,128)S(1)} %collective-permute-done.1.refs_1_, ...), custom_call_target="tpu_custom_call" | custom-call | flops 2000000000 | bytes 7340032 | tf_op jit(solution)/shard_map/pallas_call | solution.py:414
  16.6 1.0 %collective-permute-done.6.refs_2_ = f32[32,2,256]{2,1,0:T(2,128)S(1)} collective-permute-done((f32[32,2,256]{2,1,0:T(2,128)S(1)}, f32[32,2,256]{2,1,0:T(2,128)S(1)}, u32[]{:S(2)}, u32[]{:S(2)}) %collective-permute-start.6) | collective-permute-done | bytes 65568 | tf_op jit(solution)/shard_map/ppermute | solution.py:398
  17.6 0.3 shard_map.125
  18.0 2.8 %collective-permute-start.10 = (f32[32,2,256]{2,1,0:T(2,128)S(1)}, f32[32,2,256]{2,1,0:T(2,128)S(1)}, u32[]{:S(2)}, u32[]{:S(2)}) collective-permute-start(f32[32,2,256]{2,1,0:T(2,128)S(1)} %get-tuple-element.50), channel_id=1, source_target_pairs={{0,1},{1,0},{2,3},{3,2},{4,5},{5,4},{6,7},{7,6},{8,9},{9,8},{10,11... | collective-permute-start | bytes 196616 | tf_op jit(solution)/shard_map/ppermute | solution.py:398
  20.7 0.5 collective-permute-start.8
  21.2 0.4 collective-permute-start.9
  21.7 1.8 %shard_map.126 = (f32[32,32,256]{2,1,0:T(8,128)S(1)}, f32[32,32,256]{2,1,0:T(8,128)S(1)}, f32[32,32,256]{2,1,0:T(8,128)S(1)}, f32[32,32,256]{2,1,0:T(8,128)S(1)}) custom-call(s32[1]{0:T(128)} %bitcast.spot, f32[2,32,256]{2,1,0:T(8,128)S(1)} %collective-permute-done.4.refs_0_, f32[2,32,256]{2,1,0:T(8,128)S(1)} %collective-permute-done.5.refs_1_, ...), custom_call_target="tpu_custom_call" | custom-call | flops 2000000000 | bytes 7340032 | tf_op jit(solution)/shard_map/pallas_call | solution.py:414
  23.5 0.5 collective-permute-done.10.refs_2_
  24.0 2.8 %collective-permute-done.9.refs_1_ = f32[2,32,256]{2,1,0:T(8,128)S(1)} collective-permute-done((f32[2,32,256]{2,1,0:T(8,128)S(1)}, f32[2,32,256]{2,1,0:T(8,128)S(1)}, u32[]{:S(2)}, u32[]{:S(2)}) %collective-permute-start.9) | collective-permute-done | bytes 65568 | tf_op jit(solution)/shard_map/ppermute | solution.py:398
  26.8 0.3 shard_map.127
  27.1 0.7 collective-permute-start.12
  27.9 0.7 collective-permute-start.13
  28.6 2.5 %collective-permute-start.14 = (f32[32,2,256]{2,1,0:T(2,128)S(1)}, f32[32,2,256]{2,1,0:T(2,128)S(1)}, u32[]{:S(2)}, u32[]{:S(2)}) collective-permute-start(f32[32,2,256]{2,1,0:T(2,128)S(1)} %get-tuple-element.58), channel_id=1, source_target_pairs={{0,1},{1,0},{2,3},{3,2},{4,5},{5,4},{6,7},{7,6},{8,9},{9,8},{10,11... | collective-permute-start | bytes 196616 | tf_op jit(solution)/shard_map/ppermute | solution.py:398
  31.0 2.6 %collective-permute-start.15 = (f32[32,2,256]{2,1,0:T(2,128)S(1)}, f32[32,2,256]{2,1,0:T(2,128)S(1)}, u32[]{:S(2)}, u32[]{:S(2)}) collective-permute-start(f32[32,2,256]{2,1,0:T(2,128)S(1)} %get-tuple-element.59), channel_id=1, source_target_pairs={{0,16},{1,2},{2,1},{3,4},{4,3},{5,6},{6,5},{7,8},{8,7},{9,10},{10,... | collective-permute-start | bytes 196616 | tf_op jit(solution)/shard_map/ppermute | solution.py:398
  33.7 1.2 %shard_map.128 = (f32[32,32,256]{2,1,0:T(8,128)S(1)}, f32[32,32,256]{2,1,0:T(8,128)S(1)}, f32[32,32,256]{2,1,0:T(8,128)S(1)}) custom-call(s32[1]{0:T(128)} %bitcast.spot, f32[2,32,256]{2,1,0:T(8,128)S(1)} %collective-permute-done.8.refs_0_, f32[2,32,256]{2,1,0:T(8,128)S(1)} %collective-permute-done.9.refs_1_, ...), custom_call_target="tpu_custom_call" | custom-call | flops 2000000000 | bytes 7340032 | tf_op jit(solution)/shard_map/pallas_call | solution.py:414
  34.8 0.0 copy-start.12
  34.9 0.0 copy-start.2
  34.9 0.0 copy-start.3
  34.9 0.8 shard_map.129
  35.7 0.0 copy-start.7
  35.7 28.2 %all_to_all.10.chunks = f32[64,8,128]{2,1,0:T(8,128)S(1)} all-to-all(f32[64,8,128]{2,1,0:T(8,128)S(1)} %shard_map.129), channel_id=1, replica_groups={{0,1,2,3,4,5,6,7,8,9,10,11,12,13,14,15,64,65,66,67,68,69,70,71,72,73,74..., dimensions={0} | all-to-all | bytes 524288 | tf_op jit(solution)/shard_map/all_to_all | solution.py:442
  64.0 0.5 shard_map.130.refs_0_
  64.5 0.1 collective-permute-start.16
  64.6 1.2 %collective-permute-start.17 = (f32[128,128]{1,0:T(8,128)S(1)}, f32[128,128]{1,0:T(8,128)S(1)}, u32[]{:S(2)}, u32[]{:S(2)}) collective-permute-start(f32[128,128]{1,0:T(8,128)S(1)} %shard_map.130.refs_0_), channel_id=1, source_target_pairs={{0,32},{16,48},{32,0},{48,16},{64,96},{80,112},{96,64},{112,80},{1... | collective-permute-start | bytes 196616 | tf_op jit(solution)/shard_map/ppermute | solution.py:447
  65.7 2.2 %collective-permute-start.18 = (f32[128,128]{1,0:T(8,128)S(1)}, f32[128,128]{1,0:T(8,128)S(1)}, u32[]{:S(2)}, u32[]{:S(2)}) collective-permute-start(f32[128,128]{1,0:T(8,128)S(1)} %shard_map.130.refs_0_), channel_id=1, source_target_pairs={{0,48},{16,32},{32,16},{48,0},{64,112},{80,96},{96,80},{112,64},{1... | collective-permute-start | bytes 196616 | tf_op jit(solution)/shard_map/ppermute | solution.py:447
  67.9 3.1 %collective-permute-done.17.refs_2_ = f32[128,128]{1,0:T(8,128)S(1)} collective-permute-done((f32[128,128]{1,0:T(8,128)S(1)}, f32[128,128]{1,0:T(8,128)S(1)}, u32[]{:S(2)}, u32[]{:S(2)}) %collective-permute-start.17) | collective-permute-done | bytes 65568 | tf_op jit(solution)/shard_map/ppermute | solution.py:447
  71.0 0.6 collective-permute-done.18.refs_3_
  71.6 1.4 %shard_map.131 = f32[64,8,128]{2,1,0:T(8,128)} custom-call(s32[1]{0:T(128)} %bitcast.spot, f32[128,128]{1,0:T(8,128)S(1)} %shard_map.130.refs_0_, f32[128,128]{1,0:T(8,128)S(1)} %collective-permute-done.16.refs_1_, f32[128,128]{1,0:T(8,128)S(1)} %collective-permute-done.17.refs_2_, f32[128,128]{1,0:T(8,128)S(1)} %collective-permute-done.18.refs_3_, ...), custom_call_target="tpu_custom_call" | custom-call | flops 1000000 | bytes 262144 | tf_op jit(solution)/shard_map/pallas_call | solution.py:449
  72.9 6.4 %all-to-all-start.1 = ((f32[64,8,128]{2,1,0:T(8,128)}), f32[64,8,128]{2,1,0:T(8,128)S(1)}, u32[]{:S(2)}, u32[]{:S(2)}) async-start(f32[64,8,128]{2,1,0:T(8,128)} %shard_map.131), calls=%async_computation.1 | async-start | bytes 524288 | tf_op jit(solution)/shard_map/all_to_all | solution.py:459
  79.4 1.2 %copy-done.11 = f32[32,32,256]{2,1,0:T(8,128)S(1)} copy-done((f32[32,32,256]{2,1,0:T(8,128)S(1)}, f32[32,32,256]{2,1,0:T(8,128)}, u32[]{:S(2)}) %copy-start.11) | copy-done | bytes 1048600
  80.6 1.2 %copy-done.13 = f32[32,32,256]{2,1,0:T(8,128)S(1)} copy-done((f32[32,32,256]{2,1,0:T(8,128)S(1)}, f32[32,32,256]{2,1,0:T(8,128)}, u32[]{:S(2)}) %copy-start.13) | copy-done | bytes 1048600
  81.8 2.0 %shard_map.133 = (f32[32,32,256]{2,1,0:T(8,128)}, f32[32,32,256]{2,1,0:T(8,128)}) custom-call(s32[1]{0:T(128)} %bitcast.spot, f32[2,32,256]{2,1,0:T(8,128)S(1)} %collective-permute-done.12.refs_0_, f32[2,32,256]{2,1,0:T(8,128)S(1)} %collective-permute-done.13.refs_1_, f32[32,2,256]{2,1,0:T(2,128)S(1)} %collective-permute-done.14.refs_2_, ...), custom_call_target="tpu_custom_call" | custom-call | flops 2000000000 | bytes 7340032 | tf_op jit(solution)/shard_map/pallas_call | solution.py:430
  83.8 7.9 %all-to-all-done.1.coef = f32[64,8,128]{2,1,0:T(8,128)S(1)} async-done(((f32[64,8,128]{2,1,0:T(8,128)}), f32[64,8,128]{2,1,0:T(8,128)S(1)}, u32[]{:S(2)}, u32[]{:S(2)}) %all-to-all-start.1) | async-done | bytes 262176 | tf_op jit(solution)/shard_map/all_to_all | solution.py:459
  91.7 1.9 %shard_map.132 = f32[32,32,256]{2,1,0:T(8,128)} custom-call(f32[64,8,128]{2,1,0:T(8,128)S(1)} %all-to-all-done.1.coef, f32[64,256]{1,0:T(8,128)S(1)} %copy-done.5), custom_call_target="tpu_custom_call" | custom-call | flops 1000000 | bytes 262144 | tf_op jit(solution)/shard_map/pallas_call | solution.py:460
  (34 shorter events, 0.1 us)
Async XLA Ops:
  1.9 6.5 %collective-permute-start = (f32[2,32,256]{2,1,0:T(8,128)S(1)}, f32[2,32,256]{2,1,0:T(8,128)S(1)}, u32[]{:S(2)}, u32[]{:S(2)}) collective-permute-start(f32[2,32,256]{2,1,0:T(8,128)S(1)} %get-tuple-element.35), channel_id=1, source_target_pairs={{0,16},{1,17},{2,18},{3,19},{4,20},{5,21},{6,22},{7,23},{8,24},{9,... | collective-permute-start | bytes 196616 | tf_op jit(solution)/shard_map/ppermute | solution.py:398
  2.0 6.4 %collective-permute-start.1 = (f32[2,32,256]{2,1,0:T(8,128)S(1)}, f32[2,32,256]{2,1,0:T(8,128)S(1)}, u32[]{:S(2)}, u32[]{:S(2)}) collective-permute-start(f32[2,32,256]{2,1,0:T(8,128)S(1)} %get-tuple-element.36), channel_id=1, source_target_pairs={{0,1},{1,0},{2,3},{3,2},{4,5},{5,4},{6,7},{7,6},{8,9},{9,8},{10,11... | collective-permute-start | bytes 196616 | tf_op jit(solution)/shard_map/ppermute | solution.py:398
  4.2 4.3 %collective-permute-start.2 = (f32[32,2,256]{2,1,0:T(2,128)S(1)}, f32[32,2,256]{2,1,0:T(2,128)S(1)}, u32[]{:S(2)}, u32[]{:S(2)}) collective-permute-start(f32[32,2,256]{2,1,0:T(2,128)S(1)} %get-tuple-element.37), channel_id=1, source_target_pairs={{0,1},{1,0},{2,3},{3,2},{4,5},{5,4},{6,7},{7,6},{8,9},{9,8},{10,11... | collective-permute-start | bytes 196616 | tf_op jit(solution)/shard_map/ppermute | solution.py:398
  4.6 3.8 %collective-permute-start.3 = (f32[32,2,256]{2,1,0:T(2,128)S(1)}, f32[32,2,256]{2,1,0:T(2,128)S(1)}, u32[]{:S(2)}, u32[]{:S(2)}) collective-permute-start(f32[32,2,256]{2,1,0:T(2,128)S(1)} %get-tuple-element.38), channel_id=1, source_target_pairs={{0,16},{1,2},{2,1},{3,4},{4,3},{5,6},{6,5},{7,8},{8,7},{9,10},{10,... | collective-permute-start | bytes 196616 | tf_op jit(solution)/shard_map/ppermute | solution.py:398
  5.4 0.7 copy-start.6
  6.1 0.7 copy-start.8
  6.8 1.7 %copy-start = (f32[32,32,256]{2,1,0:T(8,128)S(1)}, f32[32,32,256]{2,1,0:T(8,128)}, u32[]{:S(2)}) copy-start(f32[32,32,256]{2,1,0:T(8,128)} %refs_7_.7) | copy-start | bytes 3145732
  8.4 6.3 %copy-start.1 = (bf16[4,32,32,256]{3,2,1,0:T(8,128)(2,1)S(1)}, bf16[4,32,32,256]{3,2,1,0:T(8,128)(2,1)}, u32[]{:S(2)}) copy-start(bf16[4,32,32,256]{3,2,1,0:T(8,128)(2,1)} %refs_4_.8) | copy-start | bytes 6291460
  8.8 7.8 %collective-permute-start.4 = (f32[2,32,256]{2,1,0:T(8,128)S(1)}, f32[2,32,256]{2,1,0:T(8,128)S(1)}, u32[]{:S(2)}, u32[]{:S(2)}) collective-permute-start(f32[2,32,256]{2,1,0:T(8,128)S(1)} %get-tuple-element.42), channel_id=1, source_target_pairs={{0,16},{1,17},{2,18},{3,19},{4,20},{5,21},{6,22},{7,23},{8,24},{9,... | collective-permute-start | bytes 196616 | tf_op jit(solution)/shard_map/ppermute | solution.py:398
  9.2 7.4 %collective-permute-start.5 = (f32[2,32,256]{2,1,0:T(8,128)S(1)}, f32[2,32,256]{2,1,0:T(8,128)S(1)}, u32[]{:S(2)}, u32[]{:S(2)}) collective-permute-start(f32[2,32,256]{2,1,0:T(8,128)S(1)} %get-tuple-element.43), channel_id=1, source_target_pairs={{0,1},{1,0},{2,3},{3,2},{4,5},{5,4},{6,7},{7,6},{8,9},{9,8},{10,11... | collective-permute-start | bytes 196616 | tf_op jit(solution)/shard_map/ppermute | solution.py:398
  11.3 6.3 %collective-permute-start.6 = (f32[32,2,256]{2,1,0:T(2,128)S(1)}, f32[32,2,256]{2,1,0:T(2,128)S(1)}, u32[]{:S(2)}, u32[]{:S(2)}) collective-permute-start(f32[32,2,256]{2,1,0:T(2,128)S(1)} %get-tuple-element.44), channel_id=1, source_target_pairs={{0,1},{1,0},{2,3},{3,2},{4,5},{5,4},{6,7},{7,6},{8,9},{9,8},{10,11... | collective-permute-start | bytes 196616 | tf_op jit(solution)/shard_map/ppermute | solution.py:398
  14.0 3.6 %collective-permute-start.7 = (f32[32,2,256]{2,1,0:T(2,128)S(1)}, f32[32,2,256]{2,1,0:T(2,128)S(1)}, u32[]{:S(2)}, u32[]{:S(2)}) collective-permute-start(f32[32,2,256]{2,1,0:T(2,128)S(1)} %get-tuple-element.45), channel_id=1, source_target_pairs={{0,16},{1,2},{2,1},{3,4},{4,3},{5,6},{6,5},{7,8},{8,7},{9,10},{10,... | collective-permute-start | bytes 196616 | tf_op jit(solution)/shard_map/ppermute | solution.py:398
  18.0 6.0 %collective-permute-start.10 = (f32[32,2,256]{2,1,0:T(2,128)S(1)}, f32[32,2,256]{2,1,0:T(2,128)S(1)}, u32[]{:S(2)}, u32[]{:S(2)}) collective-permute-start(f32[32,2,256]{2,1,0:T(2,128)S(1)} %get-tuple-element.50), channel_id=1, source_target_pairs={{0,1},{1,0},{2,3},{3,2},{4,5},{5,4},{6,7},{7,6},{8,9},{9,8},{10,11... | collective-permute-start | bytes 196616 | tf_op jit(solution)/shard_map/ppermute | solution.py:398
  20.7 3.2 %collective-permute-start.11 = (f32[32,2,256]{2,1,0:T(2,128)S(1)}, f32[32,2,256]{2,1,0:T(2,128)S(1)}, u32[]{:S(2)}, u32[]{:S(2)}) collective-permute-start(f32[32,2,256]{2,1,0:T(2,128)S(1)} %get-tuple-element.51), channel_id=1, source_target_pairs={{0,16},{1,2},{2,1},{3,4},{4,3},{5,6},{6,5},{7,8},{8,7},{9,10},{10,... | collective-permute-start | bytes 196616 | tf_op jit(solution)/shard_map/ppermute | solution.py:398
  20.7 3.2 %collective-permute-start.8 = (f32[2,32,256]{2,1,0:T(8,128)S(1)}, f32[2,32,256]{2,1,0:T(8,128)S(1)}, u32[]{:S(2)}, u32[]{:S(2)}) collective-permute-start(f32[2,32,256]{2,1,0:T(8,128)S(1)} %get-tuple-element.48), channel_id=1, source_target_pairs={{0,16},{1,17},{2,18},{3,19},{4,20},{5,21},{6,22},{7,23},{8,24},{9,... | collective-permute-start | bytes 196616 | tf_op jit(solution)/shard_map/ppermute | solution.py:398
  21.2 5.6 %collective-permute-start.9 = (f32[2,32,256]{2,1,0:T(8,128)S(1)}, f32[2,32,256]{2,1,0:T(8,128)S(1)}, u32[]{:S(2)}, u32[]{:S(2)}) collective-permute-start(f32[2,32,256]{2,1,0:T(8,128)S(1)} %get-tuple-element.49), channel_id=1, source_target_pairs={{0,1},{1,0},{2,3},{3,2},{4,5},{5,4},{6,7},{7,6},{8,9},{9,8},{10,11... | collective-permute-start | bytes 196616 | tf_op jit(solution)/shard_map/ppermute | solution.py:398
  27.1 7.7 %collective-permute-start.12 = (f32[2,32,256]{2,1,0:T(8,128)S(1)}, f32[2,32,256]{2,1,0:T(8,128)S(1)}, u32[]{:S(2)}, u32[]{:S(2)}) collective-permute-start(f32[2,32,256]{2,1,0:T(8,128)S(1)} %get-tuple-element.56), channel_id=1, source_target_pairs={{0,16},{1,17},{2,18},{3,19},{4,20},{5,21},{6,22},{7,23},{8,24},{9,... | collective-permute-start | bytes 196616 | tf_op jit(solution)/shard_map/ppermute | solution.py:398
  27.9 7.0 %collective-permute-start.13 = (f32[2,32,256]{2,1,0:T(8,128)S(1)}, f32[2,32,256]{2,1,0:T(8,128)S(1)}, u32[]{:S(2)}, u32[]{:S(2)}) collective-permute-start(f32[2,32,256]{2,1,0:T(8,128)S(1)} %get-tuple-element.57), channel_id=1, source_target_pairs={{0,1},{1,0},{2,3},{3,2},{4,5},{5,4},{6,7},{7,6},{8,9},{9,8},{10,11... | collective-permute-start | bytes 196616 | tf_op jit(solution)/shard_map/ppermute | solution.py:398
  28.6 6.3 %collective-permute-start.14 = (f32[32,2,256]{2,1,0:T(2,128)S(1)}, f32[32,2,256]{2,1,0:T(2,128)S(1)}, u32[]{:S(2)}, u32[]{:S(2)}) collective-permute-start(f32[32,2,256]{2,1,0:T(2,128)S(1)} %get-tuple-element.58), channel_id=1, source_target_pairs={{0,1},{1,0},{2,3},{3,2},{4,5},{5,4},{6,7},{7,6},{8,9},{9,8},{10,11... | collective-permute-start | bytes 196616 | tf_op jit(solution)/shard_map/ppermute | solution.py:398
  31.0 3.9 %collective-permute-start.15 = (f32[32,2,256]{2,1,0:T(2,128)S(1)}, f32[32,2,256]{2,1,0:T(2,128)S(1)}, u32[]{:S(2)}, u32[]{:S(2)}) collective-permute-start(f32[32,2,256]{2,1,0:T(2,128)S(1)} %get-tuple-element.59), channel_id=1, source_target_pairs={{0,16},{1,2},{2,1},{3,4},{4,3},{5,6},{6,5},{7,8},{8,7},{9,10},{10,... | collective-permute-start | bytes 196616 | tf_op jit(solution)/shard_map/ppermute | solution.py:398
  33.7 1.2 %copy-start.4 = (f32[64,256]{1,0:T(8,128)S(1)}, f32[64,256]{1,0:T(8,128)}, u32[]{:S(2)}) copy-start(f32[64,256]{1,0:T(8,128)} %constant.18.clone.refs_6_) | copy-start | bytes 196612
  34.8 29.1 %copy-start.10 = (f32[32,32,256]{2,1,0:T(8,128)}, f32[32,32,256]{2,1,0:T(8,128)S(1)}, u32[]{:S(2)}) copy-start(f32[32,32,256]{2,1,0:T(8,128)S(1)} %get-tuple-element.63.refs_4_) | copy-start | bytes 3145732
  34.8 29.1 %copy-start.12 = (f32[32,32,256]{2,1,0:T(8,128)}, f32[32,32,256]{2,1,0:T(8,128)S(1)}, u32[]{:S(2)}) copy-start(f32[32,32,256]{2,1,0:T(8,128)S(1)} %get-tuple-element.64.refs_5_) | copy-start | bytes 3145732
  34.9 29.1 %copy-start.2 = (f32[128,512]{1,0:T(8,128)S(1)}, f32[128,512]{1,0:T(8,128)}, u32[]{:S(2)}) copy-start(f32[128,512]{1,0:T(8,128)} %constant.19.clone.table_y.refs_5_) | copy-start | bytes 786436
  34.9 36.7 %copy-start.3 = (f32[7,128,128]{2,1,0:T(8,128)S(1)}, f32[7,128,128]{2,1,0:T(8,128)}, u32[]{:S(2)}) copy-start(f32[7,128,128]{2,1,0:T(8,128)} %constant.20.clone.refs_4_) | copy-start | bytes 1376260
  35.7 43.6 %copy-start.7 = (f32[1,1,4,512]{3,2,1,0:T(4,128)S(1)}, f32[1,1,4,512]{3,2,1,0:T(4,128)}, u32[]{:S(2)}) copy-start(f32[1,1,4,512]{3,2,1,0:T(4,128)} %param.15) | copy-start | bytes 24580
  35.7 43.6 %copy-start.9 = (s32[1,1,512]{2,1,0:T(1,128)S(1)}, s32[1,1,512]{2,1,0:T(1,128)}, u32[]{:S(2)}) copy-start(s32[1,1,512]{2,1,0:T(1,128)} %param.14) | copy-start | bytes 6148
  64.5 3.5 %collective-permute-start.16 = (f32[128,128]{1,0:T(8,128)S(1)}, f32[128,128]{1,0:T(8,128)S(1)}, u32[]{:S(2)}, u32[]{:S(2)}) collective-permute-start(f32[128,128]{1,0:T(8,128)S(1)} %shard_map.130.refs_0_), channel_id=1, source_target_pairs={{0,16},{16,0},{32,48},{48,32},{64,80},{80,64},{96,112},{112,96},{1... | collective-permute-start | bytes 196616 | tf_op jit(solution)/shard_map/ppermute | solution.py:447
  64.6 6.4 %collective-permute-start.17 = (f32[128,128]{1,0:T(8,128)S(1)}, f32[128,128]{1,0:T(8,128)S(1)}, u32[]{:S(2)}, u32[]{:S(2)}) collective-permute-start(f32[128,128]{1,0:T(8,128)S(1)} %shard_map.130.refs_0_), channel_id=1, source_target_pairs={{0,32},{16,48},{32,0},{48,16},{64,96},{80,112},{96,64},{112,80},{1... | collective-permute-start | bytes 196616 | tf_op jit(solution)/shard_map/ppermute | solution.py:447
  65.7 5.8 %collective-permute-start.18 = (f32[128,128]{1,0:T(8,128)S(1)}, f32[128,128]{1,0:T(8,128)S(1)}, u32[]{:S(2)}, u32[]{:S(2)}) collective-permute-start(f32[128,128]{1,0:T(8,128)S(1)} %shard_map.130.refs_0_), channel_id=1, source_target_pairs={{0,48},{16,32},{32,16},{48,0},{64,112},{80,96},{96,80},{112,64},{1... | collective-permute-start | bytes 196616 | tf_op jit(solution)/shard_map/ppermute | solution.py:447
  72.9 18.8 %all-to-all-start.1 = ((f32[64,8,128]{2,1,0:T(8,128)}), f32[64,8,128]{2,1,0:T(8,128)S(1)}, u32[]{:S(2)}, u32[]{:S(2)}) async-start(f32[64,8,128]{2,1,0:T(8,128)} %shard_map.131), calls=%async_computation.1 | async-start | bytes 524288 | tf_op jit(solution)/shard_map/all_to_all | solution.py:459
  79.4 1.2 %copy-start.11 = (f32[32,32,256]{2,1,0:T(8,128)S(1)}, f32[32,32,256]{2,1,0:T(8,128)}, u32[]{:S(2)}) copy-start(f32[32,32,256]{2,1,0:T(8,128)} %copy-done.10) | copy-start | bytes 3145732
  80.6 1.2 %copy-start.13 = (f32[32,32,256]{2,1,0:T(8,128)S(1)}, f32[32,32,256]{2,1,0:T(8,128)}, u32[]{:S(2)}) copy-start(f32[32,32,256]{2,1,0:T(8,128)} %copy-done.12) | copy-start | bytes 3145732
  81.8 9.9 %copy-start.5 = (f32[64,256]{1,0:T(8,128)S(1)}, f32[64,256]{1,0:T(8,128)}, u32[]{:S(2)}) copy-start(f32[64,256]{1,0:T(8,128)} %constant.17.clone.table_z) | copy-start | bytes 196612

commit v3 on v2

--- a/solution.py
+++ b/solution.py
@@ -17,6 +17,7 @@
 TWELFTH = 1.0 / 12.0
 PACK_ROOM = 52
 FIRST_ROOM = 50
+ORDER = (1, 3, 2, 0)
 
 HBM = pl.BlockSpec(memory_space=pltpu.HBM)
 VMEM = pl.BlockSpec(memory_space=pltpu.VMEM)
@@ -79,7 +80,7 @@
     kernel(flags, *refs)
 
 
-def pack(flags, now_hbm, now, x_even, x_odd, y_even, y_odd, sems):
+def pack(flags, now_hbm, now, x_odd, y_odd, y_even, x_even, sems):
     size_x, size_y, _ = now.shape
     step = size_x // 4
     copies = []
@@ -134,7 +135,7 @@
     return value + x_change[x] if x in x_change else value
 
 
-def faces_after(flags, x_even, x_odd, y_even, y_odd, courant, base, lap, out_x_even, out_x_odd, out_y_even, out_y_odd):
+def faces_after(flags, x_odd, y_odd, y_even, x_even, courant, base, lap, out_x_odd, out_y_odd, out_y_even, out_x_even):
     size_x, size_y, _ = base.shape
     x_change = x_changes(flags, x_even, x_odd, size_x)
     layers = {}
@@ -158,8 +159,8 @@
 
 
 def injection(step, cells, traces, size_z):
-    spots = cells[...]
-    value = traces[pl.ds(step, 1), :]
+    spots = cells[0]
+    value = traces[0, 0, pl.ds(step, 1), :]
     top = value.astype(jnp.bfloat16)
     rest = value - top.astype(jnp.float32)
     mid = rest.astype(jnp.bfloat16)
@@ -219,7 +220,7 @@
 
 
 def later_step(step, flags, *refs):
-    x_even, x_odd, y_even, y_odd, base_in, lap_in, prev, courant, forward, cells, traces, *refs = refs
+    x_odd, y_odd, y_even, x_even, base_in, lap_in, prev, courant, forward, cells, traces, *refs = refs
     gradient_in = refs.pop(0) if step > 1 else None
     last = step == STEPS - 1
     now, lap, gradient = refs[:3]
@@ -245,7 +246,7 @@
                 base[x] = (2.0 * now[x] - prev[x]) + inject[i]
 
 
-def finish(flags, x_even, x_odd, y_even, y_odd, now, lap, prev, courant, cells, traces, next_hbm, now_hbm, nxt, sems):
+def finish(flags, x_odd, y_odd, y_even, x_even, now, lap, prev, courant, cells, traces, next_hbm, now_hbm, nxt, sems):
     size_x, size_y, size_z = now.shape
     layers = ROWS // size_y
     keep = pltpu.make_async_copy(now, now_hbm, sems.at[0])
@@ -268,13 +269,13 @@
     keep.wait()
 
 
-def project_z(flags, x_even, x_odd, y_even, y_odd, forward, gradient, table_z, coef):
+def project_z(flags, x_odd, y_odd, y_even, x_even, forward, gradient, table_z, coef):
     size_x, size_y, _ = gradient.shape
     table = split(table_z[...])
     x_change = x_changes(flags, x_even, x_odd, size_x)
     for s in range(8):
         lines = []
-        for x in range(s, size_x, 8):
+        for x in range(4 * s, 4 * s + 4):
             first, last = y_tiles(flags, y_even, y_odd, x)
             scale = forward[STEPS - 1, x].astype(jnp.float32)
             tiles = (scale[0:8] * first, scale[size_y - 8 : size_y] * last)
@@ -321,9 +322,8 @@
         high, low = split(coef[:, s, :])
         value = dot(jnp.concatenate([high, low, high], axis=0), table, TN)
         lines[s] = value.reshape(4, size_y, size_z)
-        for q in range(4):
-            copies.append(pltpu.make_async_copy(lines.at[s, q], out.at[q * 8 + s], sems.at[s, q]))
-            copies[-1].start()
+        copies.append(pltpu.make_async_copy(lines.at[s], out.at[pl.ds(4 * s, 4)], sems.at[s]))
+        copies[-1].start()
     for copy in copies:
         copy.wait()
 
@@ -347,8 +347,6 @@
     both = ("row", "col")
     spot = lax.axis_index(both).reshape(1)
     placed = functools.partial(functools.partial, with_flags, rows, cols)
-    spots = receiver_cells.reshape(1, -1)
-    values = traces.reshape(STEPS, -1)
     basis_z = basis(KZ, size_z)
     table_z = jnp.asarray(basis_z, jnp.float32)
     table_z_scaled = jnp.asarray(basis_z * TWELFTH, jnp.float32)
@@ -357,7 +355,8 @@
     low_pass = (basis_x.T @ basis_x)[0]
     span = rows // GROUP
     own = span * size_x
-    place = (np.arange(span)[:, None] * GROUP * size_x + np.arange(size_x)[None, :]).reshape(-1)
+    cells = (np.arange(4)[:, None] + 4 * np.arange(8)[None, :]).reshape(-1)
+    place = (np.arange(span)[:, None] * GROUP * size_x + cells[None, :]).reshape(-1)
     gap = place[:, None] - place[None, :]
     table_x = jnp.asarray(
         np.stack([low_pass[(gap + k * size_x) % low_pass.size] for k in range(1 - GROUP, GROUP)]),
@@ -387,15 +386,16 @@
 
     now, *faces = call(
         placed(pack),
-        (field, x_face, x_face, y_face, y_face),
+        (field, x_face, y_face, y_face, x_face),
         [SMEM, HBM],
         scratch=[DMA((4,))],
         room=PACK_ROOM,
         **light,
     )(spot, adjoint_now)
+    spots, values = receiver_cells, traces
     halo = gradient = prev = None
     for step in range(STEPS):
-        sent = [lax.ppermute(face, both, pairs) for face, pairs in zip(faces, swaps)]
+        sent = [lax.ppermute(face, both, swaps[i]) for i, face in zip(ORDER, faces)]
         if step == 0:
             base, lap = call(
                 first_step,
@@ -422,7 +422,7 @@
         halo = sent
         if step < STEPS - 1:
             faces = call(
-                placed(faces_after), (x_face, x_face, y_face, y_face), [SMEM] + [VMEM] * 7, **light
+                placed(faces_after), (x_face, y_face, y_face, x_face), [SMEM] + [VMEM] * 7, **light
             )(spot, *halo, courant_sq, base, lap)
     coef = call(placed(project_z), chunks, [SMEM] + [VMEM] * 7, **light)(
         spot, *halo, forward_fields, gradient, table_z_scaled
@@ -443,9 +443,10 @@
     plane = jax.ShapeDtypeStruct((own, KY), jnp.float32)
     wide = pltpu.VMEM((own, cols * size_y), jnp.float32)
     mine = call(project_y, plane, [VMEM] * 2, scratch=[wide], **light)(coef, table_y)
-    others = [
-        lax.ppermute(mine, "row", [(i, i ^ k) for i in range(rows)]) for k in range(1, GROUP)
-    ]
+    beside, across = ([(i, i ^ k) for i in range(rows)] for k in (1, 2))
+    two = lax.ppermute(mine, "row", across)
+    one = lax.ppermute(mine, "row", beside)
+    others = (one, two, lax.ppermute(two, "row", beside))
     coef = call(
         placed(smooth_plane),
         chunks,
@@ -462,7 +463,7 @@
         field,
         [VMEM] * 2,
         out_specs=HBM,
-        scratch=[pltpu.VMEM((8, 4, size_y, size_z), jnp.float32), DMA((8, 4))],
+        scratch=[pltpu.VMEM((8, 4, size_y, size_z), jnp.float32), DMA((8,))],
         **light,
     )(coef, table_z)
     return (smoothed, final_now, final_prev)

time: 95 us -> 93.1 us (0.980)
  waiting for transfers between devices: 15.9 us -> 19.4 us
  starting transfers between devices: 29.5 us -> 26.5 us
  blocking collectives: 28.2 us -> 26.7 us
    ppermute x19, waiting for transfers between devices: 8 us -> 11.5 us  [the longest x16 5.13 us: per_device(): sent = [lax.ppermute(face, both, swaps[i]) for i, face in zip(ORDER, faces)]]
    ppermute x19, starting transfers between devices: 23.1 us -> 20.5 us  [the longest x16 19.7 us: per_device(): sent = [lax.ppermute(face, both, swaps[i]) for i, face in zip(ORDER, faces)]]
    all_to_all x1, blocking collectives: 28.2 us -> 26.7 us  [per_device(): lax.all_to_all(coef, both, 0, 0, axis_index_groups=groups, tiled=True)]
where the time goes in v3:
time: 93.1 us; the launch traced here: 92.7 us
  blocking collectives  26.7 us (29%)
  starting transfers between devices  26.5 us (28%)
  waiting for transfers between devices  19.4 us (21%)
  Pallas kernels  15 us (16%)
  local copies, waits for them, and re-layouts  3.88 us (4%)
  between operations  1.1 us (1%)
    all_to_all x1, blocking collectives, per_device(): lax.all_to_all(coef, both, 0, 0, axis_index_groups=groups, tiled=True)  26.7 us
    ppermute x16, starting transfers between devices, per_device(): sent = [lax.ppermute(face, both, swaps[i]) for i, face in zip(ORDER, faces)]  19.7 us
    all_to_all x1, waiting for transfers between devices, per_device(): lax.all_to_all(coef, both, 0, 0, axis_index_groups=groups, tiled=True)  7.93 us
    all_to_all x1, starting transfers between devices, per_device(): lax.all_to_all(coef, both, 0, 0, axis_index_groups=groups, tiled=True)  6.05 us
    ppermute x16, waiting for transfers between devices, per_device(): sent = [lax.ppermute(face, both, swaps[i]) for i, face in zip(ORDER, faces)]  5.13 us
    ppermute x1, waiting for transfers between devices, per_device(): two = lax.ppermute(mine, 'row', across)  5.12 us
    pallas_call x3, Pallas kernels, per_device(): call(placed(functools.partial(later_step, step)), (field,) * (3 if last e...  4.79 us
    unnamed x28, local copies, waits for them, and re-layouts  3.88 us
  transfers between devices with their start and end apart: 20, of which 6 were waited for; matrix products, arithmetic and copies ran while one was open for 0% of the time, Pallas kernels for 9%

profile of v3, /device:TPU:16, one launch (start us, length us, event | category | flops | bytes accessed | tf_op | source)
XLA Modules:
  0.0 92.7 jit_solution(9838857491874735334)
XLA Ops:
  0.6 1.3 %shard_map.121 = (f32[32,32,256]{2,1,0:T(8,128)S(1)}, f32[2,32,256]{2,1,0:T(8,128)S(1)}, f32[32,2,256]{2,1,0:T(2,128)S(1)}, f32[32,2,256]{2,1,0:T(2,128)S(1)}, f32[2,32,256]{2,1,0:T(8,128)S(1)}) custom-call(s32[1]{0:T(128)} %bitcast.spot, f32[32,32,256]{2,1,0:T(8,128)} %refs_0_.1), custom_call_target="tpu_custom_call" | custom-call | flops 1000000 | bytes 262144 | tf_op jit(solution)/shard_map/pallas_call | solution.py:387
  1.9 0.1 collective-permute-start
  2.0 1.4 %collective-permute-start.1 = (f32[32,2,256]{2,1,0:T(2,128)S(1)}, f32[32,2,256]{2,1,0:T(2,128)S(1)}, u32[]{:S(2)}, u32[]{:S(2)}) collective-permute-start(f32[32,2,256]{2,1,0:T(2,128)S(1)} %get-tuple-element.36), channel_id=1, source_target_pairs={{0,16},{1,2},{2,1},{3,4},{4,3},{5,6},{6,5},{7,8},{8,7},{9,10},{10,... | collective-permute-start | bytes 196616 | tf_op jit(solution)/shard_map/ppermute | solution.py:398
  3.4 2.1 %collective-permute-start.2 = (f32[32,2,256]{2,1,0:T(2,128)S(1)}, f32[32,2,256]{2,1,0:T(2,128)S(1)}, u32[]{:S(2)}, u32[]{:S(2)}) collective-permute-start(f32[32,2,256]{2,1,0:T(2,128)S(1)} %get-tuple-element.37), channel_id=1, source_target_pairs={{0,1},{1,0},{2,3},{3,2},{4,5},{5,4},{6,7},{7,6},{8,9},{9,8},{10,11... | collective-permute-start | bytes 196616 | tf_op jit(solution)/shard_map/ppermute | solution.py:398
  5.5 0.7 collective-permute-start.3
  6.2 0.7 copy-done.6
  6.9 0.7 copy-done.8
  7.6 1.6 %shard_map.122 = (f32[32,32,256]{2,1,0:T(8,128)S(1)}, f32[32,32,256]{2,1,0:T(8,128)S(1)}) custom-call(f32[32,32,256]{2,1,0:T(8,128)S(1)} %get-tuple-element.39.now.refs_6_, f32[32,32,256]{2,1,0:T(8,128)} %prev_hbm.1, s32[1,1,512]{2,1,0:T(1,128)S(1)} %copy-done.8, f32[1,1,4,512]{3,2,1,0:T(4,128)S(1)} %copy-done.6), custom_call_target="tpu_custom_call" | custom-call | flops 2000000000 | bytes 7340032 | tf_op jit(solution)/shard_map/pallas_call | solution.py:400
  9.2 0.0 copy-start.1
  9.3 0.3 shard_map.123
  9.6 2.0 %collective-permute-start.4 = (f32[2,32,256]{2,1,0:T(8,128)S(1)}, f32[2,32,256]{2,1,0:T(8,128)S(1)}, u32[]{:S(2)}, u32[]{:S(2)}) collective-permute-start(f32[2,32,256]{2,1,0:T(8,128)S(1)} %get-tuple-element.42), channel_id=1, source_target_pairs={{0,1},{1,0},{2,3},{3,2},{4,5},{5,4},{6,7},{7,6},{8,9},{9,8},{10,11... | collective-permute-start | bytes 196616 | tf_op jit(solution)/shard_map/ppermute | solution.py:398
  11.6 1.4 %collective-permute-start.5 = (f32[32,2,256]{2,1,0:T(2,128)S(1)}, f32[32,2,256]{2,1,0:T(2,128)S(1)}, u32[]{:S(2)}, u32[]{:S(2)}) collective-permute-start(f32[32,2,256]{2,1,0:T(2,128)S(1)} %get-tuple-element.43), channel_id=1, source_target_pairs={{0,16},{1,2},{2,1},{3,4},{4,3},{5,6},{6,5},{7,8},{8,7},{9,10},{10,... | collective-permute-start | bytes 196616 | tf_op jit(solution)/shard_map/ppermute | solution.py:398
  13.0 2.0 %collective-permute-start.6 = (f32[32,2,256]{2,1,0:T(2,128)S(1)}, f32[32,2,256]{2,1,0:T(2,128)S(1)}, u32[]{:S(2)}, u32[]{:S(2)}) collective-permute-start(f32[32,2,256]{2,1,0:T(2,128)S(1)} %get-tuple-element.44), channel_id=1, source_target_pairs={{0,1},{1,0},{2,3},{3,2},{4,5},{5,4},{6,7},{7,6},{8,9},{9,8},{10,11... | collective-permute-start | bytes 196616 | tf_op jit(solution)/shard_map/ppermute | solution.py:398
  15.1 1.2 %collective-permute-start.7 = (f32[2,32,256]{2,1,0:T(8,128)S(1)}, f32[2,32,256]{2,1,0:T(8,128)S(1)}, u32[]{:S(2)}, u32[]{:S(2)}) collective-permute-start(f32[2,32,256]{2,1,0:T(8,128)S(1)} %get-tuple-element.45), channel_id=1, source_target_pairs={{0,16},{1,17},{2,18},{3,19},{4,20},{5,21},{6,22},{7,23},{8,24},{9,... | collective-permute-start | bytes 196616 | tf_op jit(solution)/shard_map/ppermute | solution.py:398
  16.2 1.8 %shard_map.124 = (f32[32,32,256]{2,1,0:T(8,128)S(1)}, f32[32,32,256]{2,1,0:T(8,128)S(1)}, f32[32,32,256]{2,1,0:T(8,128)S(1)}, f32[32,32,256]{2,1,0:T(8,128)S(1)}) custom-call(s32[1]{0:T(128)} %bitcast.spot, f32[2,32,256]{2,1,0:T(8,128)S(1)} %collective-permute-done.refs_0_, f32[32,2,256]{2,1,0:T(2,128)S(1)} %collective-permute-done.1.refs_1_, ...), custom_call_target="tpu_custom_call" | custom-call | flops 2000000000 | bytes 7340032 | tf_op jit(solution)/shard_map/pallas_call | solution.py:414
  18.1 0.3 collective-permute-done.6.refs_2_
  18.4 0.3 shard_map.125
  18.7 2.6 %collective-permute-start.10 = (f32[32,2,256]{2,1,0:T(2,128)S(1)}, f32[32,2,256]{2,1,0:T(2,128)S(1)}, u32[]{:S(2)}, u32[]{:S(2)}) collective-permute-start(f32[32,2,256]{2,1,0:T(2,128)S(1)} %get-tuple-element.50), channel_id=1, source_target_pairs={{0,1},{1,0},{2,3},{3,2},{4,5},{5,4},{6,7},{7,6},{8,9},{9,8},{10,11... | collective-permute-start | bytes 196616 | tf_op jit(solution)/shard_map/ppermute | solution.py:398
  21.3 0.4 collective-permute-start.8
  21.7 0.8 collective-permute-start.9
  22.5 1.8 %shard_map.126 = (f32[32,32,256]{2,1,0:T(8,128)S(1)}, f32[32,32,256]{2,1,0:T(8,128)S(1)}, f32[32,32,256]{2,1,0:T(8,128)S(1)}, f32[32,32,256]{2,1,0:T(8,128)S(1)}) custom-call(s32[1]{0:T(128)} %bitcast.spot, f32[2,32,256]{2,1,0:T(8,128)S(1)} %collective-permute-done.4.refs_0_, f32[32,2,256]{2,1,0:T(2,128)S(1)} %collective-permute-done.5.refs_1_, ...), custom_call_target="tpu_custom_call" | custom-call | flops 2000000000 | bytes 7340032 | tf_op jit(solution)/shard_map/pallas_call | solution.py:414
  24.3 4.3 %collective-permute-done.8.refs_0_ = f32[2,32,256]{2,1,0:T(8,128)S(1)} collective-permute-done((f32[2,32,256]{2,1,0:T(8,128)S(1)}, f32[2,32,256]{2,1,0:T(8,128)S(1)}, u32[]{:S(2)}, u32[]{:S(2)}) %collective-permute-start.8) | collective-permute-done | bytes 65568 | tf_op jit(solution)/shard_map/ppermute | solution.py:398
  28.6 0.3 shard_map.127
  29.0 0.1 collective-permute-start.12
  29.1 0.1 collective-permute-start.13
  29.2 3.0 %collective-permute-start.14 = (f32[32,2,256]{2,1,0:T(2,128)S(1)}, f32[32,2,256]{2,1,0:T(2,128)S(1)}, u32[]{:S(2)}, u32[]{:S(2)}) collective-permute-start(f32[32,2,256]{2,1,0:T(2,128)S(1)} %get-tuple-element.58), channel_id=1, source_target_pairs={{0,1},{1,0},{2,3},{3,2},{4,5},{5,4},{6,7},{7,6},{8,9},{9,8},{10,11... | collective-permute-start | bytes 196616 | tf_op jit(solution)/shard_map/ppermute | solution.py:398
  32.2 1.9 %collective-permute-start.15 = (f32[2,32,256]{2,1,0:T(8,128)S(1)}, f32[2,32,256]{2,1,0:T(8,128)S(1)}, u32[]{:S(2)}, u32[]{:S(2)}) collective-permute-start(f32[2,32,256]{2,1,0:T(8,128)S(1)} %get-tuple-element.59), channel_id=1, source_target_pairs={{0,16},{1,17},{2,18},{3,19},{4,20},{5,21},{6,22},{7,23},{8,24},{9,... | collective-permute-start | bytes 196616 | tf_op jit(solution)/shard_map/ppermute | solution.py:398
  34.1 1.2 %shard_map.128 = (f32[32,32,256]{2,1,0:T(8,128)S(1)}, f32[32,32,256]{2,1,0:T(8,128)S(1)}, f32[32,32,256]{2,1,0:T(8,128)S(1)}) custom-call(s32[1]{0:T(128)} %bitcast.spot, f32[2,32,256]{2,1,0:T(8,128)S(1)} %collective-permute-done.8.refs_0_, f32[32,2,256]{2,1,0:T(2,128)S(1)} %collective-permute-done.9.refs_1_, ...), custom_call_target="tpu_custom_call" | custom-call | flops 2000000000 | bytes 7340032 | tf_op jit(solution)/shard_map/pallas_call | solution.py:414
  35.2 0.0 copy-start.10
  35.3 0.5 collective-permute-done.12.refs_0_
  35.8 0.0 copy-start.2
  35.8 0.0 copy-start.3
  35.8 0.8 shard_map.129
  36.6 0.0 copy-start.7
  36.6 0.0 copy-start.9
  36.6 26.7 %all_to_all.10.chunks = f32[64,8,128]{2,1,0:T(8,128)S(1)} all-to-all(f32[64,8,128]{2,1,0:T(8,128)S(1)} %shard_map.129), channel_id=1, replica_groups={{0,1,2,3,4,5,6,7,8,9,10,11,12,13,14,15,64,65,66,67,68,69,70,71,72,73,74..., dimensions={0} | all-to-all | bytes 524288 | tf_op jit(solution)/shard_map/all_to_all | solution.py:442
  63.4 0.5 shard_map.130.refs_0_
  63.9 0.7 collective-permute-start.17
  64.6 5.1 %collective-permute-done.17.refs_2_ = f32[128,128]{1,0:T(8,128)S(1)} collective-permute-done((f32[128,128]{1,0:T(8,128)S(1)}, f32[128,128]{1,0:T(8,128)S(1)}, u32[]{:S(2)}, u32[]{:S(2)}) %collective-permute-start.17) | collective-permute-done | bytes 65568 | tf_op jit(solution)/shard_map/ppermute | solution.py:447
  69.7 1.2 %collective-permute-done.18.refs_3_ = f32[128,128]{1,0:T(8,128)S(1)} collective-permute-done((f32[128,128]{1,0:T(8,128)S(1)}, f32[128,128]{1,0:T(8,128)S(1)}, u32[]{:S(2)}, u32[]{:S(2)}) %collective-permute-start.18) | collective-permute-done | bytes 65568 | tf_op jit(solution)/shard_map/ppermute | solution.py:449
  71.0 1.4 %shard_map.131 = f32[64,8,128]{2,1,0:T(8,128)} custom-call(s32[1]{0:T(128)} %bitcast.spot, f32[128,128]{1,0:T(8,128)S(1)} %shard_map.130.refs_0_, f32[128,128]{1,0:T(8,128)S(1)} %collective-permute-done.16.refs_1_, f32[128,128]{1,0:T(8,128)S(1)} %collective-permute-done.17.refs_2_, f32[128,128]{1,0:T(8,128)S(1)} %collective-permute-done.18.refs_3_, ...), custom_call_target="tpu_custom_call" | custom-call | flops 1000000 | bytes 262144 | tf_op jit(solution)/shard_map/pallas_call | solution.py:450
  72.4 6.0 %all-to-all-start.1 = ((f32[64,8,128]{2,1,0:T(8,128)}), f32[64,8,128]{2,1,0:T(8,128)S(1)}, u32[]{:S(2)}, u32[]{:S(2)}) async-start(f32[64,8,128]{2,1,0:T(8,128)} %shard_map.131), calls=%async_computation.1 | async-start | bytes 524288 | tf_op jit(solution)/shard_map/all_to_all | solution.py:460
  78.4 0.0 copy-start.11
  78.4 1.2 %copy-done.11 = f32[32,32,256]{2,1,0:T(8,128)S(1)} copy-done((f32[32,32,256]{2,1,0:T(8,128)S(1)}, f32[32,32,256]{2,1,0:T(8,128)}, u32[]{:S(2)}) %copy-start.11) | copy-done | bytes 1048600
  79.7 1.2 %copy-done.13 = f32[32,32,256]{2,1,0:T(8,128)S(1)} copy-done((f32[32,32,256]{2,1,0:T(8,128)S(1)}, f32[32,32,256]{2,1,0:T(8,128)}, u32[]{:S(2)}) %copy-start.13) | copy-done | bytes 1048600
  80.9 2.0 %shard_map.133 = (f32[32,32,256]{2,1,0:T(8,128)}, f32[32,32,256]{2,1,0:T(8,128)}) custom-call(s32[1]{0:T(128)} %bitcast.spot, f32[2,32,256]{2,1,0:T(8,128)S(1)} %collective-permute-done.12.refs_0_, f32[32,2,256]{2,1,0:T(2,128)S(1)} %collective-permute-done.13.refs_1_, f32[32,2,256]{2,1,0:T(2,128)S(1)} %collective-permute-done.14.refs_2_, ...), custom_call_target="tpu_custom_call" | custom-call | flops 2000000000 | bytes 7340032 | tf_op jit(solution)/shard_map/pallas_call | solution.py:430
  82.9 7.9 %all-to-all-done.1.coef = f32[64,8,128]{2,1,0:T(8,128)S(1)} async-done(((f32[64,8,128]{2,1,0:T(8,128)}), f32[64,8,128]{2,1,0:T(8,128)S(1)}, u32[]{:S(2)}, u32[]{:S(2)}) %all-to-all-start.1) | async-done | bytes 262176 | tf_op jit(solution)/shard_map/all_to_all | solution.py:460
  90.8 1.7 %shard_map.132 = f32[32,32,256]{2,1,0:T(8,128)} custom-call(f32[64,8,128]{2,1,0:T(8,128)S(1)} %all-to-all-done.1.coef, f32[64,256]{1,0:T(8,128)S(1)} %copy-done.5), custom_call_target="tpu_custom_call" | custom-call | flops 1000000 | bytes 262144 | tf_op jit(solution)/shard_map/pallas_call | solution.py:461
  (34 shorter events, 0.1 us)
Async XLA Ops:
  1.9 7.3 %collective-permute-start = (f32[2,32,256]{2,1,0:T(8,128)S(1)}, f32[2,32,256]{2,1,0:T(8,128)S(1)}, u32[]{:S(2)}, u32[]{:S(2)}) collective-permute-start(f32[2,32,256]{2,1,0:T(8,128)S(1)} %get-tuple-element.35), channel_id=1, source_target_pairs={{0,1},{1,0},{2,3},{3,2},{4,5},{5,4},{6,7},{7,6},{8,9},{9,8},{10,11... | collective-permute-start | bytes 196616 | tf_op jit(solution)/shard_map/ppermute | solution.py:398
  2.0 7.2 %collective-permute-start.1 = (f32[32,2,256]{2,1,0:T(2,128)S(1)}, f32[32,2,256]{2,1,0:T(2,128)S(1)}, u32[]{:S(2)}, u32[]{:S(2)}) collective-permute-start(f32[32,2,256]{2,1,0:T(2,128)S(1)} %get-tuple-element.36), channel_id=1, source_target_pairs={{0,16},{1,2},{2,1},{3,4},{4,3},{5,6},{6,5},{7,8},{8,7},{9,10},{10,... | collective-permute-start | bytes 196616 | tf_op jit(solution)/shard_map/ppermute | solution.py:398
  3.4 5.9 %collective-permute-start.2 = (f32[32,2,256]{2,1,0:T(2,128)S(1)}, f32[32,2,256]{2,1,0:T(2,128)S(1)}, u32[]{:S(2)}, u32[]{:S(2)}) collective-permute-start(f32[32,2,256]{2,1,0:T(2,128)S(1)} %get-tuple-element.37), channel_id=1, source_target_pairs={{0,1},{1,0},{2,3},{3,2},{4,5},{5,4},{6,7},{7,6},{8,9},{9,8},{10,11... | collective-permute-start | bytes 196616 | tf_op jit(solution)/shard_map/ppermute | solution.py:398
  5.5 3.8 %collective-permute-start.3 = (f32[2,32,256]{2,1,0:T(8,128)S(1)}, f32[2,32,256]{2,1,0:T(8,128)S(1)}, u32[]{:S(2)}, u32[]{:S(2)}) collective-permute-start(f32[2,32,256]{2,1,0:T(8,128)S(1)} %get-tuple-element.38), channel_id=1, source_target_pairs={{0,16},{1,17},{2,18},{3,19},{4,20},{5,21},{6,22},{7,23},{8,24},{9,... | collective-permute-start | bytes 196616 | tf_op jit(solution)/shard_map/ppermute | solution.py:398
  6.2 0.7 copy-start.6
  6.9 0.7 copy-start.8
  7.6 1.7 %copy-start = (f32[32,32,256]{2,1,0:T(8,128)S(1)}, f32[32,32,256]{2,1,0:T(8,128)}, u32[]{:S(2)}) copy-start(f32[32,32,256]{2,1,0:T(8,128)} %refs_7_.7) | copy-start | bytes 3145732
  9.2 7.0 %copy-start.1 = (bf16[4,32,32,256]{3,2,1,0:T(8,128)(2,1)S(1)}, bf16[4,32,32,256]{3,2,1,0:T(8,128)(2,1)}, u32[]{:S(2)}) copy-start(bf16[4,32,32,256]{3,2,1,0:T(8,128)(2,1)} %refs_4_.8) | copy-start | bytes 6291460
  9.6 8.5 %collective-permute-start.4 = (f32[2,32,256]{2,1,0:T(8,128)S(1)}, f32[2,32,256]{2,1,0:T(8,128)S(1)}, u32[]{:S(2)}, u32[]{:S(2)}) collective-permute-start(f32[2,32,256]{2,1,0:T(8,128)S(1)} %get-tuple-element.42), channel_id=1, source_target_pairs={{0,1},{1,0},{2,3},{3,2},{4,5},{5,4},{6,7},{7,6},{8,9},{9,8},{10,11... | collective-permute-start | bytes 196616 | tf_op jit(solution)/shard_map/ppermute | solution.py:398
  11.6 6.5 %collective-permute-start.5 = (f32[32,2,256]{2,1,0:T(2,128)S(1)}, f32[32,2,256]{2,1,0:T(2,128)S(1)}, u32[]{:S(2)}, u32[]{:S(2)}) collective-permute-start(f32[32,2,256]{2,1,0:T(2,128)S(1)} %get-tuple-element.43), channel_id=1, source_target_pairs={{0,16},{1,2},{2,1},{3,4},{4,3},{5,6},{6,5},{7,8},{8,7},{9,10},{10,... | collective-permute-start | bytes 196616 | tf_op jit(solution)/shard_map/ppermute | solution.py:398
  13.0 5.4 %collective-permute-start.6 = (f32[32,2,256]{2,1,0:T(2,128)S(1)}, f32[32,2,256]{2,1,0:T(2,128)S(1)}, u32[]{:S(2)}, u32[]{:S(2)}) collective-permute-start(f32[32,2,256]{2,1,0:T(2,128)S(1)} %get-tuple-element.44), channel_id=1, source_target_pairs={{0,1},{1,0},{2,3},{3,2},{4,5},{5,4},{6,7},{7,6},{8,9},{9,8},{10,11... | collective-permute-start | bytes 196616 | tf_op jit(solution)/shard_map/ppermute | solution.py:398
  15.1 3.3 %collective-permute-start.7 = (f32[2,32,256]{2,1,0:T(8,128)S(1)}, f32[2,32,256]{2,1,0:T(8,128)S(1)}, u32[]{:S(2)}, u32[]{:S(2)}) collective-permute-start(f32[2,32,256]{2,1,0:T(8,128)S(1)} %get-tuple-element.45), channel_id=1, source_target_pairs={{0,16},{1,17},{2,18},{3,19},{4,20},{5,21},{6,22},{7,23},{8,24},{9,... | collective-permute-start | bytes 196616 | tf_op jit(solution)/shard_map/ppermute | solution.py:398
  18.7 5.6 %collective-permute-start.10 = (f32[32,2,256]{2,1,0:T(2,128)S(1)}, f32[32,2,256]{2,1,0:T(2,128)S(1)}, u32[]{:S(2)}, u32[]{:S(2)}) collective-permute-start(f32[32,2,256]{2,1,0:T(2,128)S(1)} %get-tuple-element.50), channel_id=1, source_target_pairs={{0,1},{1,0},{2,3},{3,2},{4,5},{5,4},{6,7},{7,6},{8,9},{9,8},{10,11... | collective-permute-start | bytes 196616 | tf_op jit(solution)/shard_map/ppermute | solution.py:398
  21.3 3.0 %collective-permute-start.11 = (f32[2,32,256]{2,1,0:T(8,128)S(1)}, f32[2,32,256]{2,1,0:T(8,128)S(1)}, u32[]{:S(2)}, u32[]{:S(2)}) collective-permute-start(f32[2,32,256]{2,1,0:T(8,128)S(1)} %get-tuple-element.51), channel_id=1, source_target_pairs={{0,16},{1,17},{2,18},{3,19},{4,20},{5,21},{6,22},{7,23},{8,24},{9,... | collective-permute-start | bytes 196616 | tf_op jit(solution)/shard_map/ppermute | solution.py:398
  21.3 7.3 %collective-permute-start.8 = (f32[2,32,256]{2,1,0:T(8,128)S(1)}, f32[2,32,256]{2,1,0:T(8,128)S(1)}, u32[]{:S(2)}, u32[]{:S(2)}) collective-permute-start(f32[2,32,256]{2,1,0:T(8,128)S(1)} %get-tuple-element.48), channel_id=1, source_target_pairs={{0,1},{1,0},{2,3},{3,2},{4,5},{5,4},{6,7},{7,6},{8,9},{9,8},{10,11... | collective-permute-start | bytes 196616 | tf_op jit(solution)/shard_map/ppermute | solution.py:398
  21.7 6.9 %collective-permute-start.9 = (f32[32,2,256]{2,1,0:T(2,128)S(1)}, f32[32,2,256]{2,1,0:T(2,128)S(1)}, u32[]{:S(2)}, u32[]{:S(2)}) collective-permute-start(f32[32,2,256]{2,1,0:T(2,128)S(1)} %get-tuple-element.49), channel_id=1, source_target_pairs={{0,16},{1,2},{2,1},{3,4},{4,3},{5,6},{6,5},{7,8},{8,7},{9,10},{10,... | collective-permute-start | bytes 196616 | tf_op jit(solution)/shard_map/ppermute | solution.py:398
  29.0 6.8 %collective-permute-start.12 = (f32[2,32,256]{2,1,0:T(8,128)S(1)}, f32[2,32,256]{2,1,0:T(8,128)S(1)}, u32[]{:S(2)}, u32[]{:S(2)}) collective-permute-start(f32[2,32,256]{2,1,0:T(8,128)S(1)} %get-tuple-element.56), channel_id=1, source_target_pairs={{0,1},{1,0},{2,3},{3,2},{4,5},{5,4},{6,7},{7,6},{8,9},{9,8},{10,11... | collective-permute-start | bytes 196616 | tf_op jit(solution)/shard_map/ppermute | solution.py:398
  29.1 6.7 %collective-permute-start.13 = (f32[32,2,256]{2,1,0:T(2,128)S(1)}, f32[32,2,256]{2,1,0:T(2,128)S(1)}, u32[]{:S(2)}, u32[]{:S(2)}) collective-permute-start(f32[32,2,256]{2,1,0:T(2,128)S(1)} %get-tuple-element.57), channel_id=1, source_target_pairs={{0,16},{1,2},{2,1},{3,4},{4,3},{5,6},{6,5},{7,8},{8,7},{9,10},{10,... | collective-permute-start | bytes 196616 | tf_op jit(solution)/shard_map/ppermute | solution.py:398
  29.2 6.6 %collective-permute-start.14 = (f32[32,2,256]{2,1,0:T(2,128)S(1)}, f32[32,2,256]{2,1,0:T(2,128)S(1)}, u32[]{:S(2)}, u32[]{:S(2)}) collective-permute-start(f32[32,2,256]{2,1,0:T(2,128)S(1)} %get-tuple-element.58), channel_id=1, source_target_pairs={{0,1},{1,0},{2,3},{3,2},{4,5},{5,4},{6,7},{7,6},{8,9},{9,8},{10,11... | collective-permute-start | bytes 196616 | tf_op jit(solution)/shard_map/ppermute | solution.py:398
  32.2 3.6 %collective-permute-start.15 = (f32[2,32,256]{2,1,0:T(8,128)S(1)}, f32[2,32,256]{2,1,0:T(8,128)S(1)}, u32[]{:S(2)}, u32[]{:S(2)}) collective-permute-start(f32[2,32,256]{2,1,0:T(8,128)S(1)} %get-tuple-element.59), channel_id=1, source_target_pairs={{0,16},{1,17},{2,18},{3,19},{4,20},{5,21},{6,22},{7,23},{8,24},{9,... | collective-permute-start | bytes 196616 | tf_op jit(solution)/shard_map/ppermute | solution.py:398
  34.1 1.7 %copy-start.4 = (f32[64,256]{1,0:T(8,128)S(1)}, f32[64,256]{1,0:T(8,128)}, u32[]{:S(2)}) copy-start(f32[64,256]{1,0:T(8,128)} %constant.18.clone.refs_6_) | copy-start | bytes 196612
  35.2 28.1 %copy-start.10 = (f32[32,32,256]{2,1,0:T(8,128)}, f32[32,32,256]{2,1,0:T(8,128)S(1)}, u32[]{:S(2)}) copy-start(f32[32,32,256]{2,1,0:T(8,128)S(1)} %get-tuple-element.63.refs_4_) | copy-start | bytes 3145732
  35.2 28.1 %copy-start.12 = (f32[32,32,256]{2,1,0:T(8,128)}, f32[32,32,256]{2,1,0:T(8,128)S(1)}, u32[]{:S(2)}) copy-start(f32[32,32,256]{2,1,0:T(8,128)S(1)} %get-tuple-element.64.refs_5_) | copy-start | bytes 3145732
  35.8 27.6 %copy-start.2 = (f32[128,512]{1,0:T(8,128)S(1)}, f32[128,512]{1,0:T(8,128)}, u32[]{:S(2)}) copy-start(f32[128,512]{1,0:T(8,128)} %constant.19.clone.table_y.refs_5_) | copy-start | bytes 786436
  35.8 35.2 %copy-start.3 = (f32[7,128,128]{2,1,0:T(8,128)S(1)}, f32[7,128,128]{2,1,0:T(8,128)}, u32[]{:S(2)}) copy-start(f32[7,128,128]{2,1,0:T(8,128)} %constant.20.clone.refs_4_) | copy-start | bytes 1376260
  36.6 41.8 %copy-start.7 = (f32[1,1,4,512]{3,2,1,0:T(4,128)S(1)}, f32[1,1,4,512]{3,2,1,0:T(4,128)}, u32[]{:S(2)}) copy-start(f32[1,1,4,512]{3,2,1,0:T(4,128)} %refs_9_.7) | copy-start | bytes 24580
  36.6 41.8 %copy-start.9 = (s32[1,1,512]{2,1,0:T(1,128)S(1)}, s32[1,1,512]{2,1,0:T(1,128)}, u32[]{:S(2)}) copy-start(s32[1,1,512]{2,1,0:T(1,128)} %refs_8_.7) | copy-start | bytes 6148
  63.9 5.9 %collective-permute-start.17 = (f32[128,128]{1,0:T(8,128)S(1)}, f32[128,128]{1,0:T(8,128)S(1)}, u32[]{:S(2)}, u32[]{:S(2)}) collective-permute-start(f32[128,128]{1,0:T(8,128)S(1)} %shard_map.130.refs_0_), channel_id=1, source_target_pairs={{0,32},{16,48},{32,0},{48,16},{64,96},{80,112},{96,64},{112,80},{1... | collective-permute-start | bytes 196616 | tf_op jit(solution)/shard_map/ppermute | solution.py:447
  64.6 5.1 %collective-permute-start.16 = (f32[128,128]{1,0:T(8,128)S(1)}, f32[128,128]{1,0:T(8,128)S(1)}, u32[]{:S(2)}, u32[]{:S(2)}) collective-permute-start(f32[128,128]{1,0:T(8,128)S(1)} %shard_map.130.refs_0_), channel_id=1, source_target_pairs={{0,16},{16,0},{32,48},{48,32},{64,80},{80,64},{96,112},{112,96},{1... | collective-permute-start | bytes 196616 | tf_op jit(solution)/shard_map/ppermute | solution.py:448
  69.7 1.3 %collective-permute-start.18 = (f32[128,128]{1,0:T(8,128)S(1)}, f32[128,128]{1,0:T(8,128)S(1)}, u32[]{:S(2)}, u32[]{:S(2)}) collective-permute-start(f32[128,128]{1,0:T(8,128)S(1)} %collective-permute-done.17.refs_2_), channel_id=1, source_target_pairs={{0,16},{16,0},{32,48},{48,32},{64,80},{80,64},{96,112},{112,96},{1... | collective-permute-start | bytes 196616 | tf_op jit(solution)/shard_map/ppermute | solution.py:449
  72.4 18.5 %all-to-all-start.1 = ((f32[64,8,128]{2,1,0:T(8,128)}), f32[64,8,128]{2,1,0:T(8,128)S(1)}, u32[]{:S(2)}, u32[]{:S(2)}) async-start(f32[64,8,128]{2,1,0:T(8,128)} %shard_map.131), calls=%async_computation.1 | async-start | bytes 524288 | tf_op jit(solution)/shard_map/all_to_all | solution.py:460
  78.4 1.2 %copy-start.11 = (f32[32,32,256]{2,1,0:T(8,128)S(1)}, f32[32,32,256]{2,1,0:T(8,128)}, u32[]{:S(2)}) copy-start(f32[32,32,256]{2,1,0:T(8,128)} %copy-done.10) | copy-start | bytes 3145732
  79.7 1.2 %copy-start.13 = (f32[32,32,256]{2,1,0:T(8,128)S(1)}, f32[32,32,256]{2,1,0:T(8,128)}, u32[]{:S(2)}) copy-start(f32[32,32,256]{2,1,0:T(8,128)} %copy-done.12) | copy-start | bytes 3145732
  80.9 9.9 %copy-start.5 = (f32[64,256]{1,0:T(8,128)S(1)}, f32[64,256]{1,0:T(8,128)}, u32[]{:S(2)}) copy-start(f32[64,256]{1,0:T(8,128)} %constant.17.clone.table_z) | copy-start | bytes 196612

commit v4 on v3

--- a/solution.py
+++ b/solution.py
@@ -281,7 +281,8 @@
             tiles = (scale[0:8] * first, scale[size_y - 8 : size_y] * last)
             value = with_change(gradient[x], x, {}, tiles)
             lines.append(value + scale * x_change[x] if x in x_change else value)
-        coef[:, s, :] = dot3(table, split(jnp.concatenate(lines, axis=0)), NT)
+        value = dot3(table, split(jnp.concatenate(lines, axis=0)), NT)
+        coef[pl.ds(s, value.shape[0], stride=8), :] = value
 
 
 def project_y(chunks, table_y, out, plane):
@@ -293,7 +294,7 @@
     out[...] = dot3(split(plane[...]), split(table_y[...]), NT)
 
 
-def smooth_plane(flags, own, one, two, three, table_x, table_y, chunks_hbm, plane, chunks, sems):
+def smooth_plane(flags, own, one, two, three, table_x, table_y, chunks, plane):
     high, low = split(jnp.concatenate([own[...], one[...], two[...], three[...]], axis=0))
     tables = [split(table_x[flags[6 + k]]) for k in range(GROUP)]
     left_high = jnp.concatenate([table[0] for table in tables], axis=1)
@@ -301,16 +302,10 @@
     total = dot3((left_high, left_low), (high, low), NN)
     plane[...] = dot3(split(total), split(table_y[...]), NN)
     count = chunks.shape[0] // GROUP
-    copies = []
     for r in range(GROUP):
         for c in range(count):
             pieces = [plane[pl.ds((r * 4 + q) * 8, 8), c * 32 : (c + 1) * 32] for q in range(4)]
             chunks[r * count + c] = jnp.concatenate(pieces, axis=1)
-        part = pl.ds(r * count, count)
-        copies.append(pltpu.make_async_copy(chunks.at[part], chunks_hbm.at[part], sems.at[r]))
-        copies[-1].start()
-    for copy in copies:
-        copy.wait()
 
 
 def expand_z(coef, table_z, out, lines, sems):
@@ -319,7 +314,7 @@
     table = jnp.concatenate([high, high, low], axis=0)
     copies = []
     for s in range(8):
-        high, low = split(coef[:, s, :])
+        high, low = split(coef[pl.ds(s, coef.shape[0] // 8, stride=8), :])
         value = dot(jnp.concatenate([high, low, high], axis=0), table, TN)
         lines[s] = value.reshape(4, size_y, size_z)
         copies.append(pltpu.make_async_copy(lines.at[s], out.at[pl.ds(4 * s, 4)], sems.at[s]))
@@ -367,6 +362,7 @@
     x_face = jax.ShapeDtypeStruct((2, size_y, size_z), jnp.float32)
     y_face = jax.ShapeDtypeStruct((size_x, 2, size_z), jnp.float32)
     chunks = jax.ShapeDtypeStruct((KZ, 8, 128), jnp.float32)
+    lines = jax.ShapeDtypeStruct((KZ * 8, 128), jnp.float32)
     swaps = [[], [], [], []]
     for r in range(rows):
         for c in range(cols):
@@ -424,7 +420,7 @@
             faces = call(
                 placed(faces_after), (x_face, y_face, y_face, x_face), [SMEM] + [VMEM] * 7, **light
             )(spot, *halo, courant_sq, base, lap)
-    coef = call(placed(project_z), chunks, [SMEM] + [VMEM] * 7, **light)(
+    coef = call(placed(project_z), lines, [SMEM] + [VMEM] * 7, **light)(
         spot, *halo, forward_fields, gradient, table_z_scaled
     )
     final_now, final_prev = call(
@@ -439,6 +435,7 @@
     groups = [
         [(m * GROUP + g) * cols + c for m in range(span) for c in range(cols)] for g in range(GROUP)
     ]
+    coef = coef.reshape(chunks.shape)
     coef = lax.all_to_all(coef, both, 0, 0, axis_index_groups=groups, tiled=True)
     plane = jax.ShapeDtypeStruct((own, KY), jnp.float32)
     wide = pltpu.VMEM((own, cols * size_y), jnp.float32)
@@ -446,13 +443,13 @@
     beside, across = ([(i, i ^ k) for i in range(rows)] for k in (1, 2))
     two = lax.ppermute(mine, "row", across)
     one = lax.ppermute(mine, "row", beside)
+    two, final_now, final_prev = lax.optimization_barrier((two, final_now, final_prev))
     others = (one, two, lax.ppermute(two, "row", beside))
     coef = call(
         placed(smooth_plane),
         chunks,
         [SMEM] + [VMEM] * 6,
-        out_specs=HBM,
-        scratch=[wide, pltpu.VMEM(chunks.shape, jnp.float32), DMA((GROUP,))],
+        scratch=[wide],
         **light,
     )(
         spot, mine, *others, table_x, table_y
@@ -465,7 +462,7 @@
         out_specs=HBM,
         scratch=[pltpu.VMEM((8, 4, size_y, size_z), jnp.float32), DMA((8,))],
         **light,
-    )(coef, table_z)
+    )(coef.reshape(lines.shape), table_z)
     return (smoothed, final_now, final_prev)
 
 

time: 93.1 us -> 91.5 us (0.983)
  blocking collectives: 26.7 us -> 45 us
  waiting for transfers between devices: 19.4 us -> 9.38 us
  starting transfers between devices: 26.5 us -> 20.6 us
  local copies, waits for them, and re-layouts: 3.88 us -> 1.41 us
  Pallas kernels: 15 us -> 13.9 us
    all_to_all x1 -> x2, blocking collectives: 26.7 us -> 45 us  [per_device(): lax.all_to_all(coef, both, 0, 0, axis_index_groups=groups, tiled=True)]
    all_to_all x1 -> x0, waiting for transfers between devices: 7.93 us -> none  [per_device(): lax.all_to_all(coef, both, 0, 0, axis_index_groups=groups, tiled=True)]
    all_to_all x1 -> x0, starting transfers between devices: 6.05 us -> none  [per_device(): lax.all_to_all(coef, both, 0, 0, axis_index_groups=groups, tiled=True)]
    unnamed x28 -> x16, local copies, waits for them, and re-layouts: 3.88 us -> 1.41 us
    ppermute x1, waiting for transfers between devices: 5.12 us -> 3.05 us  [per_device(): two = lax.ppermute(mine, 'row', across)]
  transfers between devices with their start and end apart: 20 -> 19, of which waited for: 6 -> 5; matrix products, arithmetic and copies ran while one was open for 0% -> 0% of each run, Pallas kernels for 9% -> 9%
where the time goes in v4:
time: 91.5 us; the launch traced here: 91.2 us
  blocking collectives  45 us (49%)
  starting transfers between devices  20.6 us (23%)
  Pallas kernels  13.9 us (15%)
  waiting for transfers between devices  9.38 us (10%)
  local copies, waits for them, and re-layouts  1.41 us (2%)
  between operations  1.02 us (1%)
    all_to_all x2, blocking collectives, per_device(): lax.all_to_all(coef, both, 0, 0, axis_index_groups=groups, tiled=True)  45 us
    ppermute x16, starting transfers between devices, per_device(): sent = [lax.ppermute(face, both, swaps[i]) for i, face in zip(ORDER, faces)]  19.7 us
    ppermute x16, waiting for transfers between devices, per_device(): sent = [lax.ppermute(face, both, swaps[i]) for i, face in zip(ORDER, faces)]  5.08 us
    pallas_call x3, Pallas kernels, per_device(): call(placed(functools.partial(later_step, step)), (field,) * (3 if last e...  4.86 us
    ppermute x1, waiting for transfers between devices, per_device(): two = lax.ppermute(mine, 'row', across)  3.05 us
    pallas_call x1, Pallas kernels, per_device(): call(placed(finish), (field, field), [SMEM] + [VMEM] * 10, out_specs=(HBM...  1.98 us
  transfers between devices with their start and end apart: 19, of which 5 were waited for; matrix products, arithmetic and copies ran while one was open for 0% of the time, Pallas kernels for 9%

profile of v4, /device:TPU:16, one launch (start us, length us, event | category | flops | bytes accessed | tf_op | source)
XLA Modules:
  0.0 91.2 jit_solution(4014443985446885)
XLA Ops:
  0.6 1.3 %shard_map.121 = (f32[32,32,256]{2,1,0:T(8,128)S(1)}, f32[2,32,256]{2,1,0:T(8,128)S(1)}, f32[32,2,256]{2,1,0:T(2,128)S(1)}, f32[32,2,256]{2,1,0:T(2,128)S(1)}, f32[2,32,256]{2,1,0:T(8,128)S(1)}) custom-call(s32[1]{0:T(128)} %bitcast.spot, f32[32,32,256]{2,1,0:T(8,128)} %refs_0_.1), custom_call_target="tpu_custom_call" | custom-call | flops 1000000 | bytes 262144 | tf_op jit(solution)/shard_map/pallas_call | solution.py:383
  1.9 0.1 collective-permute-start
  2.0 1.4 %collective-permute-start.1 = (f32[32,2,256]{2,1,0:T(2,128)S(1)}, f32[32,2,256]{2,1,0:T(2,128)S(1)}, u32[]{:S(2)}, u32[]{:S(2)}) collective-permute-start(f32[32,2,256]{2,1,0:T(2,128)S(1)} %get-tuple-element.39), channel_id=1, source_target_pairs={{0,16},{1,2},{2,1},{3,4},{4,3},{5,6},{6,5},{7,8},{8,7},{9,10},{10,... | collective-permute-start | bytes 196616 | tf_op jit(solution)/shard_map/ppermute | solution.py:394
  3.4 2.1 %collective-permute-start.2 = (f32[32,2,256]{2,1,0:T(2,128)S(1)}, f32[32,2,256]{2,1,0:T(2,128)S(1)}, u32[]{:S(2)}, u32[]{:S(2)}) collective-permute-start(f32[32,2,256]{2,1,0:T(2,128)S(1)} %get-tuple-element.40), channel_id=1, source_target_pairs={{0,1},{1,0},{2,3},{3,2},{4,5},{5,4},{6,7},{7,6},{8,9},{9,8},{10,11... | collective-permute-start | bytes 196616 | tf_op jit(solution)/shard_map/ppermute | solution.py:394
  5.5 0.7 collective-permute-start.3
  6.2 0.7 copy-done.6
  6.9 0.7 copy-done.7
  7.6 1.6 %shard_map.122 = (f32[32,32,256]{2,1,0:T(8,128)S(1)}, f32[32,32,256]{2,1,0:T(8,128)S(1)}) custom-call(f32[32,32,256]{2,1,0:T(8,128)S(1)} %get-tuple-element.42.now.refs_6_, f32[32,32,256]{2,1,0:T(8,128)} %prev_hbm.1, s32[1,1,512]{2,1,0:T(1,128)S(1)} %copy-done.7, f32[1,1,4,512]{3,2,1,0:T(4,128)S(1)} %copy-done.6), custom_call_target="tpu_custom_call" | custom-call | flops 2000000000 | bytes 7340032 | tf_op jit(solution)/shard_map/pallas_call | solution.py:396
  9.2 0.0 copy-start.1
  9.2 0.0 collective-permute-done.refs_0_
  9.2 0.0 collective-permute-done.1.refs_1_
  9.3 0.0 collective-permute-done.3.refs_3_
  9.3 0.3 shard_map.123
  9.6 2.0 %collective-permute-start.4 = (f32[2,32,256]{2,1,0:T(8,128)S(1)}, f32[2,32,256]{2,1,0:T(8,128)S(1)}, u32[]{:S(2)}, u32[]{:S(2)}) collective-permute-start(f32[2,32,256]{2,1,0:T(8,128)S(1)} %get-tuple-element.45), channel_id=1, source_target_pairs={{0,1},{1,0},{2,3},{3,2},{4,5},{5,4},{6,7},{7,6},{8,9},{9,8},{10,11... | collective-permute-start | bytes 196616 | tf_op jit(solution)/shard_map/ppermute | solution.py:394
  11.6 1.4 %collective-permute-start.5 = (f32[32,2,256]{2,1,0:T(2,128)S(1)}, f32[32,2,256]{2,1,0:T(2,128)S(1)}, u32[]{:S(2)}, u32[]{:S(2)}) collective-permute-start(f32[32,2,256]{2,1,0:T(2,128)S(1)} %get-tuple-element.46), channel_id=1, source_target_pairs={{0,16},{1,2},{2,1},{3,4},{4,3},{5,6},{6,5},{7,8},{8,7},{9,10},{10,... | collective-permute-start | bytes 196616 | tf_op jit(solution)/shard_map/ppermute | solution.py:394
  13.0 2.0 %collective-permute-start.6 = (f32[32,2,256]{2,1,0:T(2,128)S(1)}, f32[32,2,256]{2,1,0:T(2,128)S(1)}, u32[]{:S(2)}, u32[]{:S(2)}) collective-permute-start(f32[32,2,256]{2,1,0:T(2,128)S(1)} %get-tuple-element.47), channel_id=1, source_target_pairs={{0,1},{1,0},{2,3},{3,2},{4,5},{5,4},{6,7},{7,6},{8,9},{9,8},{10,11... | collective-permute-start | bytes 196616 | tf_op jit(solution)/shard_map/ppermute | solution.py:394
  15.1 1.2 %collective-permute-start.7 = (f32[2,32,256]{2,1,0:T(8,128)S(1)}, f32[2,32,256]{2,1,0:T(8,128)S(1)}, u32[]{:S(2)}, u32[]{:S(2)}) collective-permute-start(f32[2,32,256]{2,1,0:T(8,128)S(1)} %get-tuple-element.48), channel_id=1, source_target_pairs={{0,16},{1,17},{2,18},{3,19},{4,20},{5,21},{6,22},{7,23},{8,24},{9,... | collective-permute-start | bytes 196616 | tf_op jit(solution)/shard_map/ppermute | solution.py:394
  16.2 1.8 %shard_map.124 = (f32[32,32,256]{2,1,0:T(8,128)S(1)}, f32[32,32,256]{2,1,0:T(8,128)S(1)}, f32[32,32,256]{2,1,0:T(8,128)S(1)}, f32[32,32,256]{2,1,0:T(8,128)S(1)}) custom-call(s32[1]{0:T(128)} %bitcast.spot, f32[2,32,256]{2,1,0:T(8,128)S(1)} %collective-permute-done.refs_0_, f32[32,2,256]{2,1,0:T(2,128)S(1)} %collective-permute-done.1.refs_1_, ...), custom_call_target="tpu_custom_call" | custom-call | flops 2000000000 | bytes 7340032 | tf_op jit(solution)/shard_map/pallas_call | solution.py:410
  18.1 0.0 collective-permute-done.5.refs_1_
  18.1 0.3 collective-permute-done.6.refs_2_
  18.4 0.0 collective-permute-done.7.refs_3_
  18.4 0.3 shard_map.125
  18.7 2.6 %collective-permute-start.10 = (f32[32,2,256]{2,1,0:T(2,128)S(1)}, f32[32,2,256]{2,1,0:T(2,128)S(1)}, u32[]{:S(2)}, u32[]{:S(2)}) collective-permute-start(f32[32,2,256]{2,1,0:T(2,128)S(1)} %get-tuple-element.53), channel_id=1, source_target_pairs={{0,1},{1,0},{2,3},{3,2},{4,5},{5,4},{6,7},{7,6},{8,9},{9,8},{10,11... | collective-permute-start | bytes 196616 | tf_op jit(solution)/shard_map/ppermute | solution.py:394
  21.3 0.4 collective-permute-start.8
  21.7 0.8 collective-permute-start.9
  22.5 1.8 %shard_map.126 = (f32[32,32,256]{2,1,0:T(8,128)S(1)}, f32[32,32,256]{2,1,0:T(8,128)S(1)}, f32[32,32,256]{2,1,0:T(8,128)S(1)}, f32[32,32,256]{2,1,0:T(8,128)S(1)}) custom-call(s32[1]{0:T(128)} %bitcast.spot, f32[2,32,256]{2,1,0:T(8,128)S(1)} %collective-permute-done.4.refs_0_, f32[32,2,256]{2,1,0:T(2,128)S(1)} %collective-permute-done.5.refs_1_, ...), custom_call_target="tpu_custom_call" | custom-call | flops 2000000000 | bytes 7340032 | tf_op jit(solution)/shard_map/pallas_call | solution.py:410
  24.3 0.0 collective-permute-done.10.refs_2_
  24.4 4.3 %collective-permute-done.8.refs_0_ = f32[2,32,256]{2,1,0:T(8,128)S(1)} collective-permute-done((f32[2,32,256]{2,1,0:T(8,128)S(1)}, f32[2,32,256]{2,1,0:T(8,128)S(1)}, u32[]{:S(2)}, u32[]{:S(2)}) %collective-permute-start.8) | collective-permute-done | bytes 65568 | tf_op jit(solution)/shard_map/ppermute | solution.py:394
  28.6 0.3 shard_map.127
  29.0 0.1 collective-permute-start.12
  29.1 0.1 collective-permute-start.13
  29.2 3.0 %collective-permute-start.14 = (f32[32,2,256]{2,1,0:T(2,128)S(1)}, f32[32,2,256]{2,1,0:T(2,128)S(1)}, u32[]{:S(2)}, u32[]{:S(2)}) collective-permute-start(f32[32,2,256]{2,1,0:T(2,128)S(1)} %get-tuple-element.61), channel_id=1, source_target_pairs={{0,1},{1,0},{2,3},{3,2},{4,5},{5,4},{6,7},{7,6},{8,9},{9,8},{10,11... | collective-permute-start | bytes 196616 | tf_op jit(solution)/shard_map/ppermute | solution.py:394
  32.2 1.9 %collective-permute-start.15 = (f32[2,32,256]{2,1,0:T(8,128)S(1)}, f32[2,32,256]{2,1,0:T(8,128)S(1)}, u32[]{:S(2)}, u32[]{:S(2)}) collective-permute-start(f32[2,32,256]{2,1,0:T(8,128)S(1)} %get-tuple-element.62), channel_id=1, source_target_pairs={{0,16},{1,17},{2,18},{3,19},{4,20},{5,21},{6,22},{7,23},{8,24},{9,... | collective-permute-start | bytes 196616 | tf_op jit(solution)/shard_map/ppermute | solution.py:394
  34.1 1.2 %shard_map.128 = (f32[32,32,256]{2,1,0:T(8,128)S(1)}, f32[32,32,256]{2,1,0:T(8,128)S(1)}, f32[32,32,256]{2,1,0:T(8,128)S(1)}) custom-call(s32[1]{0:T(128)} %bitcast.spot, f32[2,32,256]{2,1,0:T(8,128)S(1)} %collective-permute-done.8.refs_0_, f32[32,2,256]{2,1,0:T(2,128)S(1)} %collective-permute-done.9.refs_1_, ...), custom_call_target="tpu_custom_call" | custom-call | flops 2000000000 | bytes 7340032 | tf_op jit(solution)/shard_map/pallas_call | solution.py:410
  35.3 0.5 collective-permute-done.12.refs_0_
  35.8 0.0 collective-permute-done.15.refs_3_
  35.8 0.0 copy-start.2
  35.8 0.7 shard_map.129
  36.5 26.7 %all_to_all.10.chunks = f32[64,8,128]{2,1,0:T(8,128)S(1)} all-to-all(f32[64,8,128]{2,1,0:T(8,128)S(1)} %bitcast.3), channel_id=1, replica_groups={{0,1,2,3,4,5,6,7,8,9,10,11,12,13,14,15,64,65,66,67,68,69,70,71,72,73,74..., dimensions={0} | all-to-all | bytes 524288 | tf_op jit(solution)/shard_map/all_to_all | solution.py:439
  63.3 0.5 shard_map.130.refs_0_
  63.8 0.7 collective-permute-start.17
  64.5 2.0 %shard_map.131 = (f32[32,32,256]{2,1,0:T(8,128)}, f32[32,32,256]{2,1,0:T(8,128)}) custom-call(s32[1]{0:T(128)} %bitcast.spot, f32[2,32,256]{2,1,0:T(8,128)S(1)} %collective-permute-done.12.refs_0_, f32[32,2,256]{2,1,0:T(2,128)S(1)} %collective-permute-done.13.refs_1_, f32[32,2,256]{2,1,0:T(2,128)S(1)} %collective-permute-done.14.refs_2_, ...), custom_call_target="tpu_custom_call" | custom-call | flops 2000000000 | bytes 7340032 | tf_op jit(solution)/shard_map/pallas_call | solution.py:426
  66.5 0.1 collective-permute-start.16
  66.6 3.0 %collective-permute-done.17.refs_2_ = f32[128,128]{1,0:T(8,128)S(1)} collective-permute-done((f32[128,128]{1,0:T(8,128)S(1)}, f32[128,128]{1,0:T(8,128)S(1)}, u32[]{:S(2)}, u32[]{:S(2)}) %collective-permute-start.17) | collective-permute-done | bytes 65568 | tf_op jit(solution)/shard_map/ppermute | solution.py:444
  69.6 1.2 %collective-permute-done.18.refs_3_ = f32[128,128]{1,0:T(8,128)S(1)} collective-permute-done((f32[128,128]{1,0:T(8,128)S(1)}, f32[128,128]{1,0:T(8,128)S(1)}, u32[]{:S(2)}, u32[]{:S(2)}) %collective-permute-start.18) | collective-permute-done | bytes 65568 | tf_op jit(solution)/shard_map/ppermute | solution.py:447
  70.9 0.7 shard_map.132
  71.6 18.2 %all_to_all.11 = f32[64,8,128]{2,1,0:T(8,128)S(1)} all-to-all(f32[64,8,128]{2,1,0:T(8,128)S(1)} %shard_map.132), channel_id=1, replica_groups={{0,1,2,3,4,5,6,7,8,9,10,11,12,13,14,15,64,65,66,67,68,69,70,71,72,73,74..., dimensions={0} | all-to-all | bytes 524288 | tf_op jit(solution)/shard_map/all_to_all | solution.py:457
  89.8 1.2 %shard_map.133 = f32[32,32,256]{2,1,0:T(8,128)} custom-call(f32[512,128]{1,0:T(8,128)S(1)} %bitcast.4, f32[64,256]{1,0:T(8,128)S(1)} %copy-done.5), custom_call_target="tpu_custom_call" | custom-call | flops 1000000 | bytes 262144 | tf_op jit(solution)/shard_map/pallas_call | solution.py:458
  (21 shorter events, 0.0 us)
Async XLA Ops:
  1.9 7.3 %collective-permute-start = (f32[2,32,256]{2,1,0:T(8,128)S(1)}, f32[2,32,256]{2,1,0:T(8,128)S(1)}, u32[]{:S(2)}, u32[]{:S(2)}) collective-permute-start(f32[2,32,256]{2,1,0:T(8,128)S(1)} %get-tuple-element.38), channel_id=1, source_target_pairs={{0,1},{1,0},{2,3},{3,2},{4,5},{5,4},{6,7},{7,6},{8,9},{9,8},{10,11... | collective-permute-start | bytes 196616 | tf_op jit(solution)/shard_map/ppermute | solution.py:394
  2.0 7.2 %collective-permute-start.1 = (f32[32,2,256]{2,1,0:T(2,128)S(1)}, f32[32,2,256]{2,1,0:T(2,128)S(1)}, u32[]{:S(2)}, u32[]{:S(2)}) collective-permute-start(f32[32,2,256]{2,1,0:T(2,128)S(1)} %get-tuple-element.39), channel_id=1, source_target_pairs={{0,16},{1,2},{2,1},{3,4},{4,3},{5,6},{6,5},{7,8},{8,7},{9,10},{10,... | collective-permute-start | bytes 196616 | tf_op jit(solution)/shard_map/ppermute | solution.py:394
  3.4 5.9 %collective-permute-start.2 = (f32[32,2,256]{2,1,0:T(2,128)S(1)}, f32[32,2,256]{2,1,0:T(2,128)S(1)}, u32[]{:S(2)}, u32[]{:S(2)}) collective-permute-start(f32[32,2,256]{2,1,0:T(2,128)S(1)} %get-tuple-element.40), channel_id=1, source_target_pairs={{0,1},{1,0},{2,3},{3,2},{4,5},{5,4},{6,7},{7,6},{8,9},{9,8},{10,11... | collective-permute-start | bytes 196616 | tf_op jit(solution)/shard_map/ppermute | solution.py:394
  5.5 3.8 %collective-permute-start.3 = (f32[2,32,256]{2,1,0:T(8,128)S(1)}, f32[2,32,256]{2,1,0:T(8,128)S(1)}, u32[]{:S(2)}, u32[]{:S(2)}) collective-permute-start(f32[2,32,256]{2,1,0:T(8,128)S(1)} %get-tuple-element.41), channel_id=1, source_target_pairs={{0,16},{1,17},{2,18},{3,19},{4,20},{5,21},{6,22},{7,23},{8,24},{9,... | collective-permute-start | bytes 196616 | tf_op jit(solution)/shard_map/ppermute | solution.py:394
  6.2 0.7 copy-start.6
  6.9 0.7 copy-start.7
  7.6 1.7 %copy-start = (f32[32,32,256]{2,1,0:T(8,128)S(1)}, f32[32,32,256]{2,1,0:T(8,128)}, u32[]{:S(2)}) copy-start(f32[32,32,256]{2,1,0:T(8,128)} %refs_7_.7) | copy-start | bytes 3145732
  9.2 7.0 %copy-start.1 = (bf16[4,32,32,256]{3,2,1,0:T(8,128)(2,1)S(1)}, bf16[4,32,32,256]{3,2,1,0:T(8,128)(2,1)}, u32[]{:S(2)}) copy-start(bf16[4,32,32,256]{3,2,1,0:T(8,128)(2,1)} %refs_4_.8) | copy-start | bytes 6291460
  9.6 8.5 %collective-permute-start.4 = (f32[2,32,256]{2,1,0:T(8,128)S(1)}, f32[2,32,256]{2,1,0:T(8,128)S(1)}, u32[]{:S(2)}, u32[]{:S(2)}) collective-permute-start(f32[2,32,256]{2,1,0:T(8,128)S(1)} %get-tuple-element.45), channel_id=1, source_target_pairs={{0,1},{1,0},{2,3},{3,2},{4,5},{5,4},{6,7},{7,6},{8,9},{9,8},{10,11... | collective-permute-start | bytes 196616 | tf_op jit(solution)/shard_map/ppermute | solution.py:394
  11.6 6.5 %collective-permute-start.5 = (f32[32,2,256]{2,1,0:T(2,128)S(1)}, f32[32,2,256]{2,1,0:T(2,128)S(1)}, u32[]{:S(2)}, u32[]{:S(2)}) collective-permute-start(f32[32,2,256]{2,1,0:T(2,128)S(1)} %get-tuple-element.46), channel_id=1, source_target_pairs={{0,16},{1,2},{2,1},{3,4},{4,3},{5,6},{6,5},{7,8},{8,7},{9,10},{10,... | collective-permute-start | bytes 196616 | tf_op jit(solution)/shard_map/ppermute | solution.py:394
  13.0 5.4 %collective-permute-start.6 = (f32[32,2,256]{2,1,0:T(2,128)S(1)}, f32[32,2,256]{2,1,0:T(2,128)S(1)}, u32[]{:S(2)}, u32[]{:S(2)}) collective-permute-start(f32[32,2,256]{2,1,0:T(2,128)S(1)} %get-tuple-element.47), channel_id=1, source_target_pairs={{0,1},{1,0},{2,3},{3,2},{4,5},{5,4},{6,7},{7,6},{8,9},{9,8},{10,11... | collective-permute-start | bytes 196616 | tf_op jit(solution)/shard_map/ppermute | solution.py:394
  15.1 3.3 %collective-permute-start.7 = (f32[2,32,256]{2,1,0:T(8,128)S(1)}, f32[2,32,256]{2,1,0:T(8,128)S(1)}, u32[]{:S(2)}, u32[]{:S(2)}) collective-permute-start(f32[2,32,256]{2,1,0:T(8,128)S(1)} %get-tuple-element.48), channel_id=1, source_target_pairs={{0,16},{1,17},{2,18},{3,19},{4,20},{5,21},{6,22},{7,23},{8,24},{9,... | collective-permute-start | bytes 196616 | tf_op jit(solution)/shard_map/ppermute | solution.py:394
  18.7 5.6 %collective-permute-start.10 = (f32[32,2,256]{2,1,0:T(2,128)S(1)}, f32[32,2,256]{2,1,0:T(2,128)S(1)}, u32[]{:S(2)}, u32[]{:S(2)}) collective-permute-start(f32[32,2,256]{2,1,0:T(2,128)S(1)} %get-tuple-element.53), channel_id=1, source_target_pairs={{0,1},{1,0},{2,3},{3,2},{4,5},{5,4},{6,7},{7,6},{8,9},{9,8},{10,11... | collective-permute-start | bytes 196616 | tf_op jit(solution)/shard_map/ppermute | solution.py:394
  21.3 3.0 %collective-permute-start.11 = (f32[2,32,256]{2,1,0:T(8,128)S(1)}, f32[2,32,256]{2,1,0:T(8,128)S(1)}, u32[]{:S(2)}, u32[]{:S(2)}) collective-permute-start(f32[2,32,256]{2,1,0:T(8,128)S(1)} %get-tuple-element.54), channel_id=1, source_target_pairs={{0,16},{1,17},{2,18},{3,19},{4,20},{5,21},{6,22},{7,23},{8,24},{9,... | collective-permute-start | bytes 196616 | tf_op jit(solution)/shard_map/ppermute | solution.py:394
  21.3 7.3 %collective-permute-start.8 = (f32[2,32,256]{2,1,0:T(8,128)S(1)}, f32[2,32,256]{2,1,0:T(8,128)S(1)}, u32[]{:S(2)}, u32[]{:S(2)}) collective-permute-start(f32[2,32,256]{2,1,0:T(8,128)S(1)} %get-tuple-element.51), channel_id=1, source_target_pairs={{0,1},{1,0},{2,3},{3,2},{4,5},{5,4},{6,7},{7,6},{8,9},{9,8},{10,11... | collective-permute-start | bytes 196616 | tf_op jit(solution)/shard_map/ppermute | solution.py:394
  21.7 6.9 %collective-permute-start.9 = (f32[32,2,256]{2,1,0:T(2,128)S(1)}, f32[32,2,256]{2,1,0:T(2,128)S(1)}, u32[]{:S(2)}, u32[]{:S(2)}) collective-permute-start(f32[32,2,256]{2,1,0:T(2,128)S(1)} %get-tuple-element.52), channel_id=1, source_target_pairs={{0,16},{1,2},{2,1},{3,4},{4,3},{5,6},{6,5},{7,8},{8,7},{9,10},{10,... | collective-permute-start | bytes 196616 | tf_op jit(solution)/shard_map/ppermute | solution.py:394
  29.0 6.8 %collective-permute-start.12 = (f32[2,32,256]{2,1,0:T(8,128)S(1)}, f32[2,32,256]{2,1,0:T(8,128)S(1)}, u32[]{:S(2)}, u32[]{:S(2)}) collective-permute-start(f32[2,32,256]{2,1,0:T(8,128)S(1)} %get-tuple-element.59), channel_id=1, source_target_pairs={{0,1},{1,0},{2,3},{3,2},{4,5},{5,4},{6,7},{7,6},{8,9},{9,8},{10,11... | collective-permute-start | bytes 196616 | tf_op jit(solution)/shard_map/ppermute | solution.py:394
  29.1 6.7 %collective-permute-start.13 = (f32[32,2,256]{2,1,0:T(2,128)S(1)}, f32[32,2,256]{2,1,0:T(2,128)S(1)}, u32[]{:S(2)}, u32[]{:S(2)}) collective-permute-start(f32[32,2,256]{2,1,0:T(2,128)S(1)} %get-tuple-element.60), channel_id=1, source_target_pairs={{0,16},{1,2},{2,1},{3,4},{4,3},{5,6},{6,5},{7,8},{8,7},{9,10},{10,... | collective-permute-start | bytes 196616 | tf_op jit(solution)/shard_map/ppermute | solution.py:394
  29.2 6.6 %collective-permute-start.14 = (f32[32,2,256]{2,1,0:T(2,128)S(1)}, f32[32,2,256]{2,1,0:T(2,128)S(1)}, u32[]{:S(2)}, u32[]{:S(2)}) collective-permute-start(f32[32,2,256]{2,1,0:T(2,128)S(1)} %get-tuple-element.61), channel_id=1, source_target_pairs={{0,1},{1,0},{2,3},{3,2},{4,5},{5,4},{6,7},{7,6},{8,9},{9,8},{10,11... | collective-permute-start | bytes 196616 | tf_op jit(solution)/shard_map/ppermute | solution.py:394
  32.2 3.6 %collective-permute-start.15 = (f32[2,32,256]{2,1,0:T(8,128)S(1)}, f32[2,32,256]{2,1,0:T(8,128)S(1)}, u32[]{:S(2)}, u32[]{:S(2)}) collective-permute-start(f32[2,32,256]{2,1,0:T(8,128)S(1)} %get-tuple-element.62), channel_id=1, source_target_pairs={{0,16},{1,17},{2,18},{3,19},{4,20},{5,21},{6,22},{7,23},{8,24},{9,... | collective-permute-start | bytes 196616 | tf_op jit(solution)/shard_map/ppermute | solution.py:394
  34.1 1.7 %copy-start.4 = (f32[64,256]{1,0:T(8,128)S(1)}, f32[64,256]{1,0:T(8,128)}, u32[]{:S(2)}) copy-start(f32[64,256]{1,0:T(8,128)} %constant.18.clone.refs_6_) | copy-start | bytes 196612
  35.8 27.5 %copy-start.2 = (f32[128,512]{1,0:T(8,128)S(1)}, f32[128,512]{1,0:T(8,128)}, u32[]{:S(2)}) copy-start(f32[128,512]{1,0:T(8,128)} %constant.19.clone.table_y.refs_5_) | copy-start | bytes 786436
  63.8 5.9 %collective-permute-start.17 = (f32[128,128]{1,0:T(8,128)S(1)}, f32[128,128]{1,0:T(8,128)S(1)}, u32[]{:S(2)}, u32[]{:S(2)}) collective-permute-start(f32[128,128]{1,0:T(8,128)S(1)} %shard_map.130.refs_0_), channel_id=1, source_target_pairs={{0,32},{16,48},{32,0},{48,16},{64,96},{80,112},{96,64},{112,80},{1... | collective-permute-start | bytes 196616 | tf_op jit(solution)/shard_map/ppermute | solution.py:444
  64.5 6.4 %copy-start.3 = (f32[7,128,128]{2,1,0:T(8,128)S(1)}, f32[7,128,128]{2,1,0:T(8,128)}, u32[]{:S(2)}) copy-start(f32[7,128,128]{2,1,0:T(8,128)} %constant.20.clone.refs_4_) | copy-start | bytes 1376260
  64.5 25.3 %copy-start.5 = (f32[64,256]{1,0:T(8,128)S(1)}, f32[64,256]{1,0:T(8,128)}, u32[]{:S(2)}) copy-start(f32[64,256]{1,0:T(8,128)} %constant.17.clone.table_z) | copy-start | bytes 196612
  66.5 3.2 %collective-permute-start.16 = (f32[128,128]{1,0:T(8,128)S(1)}, f32[128,128]{1,0:T(8,128)S(1)}, u32[]{:S(2)}, u32[]{:S(2)}) collective-permute-start(f32[128,128]{1,0:T(8,128)S(1)} %shard_map.130.refs_0_), channel_id=1, source_target_pairs={{0,16},{16,0},{32,48},{48,32},{64,80},{80,64},{96,112},{112,96},{1... | collective-permute-start | bytes 196616 | tf_op jit(solution)/shard_map/ppermute | solution.py:445
  69.6 1.3 %collective-permute-start.18 = (f32[128,128]{1,0:T(8,128)S(1)}, f32[128,128]{1,0:T(8,128)S(1)}, u32[]{:S(2)}, u32[]{:S(2)}) collective-permute-start(f32[128,128]{1,0:T(8,128)S(1)} %collective-permute-done.17.refs_2_), channel_id=1, source_target_pairs={{0,16},{16,0},{32,48},{48,32},{64,80},{80,64},{96,112},{112,96},{1... | collective-permute-start | bytes 196616 | tf_op jit(solution)/shard_map/ppermute | solution.py:447

commit v5 on v4

--- a/solution.py
+++ b/solution.py
@@ -17,7 +17,7 @@
 TWELFTH = 1.0 / 12.0
 PACK_ROOM = 52
 FIRST_ROOM = 50
-ORDER = (1, 3, 2, 0)
+ORDER = (3, 1, 2, 0)
 
 HBM = pl.BlockSpec(memory_space=pltpu.HBM)
 VMEM = pl.BlockSpec(memory_space=pltpu.VMEM)
@@ -80,7 +80,7 @@
     kernel(flags, *refs)
 
 
-def pack(flags, now_hbm, now, x_odd, y_odd, y_even, x_even, sems):
+def pack(flags, now_hbm, now, y_odd, x_odd, y_even, x_even, sems):
     size_x, size_y, _ = now.shape
     step = size_x // 4
     copies = []
@@ -135,7 +135,7 @@
     return value + x_change[x] if x in x_change else value
 
 
-def faces_after(flags, x_odd, y_odd, y_even, x_even, courant, base, lap, out_x_odd, out_y_odd, out_y_even, out_x_even):
+def faces_after(flags, y_odd, x_odd, y_even, x_even, courant, base, lap, out_y_odd, out_x_odd, out_y_even, out_x_even):
     size_x, size_y, _ = base.shape
     x_change = x_changes(flags, x_even, x_odd, size_x)
     layers = {}
@@ -220,7 +220,7 @@
 
 
 def later_step(step, flags, *refs):
-    x_odd, y_odd, y_even, x_even, base_in, lap_in, prev, courant, forward, cells, traces, *refs = refs
+    y_odd, x_odd, y_even, x_even, base_in, lap_in, prev, courant, forward, cells, traces, *refs = refs
     gradient_in = refs.pop(0) if step > 1 else None
     last = step == STEPS - 1
     now, lap, gradient = refs[:3]
@@ -246,7 +246,7 @@
                 base[x] = (2.0 * now[x] - prev[x]) + inject[i]
 
 
-def finish(flags, x_odd, y_odd, y_even, x_even, now, lap, prev, courant, cells, traces, next_hbm, now_hbm, nxt, sems):
+def finish(flags, y_odd, x_odd, y_even, x_even, now, lap, prev, courant, cells, traces, next_hbm, now_hbm, nxt, sems):
     size_x, size_y, size_z = now.shape
     layers = ROWS // size_y
     keep = pltpu.make_async_copy(now, now_hbm, sems.at[0])
@@ -269,7 +269,7 @@
     keep.wait()
 
 
-def project_z(flags, x_odd, y_odd, y_even, x_even, forward, gradient, table_z, coef):
+def project_z(flags, y_odd, x_odd, y_even, x_even, forward, gradient, table_z, coef):
     size_x, size_y, _ = gradient.shape
     table = split(table_z[...])
     x_change = x_changes(flags, x_even, x_odd, size_x)
@@ -382,7 +382,7 @@
 
     now, *faces = call(
         placed(pack),
-        (field, x_face, y_face, y_face, x_face),
+        (field, y_face, x_face, y_face, x_face),
         [SMEM, HBM],
         scratch=[DMA((4,))],
         room=PACK_ROOM,
@@ -418,7 +418,7 @@
         halo = sent
         if step < STEPS - 1:
             faces = call(
-                placed(faces_after), (x_face, y_face, y_face, x_face), [SMEM] + [VMEM] * 7, **light
+                placed(faces_after), (y_face, x_face, y_face, x_face), [SMEM] + [VMEM] * 7, **light
             )(spot, *halo, courant_sq, base, lap)
     coef = call(placed(project_z), lines, [SMEM] + [VMEM] * 7, **light)(
         spot, *halo, forward_fields, gradient, table_z_scaled

time: 91.5 us -> 90.9 us (level)
  blocking collectives: 45 us -> 43.4 us
  waiting for transfers between devices: 9.38 us -> 10.7 us
    ppermute x16, waiting for transfers between devices: 5.08 us -> 7.02 us  [per_device(): sent = [lax.ppermute(face, both, swaps[i]) for i, face in zip(ORDER, faces)]]
    all_to_all x2, blocking collectives: 45 us -> 43.4 us  [per_device(): lax.all_to_all(coef, both, 0, 0, axis_index_groups=groups, tiled=True)]
    ppermute x16, starting transfers between devices: 19.7 us -> 18.6 us  [per_device(): sent = [lax.ppermute(face, both, swaps[i]) for i, face in zip(ORDER, faces)]]
  transfers between devices with their start and end apart: 19 -> 19, of which waited for: 5 -> 7; matrix products, arithmetic and copies ran while one was open for 0% -> 0% of each run, Pallas kernels for 9% -> 9%
where the time goes in v5:
time: 90.9 us; the launch traced here: 90.5 us
  blocking collectives  43.4 us (48%)
  starting transfers between devices  20.1 us (22%)
  Pallas kernels  13.9 us (15%)
  waiting for transfers between devices  10.7 us (12%)
  local copies, waits for them, and re-layouts  1.4 us (2%)
  between operations  1 us (1%)
    all_to_all x2, blocking collectives, per_device(): lax.all_to_all(coef, both, 0, 0, axis_index_groups=groups, tiled=True)  43.4 us
    ppermute x16, starting transfers between devices, per_device(): sent = [lax.ppermute(face, both, swaps[i]) for i, face in zip(ORDER, faces)]  18.6 us
    ppermute x16, waiting for transfers between devices, per_device(): sent = [lax.ppermute(face, both, swaps[i]) for i, face in zip(ORDER, faces)]  7.02 us
    pallas_call x3, Pallas kernels, per_device(): call(placed(functools.partial(later_step, step)), (field,) * (3 if last e...  4.86 us
    ppermute x1, waiting for transfers between devices, per_device(): two = lax.ppermute(mine, 'row', across)  2.42 us
    pallas_call x1, Pallas kernels, per_device(): call(placed(finish), (field, field), [SMEM] + [VMEM] * 10, out_specs=(HBM...  1.98 us
  transfers between devices with their start and end apart: 19, of which 7 were waited for; matrix products, arithmetic and copies ran while one was open for 0% of the time, Pallas kernels for 9%

profile of v5, /device:TPU:16, one launch (start us, length us, event | category | flops | bytes accessed | tf_op | source)
XLA Modules:
  0.0 90.5 jit_solution(11401316199452517162)
XLA Ops:
  0.6 1.3 %shard_map.121 = (f32[32,32,256]{2,1,0:T(8,128)S(1)}, f32[32,2,256]{2,1,0:T(2,128)S(1)}, f32[2,32,256]{2,1,0:T(8,128)S(1)}, f32[32,2,256]{2,1,0:T(2,128)S(1)}, f32[2,32,256]{2,1,0:T(8,128)S(1)}) custom-call(s32[1]{0:T(128)} %bitcast.spot, f32[32,32,256]{2,1,0:T(8,128)} %refs_0_.1), custom_call_target="tpu_custom_call" | custom-call | flops 1000000 | bytes 262144 | tf_op jit(solution)/shard_map/pallas_call | solution.py:383
  1.9 0.1 collective-permute-start
  2.0 2.2 %collective-permute-start.1 = (f32[2,32,256]{2,1,0:T(8,128)S(1)}, f32[2,32,256]{2,1,0:T(8,128)S(1)}, u32[]{:S(2)}, u32[]{:S(2)}) collective-permute-start(f32[2,32,256]{2,1,0:T(8,128)S(1)} %get-tuple-element.39), channel_id=1, source_target_pairs={{0,1},{1,0},{2,3},{3,2},{4,5},{5,4},{6,7},{7,6},{8,9},{9,8},{10,11... | collective-permute-start | bytes 196616 | tf_op jit(solution)/shard_map/ppermute | solution.py:394
  4.2 1.3 %collective-permute-start.2 = (f32[32,2,256]{2,1,0:T(2,128)S(1)}, f32[32,2,256]{2,1,0:T(2,128)S(1)}, u32[]{:S(2)}, u32[]{:S(2)}) collective-permute-start(f32[32,2,256]{2,1,0:T(2,128)S(1)} %get-tuple-element.40), channel_id=1, source_target_pairs={{0,1},{1,0},{2,3},{3,2},{4,5},{5,4},{6,7},{7,6},{8,9},{9,8},{10,11... | collective-permute-start | bytes 196616 | tf_op jit(solution)/shard_map/ppermute | solution.py:394
  5.5 1.6 %collective-permute-start.3 = (f32[2,32,256]{2,1,0:T(8,128)S(1)}, f32[2,32,256]{2,1,0:T(8,128)S(1)}, u32[]{:S(2)}, u32[]{:S(2)}) collective-permute-start(f32[2,32,256]{2,1,0:T(8,128)S(1)} %get-tuple-element.41), channel_id=1, source_target_pairs={{0,16},{1,17},{2,18},{3,19},{4,20},{5,21},{6,22},{7,23},{8,24},{9,... | collective-permute-start | bytes 196616 | tf_op jit(solution)/shard_map/ppermute | solution.py:394
  7.1 0.7 copy-done.6
  7.8 0.7 copy-done.7
  8.5 1.6 %shard_map.122 = (f32[32,32,256]{2,1,0:T(8,128)S(1)}, f32[32,32,256]{2,1,0:T(8,128)S(1)}) custom-call(f32[32,32,256]{2,1,0:T(8,128)S(1)} %get-tuple-element.42.now.refs_6_, f32[32,32,256]{2,1,0:T(8,128)} %prev_hbm.1, s32[1,1,512]{2,1,0:T(1,128)S(1)} %copy-done.7, f32[1,1,4,512]{3,2,1,0:T(4,128)S(1)} %copy-done.6), custom_call_target="tpu_custom_call" | custom-call | flops 2000000000 | bytes 7340032 | tf_op jit(solution)/shard_map/pallas_call | solution.py:396
  10.1 0.0 copy-start.1
  10.1 0.0 collective-permute-done.2.refs_2_
  10.2 0.0 collective-permute-done.3.refs_3_
  10.2 0.3 shard_map.123
  10.5 0.1 collective-permute-start.4
  10.6 1.4 %collective-permute-start.5 = (f32[2,32,256]{2,1,0:T(8,128)S(1)}, f32[2,32,256]{2,1,0:T(8,128)S(1)}, u32[]{:S(2)}, u32[]{:S(2)}) collective-permute-start(f32[2,32,256]{2,1,0:T(8,128)S(1)} %get-tuple-element.46), channel_id=1, source_target_pairs={{0,1},{1,0},{2,3},{3,2},{4,5},{5,4},{6,7},{7,6},{8,9},{9,8},{10,11... | collective-permute-start | bytes 196616 | tf_op jit(solution)/shard_map/ppermute | solution.py:394
  12.0 3.6 %collective-permute-start.6 = (f32[32,2,256]{2,1,0:T(2,128)S(1)}, f32[32,2,256]{2,1,0:T(2,128)S(1)}, u32[]{:S(2)}, u32[]{:S(2)}) collective-permute-start(f32[32,2,256]{2,1,0:T(2,128)S(1)} %get-tuple-element.47), channel_id=1, source_target_pairs={{0,1},{1,0},{2,3},{3,2},{4,5},{5,4},{6,7},{7,6},{8,9},{9,8},{10,11... | collective-permute-start | bytes 196616 | tf_op jit(solution)/shard_map/ppermute | solution.py:394
  15.6 0.8 collective-permute-start.7
  16.4 1.8 %shard_map.124 = (f32[32,32,256]{2,1,0:T(8,128)S(1)}, f32[32,32,256]{2,1,0:T(8,128)S(1)}, f32[32,32,256]{2,1,0:T(8,128)S(1)}, f32[32,32,256]{2,1,0:T(8,128)S(1)}) custom-call(s32[1]{0:T(128)} %bitcast.spot, f32[32,2,256]{2,1,0:T(2,128)S(1)} %collective-permute-done.refs_0_, f32[2,32,256]{2,1,0:T(8,128)S(1)} %collective-permute-done.1.refs_1_, ...), custom_call_target="tpu_custom_call" | custom-call | flops 2000000000 | bytes 7340032 | tf_op jit(solution)/shard_map/pallas_call | solution.py:410
  18.3 0.0 collective-permute-done.5.refs_1_
  18.3 1.0 %collective-permute-done.6.refs_2_ = f32[32,2,256]{2,1,0:T(2,128)S(1)} collective-permute-done((f32[32,2,256]{2,1,0:T(2,128)S(1)}, f32[32,2,256]{2,1,0:T(2,128)S(1)}, u32[]{:S(2)}, u32[]{:S(2)}) %collective-permute-start.6) | collective-permute-done | bytes 65568 | tf_op jit(solution)/shard_map/ppermute | solution.py:394
  19.3 0.0 collective-permute-done.7.refs_3_
  19.3 0.3 shard_map.125
  19.6 1.3 %collective-permute-start.10 = (f32[32,2,256]{2,1,0:T(2,128)S(1)}, f32[32,2,256]{2,1,0:T(2,128)S(1)}, u32[]{:S(2)}, u32[]{:S(2)}) collective-permute-start(f32[32,2,256]{2,1,0:T(2,128)S(1)} %get-tuple-element.53), channel_id=1, source_target_pairs={{0,1},{1,0},{2,3},{3,2},{4,5},{5,4},{6,7},{7,6},{8,9},{9,8},{10,11... | collective-permute-start | bytes 196616 | tf_op jit(solution)/shard_map/ppermute | solution.py:394
  21.0 0.5 collective-permute-start.8
  21.5 0.6 collective-permute-start.9
  22.1 1.8 %shard_map.126 = (f32[32,32,256]{2,1,0:T(8,128)S(1)}, f32[32,32,256]{2,1,0:T(8,128)S(1)}, f32[32,32,256]{2,1,0:T(8,128)S(1)}, f32[32,32,256]{2,1,0:T(8,128)S(1)}) custom-call(s32[1]{0:T(128)} %bitcast.spot, f32[32,2,256]{2,1,0:T(2,128)S(1)} %collective-permute-done.4.refs_0_, f32[2,32,256]{2,1,0:T(8,128)S(1)} %collective-permute-done.5.refs_1_, ...), custom_call_target="tpu_custom_call" | custom-call | flops 2000000000 | bytes 7340032 | tf_op jit(solution)/shard_map/pallas_call | solution.py:410
  23.9 0.1 collective-permute-done.10.refs_2_
  24.0 0.0 collective-permute-done.8.refs_0_
  24.0 4.0 %collective-permute-done.9.refs_1_ = f32[2,32,256]{2,1,0:T(8,128)S(1)} collective-permute-done((f32[2,32,256]{2,1,0:T(8,128)S(1)}, f32[2,32,256]{2,1,0:T(8,128)S(1)}, u32[]{:S(2)}, u32[]{:S(2)}) %collective-permute-start.9) | collective-permute-done | bytes 65568 | tf_op jit(solution)/shard_map/ppermute | solution.py:394
  28.0 0.3 shard_map.127
  28.3 0.1 collective-permute-start.12
  28.4 0.8 collective-permute-start.13
  29.2 3.7 %collective-permute-start.14 = (f32[32,2,256]{2,1,0:T(2,128)S(1)}, f32[32,2,256]{2,1,0:T(2,128)S(1)}, u32[]{:S(2)}, u32[]{:S(2)}) collective-permute-start(f32[32,2,256]{2,1,0:T(2,128)S(1)} %get-tuple-element.61), channel_id=1, source_target_pairs={{0,1},{1,0},{2,3},{3,2},{4,5},{5,4},{6,7},{7,6},{8,9},{9,8},{10,11... | collective-permute-start | bytes 196616 | tf_op jit(solution)/shard_map/ppermute | solution.py:394
  33.0 0.5 collective-permute-start.15
  33.5 1.2 %shard_map.128 = (f32[32,32,256]{2,1,0:T(8,128)S(1)}, f32[32,32,256]{2,1,0:T(8,128)S(1)}, f32[32,32,256]{2,1,0:T(8,128)S(1)}) custom-call(s32[1]{0:T(128)} %bitcast.spot, f32[32,2,256]{2,1,0:T(2,128)S(1)} %collective-permute-done.8.refs_0_, f32[2,32,256]{2,1,0:T(8,128)S(1)} %collective-permute-done.9.refs_1_, ...), custom_call_target="tpu_custom_call" | custom-call | flops 2000000000 | bytes 7340032 | tf_op jit(solution)/shard_map/pallas_call | solution.py:410
  34.6 0.0 collective-permute-done.12.refs_0_
  34.7 1.7 %collective-permute-done.13.refs_1_ = f32[2,32,256]{2,1,0:T(8,128)S(1)} collective-permute-done((f32[2,32,256]{2,1,0:T(8,128)S(1)}, f32[2,32,256]{2,1,0:T(8,128)S(1)}, u32[]{:S(2)}, u32[]{:S(2)}) %collective-permute-start.13) | collective-permute-done | bytes 65568 | tf_op jit(solution)/shard_map/ppermute | solution.py:394
  36.3 0.3 collective-permute-done.14.refs_2_
  36.6 0.7 shard_map.129
  37.3 25.3 %all_to_all.10.chunks = f32[64,8,128]{2,1,0:T(8,128)S(1)} all-to-all(f32[64,8,128]{2,1,0:T(8,128)S(1)} %bitcast.3), channel_id=1, replica_groups={{0,1,2,3,4,5,6,7,8,9,10,11,12,13,14,15,64,65,66,67,68,69,70,71,72,73,74..., dimensions={0} | all-to-all | bytes 524288 | tf_op jit(solution)/shard_map/all_to_all | solution.py:439
  62.6 0.5 shard_map.130.refs_0_
  63.1 1.3 %collective-permute-start.17 = (f32[128,128]{1,0:T(8,128)S(1)}, f32[128,128]{1,0:T(8,128)S(1)}, u32[]{:S(2)}, u32[]{:S(2)}) collective-permute-start(f32[128,128]{1,0:T(8,128)S(1)} %shard_map.130.refs_0_), channel_id=1, source_target_pairs={{0,32},{16,48},{32,0},{48,16},{64,96},{80,112},{96,64},{112,80},{1... | collective-permute-start | bytes 196616 | tf_op jit(solution)/shard_map/ppermute | solution.py:444
  64.5 2.0 %shard_map.131 = (f32[32,32,256]{2,1,0:T(8,128)}, f32[32,32,256]{2,1,0:T(8,128)}) custom-call(s32[1]{0:T(128)} %bitcast.spot, f32[32,2,256]{2,1,0:T(2,128)S(1)} %collective-permute-done.12.refs_0_, f32[2,32,256]{2,1,0:T(8,128)S(1)} %collective-permute-done.13.refs_1_, f32[32,2,256]{2,1,0:T(2,128)S(1)} %collective-permute-done.14.refs_2_, ...), custom_call_target="tpu_custom_call" | custom-call | flops 2000000000 | bytes 7340032 | tf_op jit(solution)/shard_map/pallas_call | solution.py:426
  66.4 0.1 collective-permute-start.16
  66.5 2.4 %collective-permute-done.17.refs_2_ = f32[128,128]{1,0:T(8,128)S(1)} collective-permute-done((f32[128,128]{1,0:T(8,128)S(1)}, f32[128,128]{1,0:T(8,128)S(1)}, u32[]{:S(2)}, u32[]{:S(2)}) %collective-permute-start.17) | collective-permute-done | bytes 65568 | tf_op jit(solution)/shard_map/ppermute | solution.py:444
  69.0 1.2 %collective-permute-done.18.refs_3_ = f32[128,128]{1,0:T(8,128)S(1)} collective-permute-done((f32[128,128]{1,0:T(8,128)S(1)}, f32[128,128]{1,0:T(8,128)S(1)}, u32[]{:S(2)}, u32[]{:S(2)}) %collective-permute-start.18) | collective-permute-done | bytes 65568 | tf_op jit(solution)/shard_map/ppermute | solution.py:447
  70.2 0.7 shard_map.132
  70.9 18.2 %all_to_all.11 = f32[64,8,128]{2,1,0:T(8,128)S(1)} all-to-all(f32[64,8,128]{2,1,0:T(8,128)S(1)} %shard_map.132), channel_id=1, replica_groups={{0,1,2,3,4,5,6,7,8,9,10,11,12,13,14,15,64,65,66,67,68,69,70,71,72,73,74..., dimensions={0} | all-to-all | bytes 524288 | tf_op jit(solution)/shard_map/all_to_all | solution.py:457
  89.1 1.2 %shard_map.133 = f32[32,32,256]{2,1,0:T(8,128)} custom-call(f32[512,128]{1,0:T(8,128)S(1)} %bitcast.4, f32[64,256]{1,0:T(8,128)S(1)} %copy-done.5), custom_call_target="tpu_custom_call" | custom-call | flops 1000000 | bytes 262144 | tf_op jit(solution)/shard_map/pallas_call | solution.py:458
  (21 shorter events, 0.0 us)
Async XLA Ops:
  1.9 8.2 %collective-permute-start = (f32[32,2,256]{2,1,0:T(2,128)S(1)}, f32[32,2,256]{2,1,0:T(2,128)S(1)}, u32[]{:S(2)}, u32[]{:S(2)}) collective-permute-start(f32[32,2,256]{2,1,0:T(2,128)S(1)} %get-tuple-element.38), channel_id=1, source_target_pairs={{0,16},{1,2},{2,1},{3,4},{4,3},{5,6},{6,5},{7,8},{8,7},{9,10},{10,... | collective-permute-start | bytes 196616 | tf_op jit(solution)/shard_map/ppermute | solution.py:394
  2.0 8.1 %collective-permute-start.1 = (f32[2,32,256]{2,1,0:T(8,128)S(1)}, f32[2,32,256]{2,1,0:T(8,128)S(1)}, u32[]{:S(2)}, u32[]{:S(2)}) collective-permute-start(f32[2,32,256]{2,1,0:T(8,128)S(1)} %get-tuple-element.39), channel_id=1, source_target_pairs={{0,1},{1,0},{2,3},{3,2},{4,5},{5,4},{6,7},{7,6},{8,9},{9,8},{10,11... | collective-permute-start | bytes 196616 | tf_op jit(solution)/shard_map/ppermute | solution.py:394
  4.2 6.0 %collective-permute-start.2 = (f32[32,2,256]{2,1,0:T(2,128)S(1)}, f32[32,2,256]{2,1,0:T(2,128)S(1)}, u32[]{:S(2)}, u32[]{:S(2)}) collective-permute-start(f32[32,2,256]{2,1,0:T(2,128)S(1)} %get-tuple-element.40), channel_id=1, source_target_pairs={{0,1},{1,0},{2,3},{3,2},{4,5},{5,4},{6,7},{7,6},{8,9},{9,8},{10,11... | collective-permute-start | bytes 196616 | tf_op jit(solution)/shard_map/ppermute | solution.py:394
  5.5 4.7 %collective-permute-start.3 = (f32[2,32,256]{2,1,0:T(8,128)S(1)}, f32[2,32,256]{2,1,0:T(8,128)S(1)}, u32[]{:S(2)}, u32[]{:S(2)}) collective-permute-start(f32[2,32,256]{2,1,0:T(8,128)S(1)} %get-tuple-element.41), channel_id=1, source_target_pairs={{0,16},{1,17},{2,18},{3,19},{4,20},{5,21},{6,22},{7,23},{8,24},{9,... | collective-permute-start | bytes 196616 | tf_op jit(solution)/shard_map/ppermute | solution.py:394
  7.1 0.7 copy-start.6
  7.8 0.7 copy-start.7
  8.5 1.7 %copy-start = (f32[32,32,256]{2,1,0:T(8,128)S(1)}, f32[32,32,256]{2,1,0:T(8,128)}, u32[]{:S(2)}) copy-start(f32[32,32,256]{2,1,0:T(8,128)} %refs_7_.7) | copy-start | bytes 3145732
  10.1 6.3 %copy-start.1 = (bf16[4,32,32,256]{3,2,1,0:T(8,128)(2,1)S(1)}, bf16[4,32,32,256]{3,2,1,0:T(8,128)(2,1)}, u32[]{:S(2)}) copy-start(bf16[4,32,32,256]{3,2,1,0:T(8,128)(2,1)} %refs_4_.8) | copy-start | bytes 6291460
  10.5 7.8 %collective-permute-start.4 = (f32[32,2,256]{2,1,0:T(2,128)S(1)}, f32[32,2,256]{2,1,0:T(2,128)S(1)}, u32[]{:S(2)}, u32[]{:S(2)}) collective-permute-start(f32[32,2,256]{2,1,0:T(2,128)S(1)} %get-tuple-element.45), channel_id=1, source_target_pairs={{0,16},{1,2},{2,1},{3,4},{4,3},{5,6},{6,5},{7,8},{8,7},{9,10},{10,... | collective-permute-start | bytes 196616 | tf_op jit(solution)/shard_map/ppermute | solution.py:394
  10.6 7.7 %collective-permute-start.5 = (f32[2,32,256]{2,1,0:T(8,128)S(1)}, f32[2,32,256]{2,1,0:T(8,128)S(1)}, u32[]{:S(2)}, u32[]{:S(2)}) collective-permute-start(f32[2,32,256]{2,1,0:T(8,128)S(1)} %get-tuple-element.46), channel_id=1, source_target_pairs={{0,1},{1,0},{2,3},{3,2},{4,5},{5,4},{6,7},{7,6},{8,9},{9,8},{10,11... | collective-permute-start | bytes 196616 | tf_op jit(solution)/shard_map/ppermute | solution.py:394
  12.0 7.2 %collective-permute-start.6 = (f32[32,2,256]{2,1,0:T(2,128)S(1)}, f32[32,2,256]{2,1,0:T(2,128)S(1)}, u32[]{:S(2)}, u32[]{:S(2)}) collective-permute-start(f32[32,2,256]{2,1,0:T(2,128)S(1)} %get-tuple-element.47), channel_id=1, source_target_pairs={{0,1},{1,0},{2,3},{3,2},{4,5},{5,4},{6,7},{7,6},{8,9},{9,8},{10,11... | collective-permute-start | bytes 196616 | tf_op jit(solution)/shard_map/ppermute | solution.py:394
  15.6 3.6 %collective-permute-start.7 = (f32[2,32,256]{2,1,0:T(8,128)S(1)}, f32[2,32,256]{2,1,0:T(8,128)S(1)}, u32[]{:S(2)}, u32[]{:S(2)}) collective-permute-start(f32[2,32,256]{2,1,0:T(8,128)S(1)} %get-tuple-element.48), channel_id=1, source_target_pairs={{0,16},{1,17},{2,18},{3,19},{4,20},{5,21},{6,22},{7,23},{8,24},{9,... | collective-permute-start | bytes 196616 | tf_op jit(solution)/shard_map/ppermute | solution.py:394
  19.6 4.4 %collective-permute-start.10 = (f32[32,2,256]{2,1,0:T(2,128)S(1)}, f32[32,2,256]{2,1,0:T(2,128)S(1)}, u32[]{:S(2)}, u32[]{:S(2)}) collective-permute-start(f32[32,2,256]{2,1,0:T(2,128)S(1)} %get-tuple-element.53), channel_id=1, source_target_pairs={{0,1},{1,0},{2,3},{3,2},{4,5},{5,4},{6,7},{7,6},{8,9},{9,8},{10,11... | collective-permute-start | bytes 196616 | tf_op jit(solution)/shard_map/ppermute | solution.py:394
  20.9 3.0 %collective-permute-start.11 = (f32[2,32,256]{2,1,0:T(8,128)S(1)}, f32[2,32,256]{2,1,0:T(8,128)S(1)}, u32[]{:S(2)}, u32[]{:S(2)}) collective-permute-start(f32[2,32,256]{2,1,0:T(8,128)S(1)} %get-tuple-element.54), channel_id=1, source_target_pairs={{0,16},{1,17},{2,18},{3,19},{4,20},{5,21},{6,22},{7,23},{8,24},{9,... | collective-permute-start | bytes 196616 | tf_op jit(solution)/shard_map/ppermute | solution.py:394
  21.0 3.0 %collective-permute-start.8 = (f32[32,2,256]{2,1,0:T(2,128)S(1)}, f32[32,2,256]{2,1,0:T(2,128)S(1)}, u32[]{:S(2)}, u32[]{:S(2)}) collective-permute-start(f32[32,2,256]{2,1,0:T(2,128)S(1)} %get-tuple-element.51), channel_id=1, source_target_pairs={{0,16},{1,2},{2,1},{3,4},{4,3},{5,6},{6,5},{7,8},{8,7},{9,10},{10,... | collective-permute-start | bytes 196616 | tf_op jit(solution)/shard_map/ppermute | solution.py:394
  21.5 6.5 %collective-permute-start.9 = (f32[2,32,256]{2,1,0:T(8,128)S(1)}, f32[2,32,256]{2,1,0:T(8,128)S(1)}, u32[]{:S(2)}, u32[]{:S(2)}) collective-permute-start(f32[2,32,256]{2,1,0:T(8,128)S(1)} %get-tuple-element.52), channel_id=1, source_target_pairs={{0,1},{1,0},{2,3},{3,2},{4,5},{5,4},{6,7},{7,6},{8,9},{9,8},{10,11... | collective-permute-start | bytes 196616 | tf_op jit(solution)/shard_map/ppermute | solution.py:394
  28.3 6.3 %collective-permute-start.12 = (f32[32,2,256]{2,1,0:T(2,128)S(1)}, f32[32,2,256]{2,1,0:T(2,128)S(1)}, u32[]{:S(2)}, u32[]{:S(2)}) collective-permute-start(f32[32,2,256]{2,1,0:T(2,128)S(1)} %get-tuple-element.59), channel_id=1, source_target_pairs={{0,16},{1,2},{2,1},{3,4},{4,3},{5,6},{6,5},{7,8},{8,7},{9,10},{10,... | collective-permute-start | bytes 196616 | tf_op jit(solution)/shard_map/ppermute | solution.py:394
  28.4 7.9 %collective-permute-start.13 = (f32[2,32,256]{2,1,0:T(8,128)S(1)}, f32[2,32,256]{2,1,0:T(8,128)S(1)}, u32[]{:S(2)}, u32[]{:S(2)}) collective-permute-start(f32[2,32,256]{2,1,0:T(8,128)S(1)} %get-tuple-element.60), channel_id=1, source_target_pairs={{0,1},{1,0},{2,3},{3,2},{4,5},{5,4},{6,7},{7,6},{8,9},{9,8},{10,11... | collective-permute-start | bytes 196616 | tf_op jit(solution)/shard_map/ppermute | solution.py:394
  29.2 7.4 %collective-permute-start.14 = (f32[32,2,256]{2,1,0:T(2,128)S(1)}, f32[32,2,256]{2,1,0:T(2,128)S(1)}, u32[]{:S(2)}, u32[]{:S(2)}) collective-permute-start(f32[32,2,256]{2,1,0:T(2,128)S(1)} %get-tuple-element.61), channel_id=1, source_target_pairs={{0,1},{1,0},{2,3},{3,2},{4,5},{5,4},{6,7},{7,6},{8,9},{9,8},{10,11... | collective-permute-start | bytes 196616 | tf_op jit(solution)/shard_map/ppermute | solution.py:394
  33.0 3.6 %collective-permute-start.15 = (f32[2,32,256]{2,1,0:T(8,128)S(1)}, f32[2,32,256]{2,1,0:T(8,128)S(1)}, u32[]{:S(2)}, u32[]{:S(2)}) collective-permute-start(f32[2,32,256]{2,1,0:T(8,128)S(1)} %get-tuple-element.62), channel_id=1, source_target_pairs={{0,16},{1,17},{2,18},{3,19},{4,20},{5,21},{6,22},{7,23},{8,24},{9,... | collective-permute-start | bytes 196616 | tf_op jit(solution)/shard_map/ppermute | solution.py:394
  33.5 3.2 %copy-start.4 = (f32[64,256]{1,0:T(8,128)S(1)}, f32[64,256]{1,0:T(8,128)}, u32[]{:S(2)}) copy-start(f32[64,256]{1,0:T(8,128)} %constant.18.clone.refs_6_) | copy-start | bytes 196612
  36.6 26.0 %copy-start.2 = (f32[128,512]{1,0:T(8,128)S(1)}, f32[128,512]{1,0:T(8,128)}, u32[]{:S(2)}) copy-start(f32[128,512]{1,0:T(8,128)} %constant.19.clone.table_y.refs_5_) | copy-start | bytes 786436
  63.1 5.9 %collective-permute-start.17 = (f32[128,128]{1,0:T(8,128)S(1)}, f32[128,128]{1,0:T(8,128)S(1)}, u32[]{:S(2)}, u32[]{:S(2)}) collective-permute-start(f32[128,128]{1,0:T(8,128)S(1)} %shard_map.130.refs_0_), channel_id=1, source_target_pairs={{0,32},{16,48},{32,0},{48,16},{64,96},{80,112},{96,64},{112,80},{1... | collective-permute-start | bytes 196616 | tf_op jit(solution)/shard_map/ppermute | solution.py:444
  64.5 5.8 %copy-start.3 = (f32[7,128,128]{2,1,0:T(8,128)S(1)}, f32[7,128,128]{2,1,0:T(8,128)}, u32[]{:S(2)}) copy-start(f32[7,128,128]{2,1,0:T(8,128)} %constant.20.clone.refs_4_) | copy-start | bytes 1376260
  64.5 24.6 %copy-start.5 = (f32[64,256]{1,0:T(8,128)S(1)}, f32[64,256]{1,0:T(8,128)}, u32[]{:S(2)}) copy-start(f32[64,256]{1,0:T(8,128)} %constant.17.clone.table_z) | copy-start | bytes 196612
  66.4 2.5 %collective-permute-start.16 = (f32[128,128]{1,0:T(8,128)S(1)}, f32[128,128]{1,0:T(8,128)S(1)}, u32[]{:S(2)}, u32[]{:S(2)}) collective-permute-start(f32[128,128]{1,0:T(8,128)S(1)} %shard_map.130.refs_0_), channel_id=1, source_target_pairs={{0,16},{16,0},{32,48},{48,32},{64,80},{80,64},{96,112},{112,96},{1... | collective-permute-start | bytes 196616 | tf_op jit(solution)/shard_map/ppermute | solution.py:445
  69.0 1.3 %collective-permute-start.18 = (f32[128,128]{1,0:T(8,128)S(1)}, f32[128,128]{1,0:T(8,128)S(1)}, u32[]{:S(2)}, u32[]{:S(2)}) collective-permute-start(f32[128,128]{1,0:T(8,128)S(1)} %collective-permute-done.17.refs_2_), channel_id=1, source_target_pairs={{0,16},{16,0},{32,48},{48,32},{64,80},{80,64},{96,112},{112,96},{1... | collective-permute-start | bytes 196616 | tf_op jit(solution)/shard_map/ppermute | solution.py:447

commit v6 on v5

--- a/solution.py
+++ b/solution.py
@@ -17,7 +17,7 @@
 TWELFTH = 1.0 / 12.0
 PACK_ROOM = 52
 FIRST_ROOM = 50
-ORDER = (3, 1, 2, 0)
+ORDER = (3, 2, 1, 0)
 
 HBM = pl.BlockSpec(memory_space=pltpu.HBM)
 VMEM = pl.BlockSpec(memory_space=pltpu.VMEM)
@@ -80,7 +80,7 @@
     kernel(flags, *refs)
 
 
-def pack(flags, now_hbm, now, y_odd, x_odd, y_even, x_even, sems):
+def pack(flags, now_hbm, now, y_odd, y_even, x_odd, x_even, sems):
     size_x, size_y, _ = now.shape
     step = size_x // 4
     copies = []
@@ -135,7 +135,7 @@
     return value + x_change[x] if x in x_change else value
 
 
-def faces_after(flags, y_odd, x_odd, y_even, x_even, courant, base, lap, out_y_odd, out_x_odd, out_y_even, out_x_even):
+def faces_after(flags, y_odd, y_even, x_odd, x_even, courant, base, lap, out_y_odd, out_y_even, out_x_odd, out_x_even):
     size_x, size_y, _ = base.shape
     x_change = x_changes(flags, x_even, x_odd, size_x)
     layers = {}
@@ -220,7 +220,7 @@
 
 
 def later_step(step, flags, *refs):
-    y_odd, x_odd, y_even, x_even, base_in, lap_in, prev, courant, forward, cells, traces, *refs = refs
+    y_odd, y_even, x_odd, x_even, base_in, lap_in, prev, courant, forward, cells, traces, *refs = refs
     gradient_in = refs.pop(0) if step > 1 else None
     last = step == STEPS - 1
     now, lap, gradient = refs[:3]
@@ -246,7 +246,7 @@
                 base[x] = (2.0 * now[x] - prev[x]) + inject[i]
 
 
-def finish(flags, y_odd, x_odd, y_even, x_even, now, lap, prev, courant, cells, traces, next_hbm, now_hbm, nxt, sems):
+def finish(flags, y_odd, y_even, x_odd, x_even, now, lap, prev, courant, cells, traces, next_hbm, now_hbm, nxt, sems):
     size_x, size_y, size_z = now.shape
     layers = ROWS // size_y
     keep = pltpu.make_async_copy(now, now_hbm, sems.at[0])
@@ -269,7 +269,7 @@
     keep.wait()
 
 
-def project_z(flags, y_odd, x_odd, y_even, x_even, forward, gradient, table_z, coef):
+def project_z(flags, y_odd, y_even, x_odd, x_even, forward, gradient, table_z, coef):
     size_x, size_y, _ = gradient.shape
     table = split(table_z[...])
     x_change = x_changes(flags, x_even, x_odd, size_x)
@@ -382,7 +382,7 @@
 
     now, *faces = call(
         placed(pack),
-        (field, y_face, x_face, y_face, x_face),
+        (field, y_face, y_face, x_face, x_face),
         [SMEM, HBM],
         scratch=[DMA((4,))],
         room=PACK_ROOM,
@@ -418,7 +418,7 @@
         halo = sent
         if step < STEPS - 1:
             faces = call(
-                placed(faces_after), (y_face, x_face, y_face, x_face), [SMEM] + [VMEM] * 7, **light
+                placed(faces_after), (y_face, y_face, x_face, x_face), [SMEM] + [VMEM] * 7, **light
             )(spot, *halo, courant_sq, base, lap)
     coef = call(placed(project_z), lines, [SMEM] + [VMEM] * 7, **light)(
         spot, *halo, forward_fields, gradient, table_z_scaled

time: 90.9 us -> 92.2 us (1.014); the launches traced: 90.5 us -> 90.6 us
  starting transfers between devices: 20.1 us -> 24.8 us
  blocking collectives: 43.4 us -> 40 us
  waiting for transfers between devices: 10.7 us -> 9.44 us
    ppermute x16, starting transfers between devices: 18.6 us -> 23 us  [per_device(): sent = [lax.ppermute(face, both, swaps[i]) for i, face in zip(ORDER, faces)]]
    all_to_all x2, blocking collectives: 43.4 us -> 40 us  [per_device(): lax.all_to_all(coef, both, 0, 0, axis_index_groups=groups, tiled=True)]
    ppermute x16, waiting for transfers between devices: 7.02 us -> 6.09 us  [per_device(): sent = [lax.ppermute(face, both, swaps[i]) for i, face in zip(ORDER, faces)]]
  transfers between devices with their start and end apart: 19 -> 19, of which waited for: 7 -> 6; matrix products, arithmetic and copies ran while one was open for 0% -> 0% of each run, Pallas kernels for 9% -> 9%
where the time goes in v6:
time: 92.2 us; the launch traced here: 90.6 us
  blocking collectives  40 us (43%)
  starting transfers between devices  24.8 us (27%)
  Pallas kernels  13.9 us (15%)
  waiting for transfers between devices  9.44 us (10%)
  local copies, waits for them, and re-layouts  1.4 us (2%)
  between operations  1.01 us (1%)
    all_to_all x2, blocking collectives, per_device(): lax.all_to_all(coef, both, 0, 0, axis_index_groups=groups, tiled=True)  40 us
    ppermute x16, starting transfers between devices, per_device(): sent = [lax.ppermute(face, both, swaps[i]) for i, face in zip(ORDER, faces)]  23 us
    ppermute x16, waiting for transfers between devices, per_device(): sent = [lax.ppermute(face, both, swaps[i]) for i, face in zip(ORDER, faces)]  6.09 us
    pallas_call x3, Pallas kernels, per_device(): call(placed(functools.partial(later_step, step)), (field,) * (3 if last e...  4.86 us
    ppermute x1, waiting for transfers between devices, per_device(): two = lax.ppermute(mine, 'row', across)  2.1 us
    pallas_call x1, Pallas kernels, per_device(): call(placed(finish), (field, field), [SMEM] + [VMEM] * 10, out_specs=(HBM...  1.98 us
  transfers between devices with their start and end apart: 19, of which 6 were waited for; matrix products, arithmetic and copies ran while one was open for 0% of the time, Pallas kernels for 9%

profile of v6, /device:TPU:16, one launch (start us, length us, event | category | flops | bytes accessed | tf_op | source)
XLA Modules:
  0.0 90.6 jit_solution(13221030579583524272)
XLA Ops:
  0.6 1.3 %shard_map.121 = (f32[32,32,256]{2,1,0:T(8,128)S(1)}, f32[32,2,256]{2,1,0:T(2,128)S(1)}, f32[32,2,256]{2,1,0:T(2,128)S(1)}, f32[2,32,256]{2,1,0:T(8,128)S(1)}, f32[2,32,256]{2,1,0:T(8,128)S(1)}) custom-call(s32[1]{0:T(128)} %bitcast.spot, f32[32,32,256]{2,1,0:T(8,128)} %refs_0_.1), custom_call_target="tpu_custom_call" | custom-call | flops 1000000 | bytes 262144 | tf_op jit(solution)/shard_map/pallas_call | solution.py:383
  1.9 0.1 collective-permute-start
  2.0 3.4 %collective-permute-start.1 = (f32[32,2,256]{2,1,0:T(2,128)S(1)}, f32[32,2,256]{2,1,0:T(2,128)S(1)}, u32[]{:S(2)}, u32[]{:S(2)}) collective-permute-start(f32[32,2,256]{2,1,0:T(2,128)S(1)} %get-tuple-element.39), channel_id=1, source_target_pairs={{0,1},{1,0},{2,3},{3,2},{4,5},{5,4},{6,7},{7,6},{8,9},{9,8},{10,11... | collective-permute-start | bytes 196616 | tf_op jit(solution)/shard_map/ppermute | solution.py:394
  5.4 0.0 collective-permute-start.2
  5.4 1.4 %collective-permute-start.3 = (f32[2,32,256]{2,1,0:T(8,128)S(1)}, f32[2,32,256]{2,1,0:T(8,128)S(1)}, u32[]{:S(2)}, u32[]{:S(2)}) collective-permute-start(f32[2,32,256]{2,1,0:T(8,128)S(1)} %get-tuple-element.41), channel_id=1, source_target_pairs={{0,16},{1,17},{2,18},{3,19},{4,20},{5,21},{6,22},{7,23},{8,24},{9,... | collective-permute-start | bytes 196616 | tf_op jit(solution)/shard_map/ppermute | solution.py:394
  6.8 0.7 copy-done.6
  7.5 0.7 copy-done.7
  8.1 1.6 %shard_map.122 = (f32[32,32,256]{2,1,0:T(8,128)S(1)}, f32[32,32,256]{2,1,0:T(8,128)S(1)}) custom-call(f32[32,32,256]{2,1,0:T(8,128)S(1)} %get-tuple-element.42.now.refs_6_, f32[32,32,256]{2,1,0:T(8,128)} %prev_hbm.1, s32[1,1,512]{2,1,0:T(1,128)S(1)} %copy-done.7, f32[1,1,4,512]{3,2,1,0:T(4,128)S(1)} %copy-done.6), custom_call_target="tpu_custom_call" | custom-call | flops 2000000000 | bytes 7340032 | tf_op jit(solution)/shard_map/pallas_call | solution.py:396
  9.8 0.0 copy-start.1
  9.8 0.0 collective-permute-done.1.refs_1_
  9.8 1.5 %collective-permute-done.2.refs_2_ = f32[2,32,256]{2,1,0:T(8,128)S(1)} collective-permute-done((f32[2,32,256]{2,1,0:T(8,128)S(1)}, f32[2,32,256]{2,1,0:T(8,128)S(1)}, u32[]{:S(2)}, u32[]{:S(2)}) %collective-permute-start.2) | collective-permute-done | bytes 65568 | tf_op jit(solution)/shard_map/ppermute | solution.py:394
  11.3 0.3 shard_map.123
  11.6 0.1 collective-permute-start.4
  11.7 3.4 %collective-permute-start.5 = (f32[32,2,256]{2,1,0:T(2,128)S(1)}, f32[32,2,256]{2,1,0:T(2,128)S(1)}, u32[]{:S(2)}, u32[]{:S(2)}) collective-permute-start(f32[32,2,256]{2,1,0:T(2,128)S(1)} %get-tuple-element.46), channel_id=1, source_target_pairs={{0,1},{1,0},{2,3},{3,2},{4,5},{5,4},{6,7},{7,6},{8,9},{9,8},{10,11... | collective-permute-start | bytes 196616 | tf_op jit(solution)/shard_map/ppermute | solution.py:394
  15.1 0.0 collective-permute-start.6
  15.1 1.9 %collective-permute-start.7 = (f32[2,32,256]{2,1,0:T(8,128)S(1)}, f32[2,32,256]{2,1,0:T(8,128)S(1)}, u32[]{:S(2)}, u32[]{:S(2)}) collective-permute-start(f32[2,32,256]{2,1,0:T(8,128)S(1)} %get-tuple-element.48), channel_id=1, source_target_pairs={{0,16},{1,17},{2,18},{3,19},{4,20},{5,21},{6,22},{7,23},{8,24},{9,... | collective-permute-start | bytes 196616 | tf_op jit(solution)/shard_map/ppermute | solution.py:394
  17.0 1.8 %shard_map.124 = (f32[32,32,256]{2,1,0:T(8,128)S(1)}, f32[32,32,256]{2,1,0:T(8,128)S(1)}, f32[32,32,256]{2,1,0:T(8,128)S(1)}, f32[32,32,256]{2,1,0:T(8,128)S(1)}) custom-call(s32[1]{0:T(128)} %bitcast.spot, f32[32,2,256]{2,1,0:T(2,128)S(1)} %collective-permute-done.refs_0_, f32[32,2,256]{2,1,0:T(2,128)S(1)} %collective-permute-done.1.refs_1_, ...), custom_call_target="tpu_custom_call" | custom-call | flops 2000000000 | bytes 7340032 | tf_op jit(solution)/shard_map/pallas_call | solution.py:410
  18.8 0.0 collective-permute-done.5.refs_1_
  18.8 2.1 %collective-permute-done.6.refs_2_ = f32[2,32,256]{2,1,0:T(8,128)S(1)} collective-permute-done((f32[2,32,256]{2,1,0:T(8,128)S(1)}, f32[2,32,256]{2,1,0:T(8,128)S(1)}, u32[]{:S(2)}, u32[]{:S(2)}) %collective-permute-start.6) | collective-permute-done | bytes 65568 | tf_op jit(solution)/shard_map/ppermute | solution.py:394
  21.0 0.0 collective-permute-done.7.refs_3_
  21.0 0.3 shard_map.125
  21.3 0.1 collective-permute-start.10
  21.4 2.2 %collective-permute-start.11 = (f32[2,32,256]{2,1,0:T(8,128)S(1)}, f32[2,32,256]{2,1,0:T(8,128)S(1)}, u32[]{:S(2)}, u32[]{:S(2)}) collective-permute-start(f32[2,32,256]{2,1,0:T(8,128)S(1)} %get-tuple-element.54), channel_id=1, source_target_pairs={{0,16},{1,17},{2,18},{3,19},{4,20},{5,21},{6,22},{7,23},{8,24},{9,... | collective-permute-start | bytes 196616 | tf_op jit(solution)/shard_map/ppermute | solution.py:394
  23.6 0.0 collective-permute-start.8
  23.6 3.4 %collective-permute-start.9 = (f32[32,2,256]{2,1,0:T(2,128)S(1)}, f32[32,2,256]{2,1,0:T(2,128)S(1)}, u32[]{:S(2)}, u32[]{:S(2)}) collective-permute-start(f32[32,2,256]{2,1,0:T(2,128)S(1)} %get-tuple-element.52), channel_id=1, source_target_pairs={{0,1},{1,0},{2,3},{3,2},{4,5},{5,4},{6,7},{7,6},{8,9},{9,8},{10,11... | collective-permute-start | bytes 196616 | tf_op jit(solution)/shard_map/ppermute | solution.py:394
  27.0 1.8 %shard_map.126 = (f32[32,32,256]{2,1,0:T(8,128)S(1)}, f32[32,32,256]{2,1,0:T(8,128)S(1)}, f32[32,32,256]{2,1,0:T(8,128)S(1)}, f32[32,32,256]{2,1,0:T(8,128)S(1)}) custom-call(s32[1]{0:T(128)} %bitcast.spot, f32[32,2,256]{2,1,0:T(2,128)S(1)} %collective-permute-done.4.refs_0_, f32[32,2,256]{2,1,0:T(2,128)S(1)} %collective-permute-done.5.refs_1_, ...), custom_call_target="tpu_custom_call" | custom-call | flops 2000000000 | bytes 7340032 | tf_op jit(solution)/shard_map/pallas_call | solution.py:410
  28.8 0.0 collective-permute-done.11.refs_3_
  28.9 0.4 collective-permute-done.9.refs_1_
  29.2 0.3 shard_map.127
  29.6 0.1 collective-permute-start.12
  29.7 4.6 %collective-permute-start.13 = (f32[32,2,256]{2,1,0:T(2,128)S(1)}, f32[32,2,256]{2,1,0:T(2,128)S(1)}, u32[]{:S(2)}, u32[]{:S(2)}) collective-permute-start(f32[32,2,256]{2,1,0:T(2,128)S(1)} %get-tuple-element.60), channel_id=1, source_target_pairs={{0,1},{1,0},{2,3},{3,2},{4,5},{5,4},{6,7},{7,6},{8,9},{9,8},{10,11... | collective-permute-start | bytes 196616 | tf_op jit(solution)/shard_map/ppermute | solution.py:394
  34.3 2.5 %collective-permute-start.15 = (f32[2,32,256]{2,1,0:T(8,128)S(1)}, f32[2,32,256]{2,1,0:T(8,128)S(1)}, u32[]{:S(2)}, u32[]{:S(2)}) collective-permute-start(f32[2,32,256]{2,1,0:T(8,128)S(1)} %get-tuple-element.62), channel_id=1, source_target_pairs={{0,16},{1,17},{2,18},{3,19},{4,20},{5,21},{6,22},{7,23},{8,24},{9,... | collective-permute-start | bytes 196616 | tf_op jit(solution)/shard_map/ppermute | solution.py:394
  36.8 1.2 %shard_map.128 = (f32[32,32,256]{2,1,0:T(8,128)S(1)}, f32[32,32,256]{2,1,0:T(8,128)S(1)}, f32[32,32,256]{2,1,0:T(8,128)S(1)}) custom-call(s32[1]{0:T(128)} %bitcast.spot, f32[32,2,256]{2,1,0:T(2,128)S(1)} %collective-permute-done.8.refs_0_, f32[32,2,256]{2,1,0:T(2,128)S(1)} %collective-permute-done.9.refs_1_, ...), custom_call_target="tpu_custom_call" | custom-call | flops 2000000000 | bytes 7340032 | tf_op jit(solution)/shard_map/pallas_call | solution.py:410
  37.9 0.0 collective-permute-done.12.refs_0_
  38.0 0.0 collective-permute-done.13.refs_1_
  38.0 2.1 %collective-permute-done.14.refs_2_ = f32[2,32,256]{2,1,0:T(8,128)S(1)} collective-permute-done((f32[2,32,256]{2,1,0:T(8,128)S(1)}, f32[2,32,256]{2,1,0:T(8,128)S(1)}, u32[]{:S(2)}, u32[]{:S(2)}) %collective-permute-start.14) | collective-permute-done | bytes 65568 | tf_op jit(solution)/shard_map/ppermute | solution.py:394
  40.1 0.0 collective-permute-done.15.refs_3_
  40.1 0.7 shard_map.129
  40.8 22.7 %all_to_all.10.chunks = f32[64,8,128]{2,1,0:T(8,128)S(1)} all-to-all(f32[64,8,128]{2,1,0:T(8,128)S(1)} %bitcast.3), channel_id=1, replica_groups={{0,1,2,3,4,5,6,7,8,9,10,11,12,13,14,15,64,65,66,67,68,69,70,71,72,73,74..., dimensions={0} | all-to-all | bytes 524288 | tf_op jit(solution)/shard_map/all_to_all | solution.py:439
  63.5 0.5 shard_map.130.refs_0_
  64.0 1.7 %collective-permute-start.17 = (f32[128,128]{1,0:T(8,128)S(1)}, f32[128,128]{1,0:T(8,128)S(1)}, u32[]{:S(2)}, u32[]{:S(2)}) collective-permute-start(f32[128,128]{1,0:T(8,128)S(1)} %shard_map.130.refs_0_), channel_id=1, source_target_pairs={{0,32},{16,48},{32,0},{48,16},{64,96},{80,112},{96,64},{112,80},{1... | collective-permute-start | bytes 196616 | tf_op jit(solution)/shard_map/ppermute | solution.py:444
  65.7 2.0 %shard_map.131 = (f32[32,32,256]{2,1,0:T(8,128)}, f32[32,32,256]{2,1,0:T(8,128)}) custom-call(s32[1]{0:T(128)} %bitcast.spot, f32[32,2,256]{2,1,0:T(2,128)S(1)} %collective-permute-done.12.refs_0_, f32[32,2,256]{2,1,0:T(2,128)S(1)} %collective-permute-done.13.refs_1_, f32[2,32,256]{2,1,0:T(8,128)S(1)} %collective-permute-done.14.refs_2_, ...), custom_call_target="tpu_custom_call" | custom-call | flops 2000000000 | bytes 7340032 | tf_op jit(solution)/shard_map/pallas_call | solution.py:426
  67.6 0.1 collective-permute-start.16
  67.7 2.1 %collective-permute-done.17.refs_2_ = f32[128,128]{1,0:T(8,128)S(1)} collective-permute-done((f32[128,128]{1,0:T(8,128)S(1)}, f32[128,128]{1,0:T(8,128)S(1)}, u32[]{:S(2)}, u32[]{:S(2)}) %collective-permute-start.17) | collective-permute-done | bytes 65568 | tf_op jit(solution)/shard_map/ppermute | solution.py:444
  69.9 1.2 %collective-permute-done.18.refs_3_ = f32[128,128]{1,0:T(8,128)S(1)} collective-permute-done((f32[128,128]{1,0:T(8,128)S(1)}, f32[128,128]{1,0:T(8,128)S(1)}, u32[]{:S(2)}, u32[]{:S(2)}) %collective-permute-start.18) | collective-permute-done | bytes 65568 | tf_op jit(solution)/shard_map/ppermute | solution.py:447
  71.1 0.7 shard_map.132
  71.8 17.3 %all_to_all.11 = f32[64,8,128]{2,1,0:T(8,128)S(1)} all-to-all(f32[64,8,128]{2,1,0:T(8,128)S(1)} %shard_map.132), channel_id=1, replica_groups={{0,1,2,3,4,5,6,7,8,9,10,11,12,13,14,15,64,65,66,67,68,69,70,71,72,73,74..., dimensions={0} | all-to-all | bytes 524288 | tf_op jit(solution)/shard_map/all_to_all | solution.py:457
  89.1 1.3 %shard_map.133 = f32[32,32,256]{2,1,0:T(8,128)} custom-call(f32[512,128]{1,0:T(8,128)S(1)} %bitcast.4, f32[64,256]{1,0:T(8,128)S(1)} %copy-done.5), custom_call_target="tpu_custom_call" | custom-call | flops 1000000 | bytes 262144 | tf_op jit(solution)/shard_map/pallas_call | solution.py:458
  (21 shorter events, 0.0 us)
Async XLA Ops:
  1.9 7.9 %collective-permute-start = (f32[32,2,256]{2,1,0:T(2,128)S(1)}, f32[32,2,256]{2,1,0:T(2,128)S(1)}, u32[]{:S(2)}, u32[]{:S(2)}) collective-permute-start(f32[32,2,256]{2,1,0:T(2,128)S(1)} %get-tuple-element.38), channel_id=1, source_target_pairs={{0,16},{1,2},{2,1},{3,4},{4,3},{5,6},{6,5},{7,8},{8,7},{9,10},{10,... | collective-permute-start | bytes 196616 | tf_op jit(solution)/shard_map/ppermute | solution.py:394
  2.0 7.8 %collective-permute-start.1 = (f32[32,2,256]{2,1,0:T(2,128)S(1)}, f32[32,2,256]{2,1,0:T(2,128)S(1)}, u32[]{:S(2)}, u32[]{:S(2)}) collective-permute-start(f32[32,2,256]{2,1,0:T(2,128)S(1)} %get-tuple-element.39), channel_id=1, source_target_pairs={{0,1},{1,0},{2,3},{3,2},{4,5},{5,4},{6,7},{7,6},{8,9},{9,8},{10,11... | collective-permute-start | bytes 196616 | tf_op jit(solution)/shard_map/ppermute | solution.py:394
  5.4 5.9 %collective-permute-start.2 = (f32[2,32,256]{2,1,0:T(8,128)S(1)}, f32[2,32,256]{2,1,0:T(8,128)S(1)}, u32[]{:S(2)}, u32[]{:S(2)}) collective-permute-start(f32[2,32,256]{2,1,0:T(8,128)S(1)} %get-tuple-element.40), channel_id=1, source_target_pairs={{0,1},{1,0},{2,3},{3,2},{4,5},{5,4},{6,7},{7,6},{8,9},{9,8},{10,11... | collective-permute-start | bytes 196616 | tf_op jit(solution)/shard_map/ppermute | solution.py:394
  5.4 5.9 %collective-permute-start.3 = (f32[2,32,256]{2,1,0:T(8,128)S(1)}, f32[2,32,256]{2,1,0:T(8,128)S(1)}, u32[]{:S(2)}, u32[]{:S(2)}) collective-permute-start(f32[2,32,256]{2,1,0:T(8,128)S(1)} %get-tuple-element.41), channel_id=1, source_target_pairs={{0,16},{1,17},{2,18},{3,19},{4,20},{5,21},{6,22},{7,23},{8,24},{9,... | collective-permute-start | bytes 196616 | tf_op jit(solution)/shard_map/ppermute | solution.py:394
  6.8 0.7 copy-start.6
  7.5 0.7 copy-start.7
  8.1 3.1 %copy-start = (f32[32,32,256]{2,1,0:T(8,128)S(1)}, f32[32,32,256]{2,1,0:T(8,128)}, u32[]{:S(2)}) copy-start(f32[32,32,256]{2,1,0:T(8,128)} %refs_7_.7) | copy-start | bytes 3145732
  9.8 7.2 %copy-start.1 = (bf16[4,32,32,256]{3,2,1,0:T(8,128)(2,1)S(1)}, bf16[4,32,32,256]{3,2,1,0:T(8,128)(2,1)}, u32[]{:S(2)}) copy-start(bf16[4,32,32,256]{3,2,1,0:T(8,128)(2,1)} %refs_4_.8) | copy-start | bytes 6291460
  11.6 7.2 %collective-permute-start.4 = (f32[32,2,256]{2,1,0:T(2,128)S(1)}, f32[32,2,256]{2,1,0:T(2,128)S(1)}, u32[]{:S(2)}, u32[]{:S(2)}) collective-permute-start(f32[32,2,256]{2,1,0:T(2,128)S(1)} %get-tuple-element.45), channel_id=1, source_target_pairs={{0,16},{1,2},{2,1},{3,4},{4,3},{5,6},{6,5},{7,8},{8,7},{9,10},{10,... | collective-permute-start | bytes 196616 | tf_op jit(solution)/shard_map/ppermute | solution.py:394
  11.7 7.1 %collective-permute-start.5 = (f32[32,2,256]{2,1,0:T(2,128)S(1)}, f32[32,2,256]{2,1,0:T(2,128)S(1)}, u32[]{:S(2)}, u32[]{:S(2)}) collective-permute-start(f32[32,2,256]{2,1,0:T(2,128)S(1)} %get-tuple-element.46), channel_id=1, source_target_pairs={{0,1},{1,0},{2,3},{3,2},{4,5},{5,4},{6,7},{7,6},{8,9},{9,8},{10,11... | collective-permute-start | bytes 196616 | tf_op jit(solution)/shard_map/ppermute | solution.py:394
  15.1 5.9 %collective-permute-start.6 = (f32[2,32,256]{2,1,0:T(8,128)S(1)}, f32[2,32,256]{2,1,0:T(8,128)S(1)}, u32[]{:S(2)}, u32[]{:S(2)}) collective-permute-start(f32[2,32,256]{2,1,0:T(8,128)S(1)} %get-tuple-element.47), channel_id=1, source_target_pairs={{0,1},{1,0},{2,3},{3,2},{4,5},{5,4},{6,7},{7,6},{8,9},{9,8},{10,11... | collective-permute-start | bytes 196616 | tf_op jit(solution)/shard_map/ppermute | solution.py:394
  15.1 5.9 %collective-permute-start.7 = (f32[2,32,256]{2,1,0:T(8,128)S(1)}, f32[2,32,256]{2,1,0:T(8,128)S(1)}, u32[]{:S(2)}, u32[]{:S(2)}) collective-permute-start(f32[2,32,256]{2,1,0:T(8,128)S(1)} %get-tuple-element.48), channel_id=1, source_target_pairs={{0,16},{1,17},{2,18},{3,19},{4,20},{5,21},{6,22},{7,23},{8,24},{9,... | collective-permute-start | bytes 196616 | tf_op jit(solution)/shard_map/ppermute | solution.py:394
  21.3 7.5 %collective-permute-start.10 = (f32[2,32,256]{2,1,0:T(8,128)S(1)}, f32[2,32,256]{2,1,0:T(8,128)S(1)}, u32[]{:S(2)}, u32[]{:S(2)}) collective-permute-start(f32[2,32,256]{2,1,0:T(8,128)S(1)} %get-tuple-element.53), channel_id=1, source_target_pairs={{0,1},{1,0},{2,3},{3,2},{4,5},{5,4},{6,7},{7,6},{8,9},{9,8},{10,11... | collective-permute-start | bytes 196616 | tf_op jit(solution)/shard_map/ppermute | solution.py:394
  21.4 7.4 %collective-permute-start.11 = (f32[2,32,256]{2,1,0:T(8,128)S(1)}, f32[2,32,256]{2,1,0:T(8,128)S(1)}, u32[]{:S(2)}, u32[]{:S(2)}) collective-permute-start(f32[2,32,256]{2,1,0:T(8,128)S(1)} %get-tuple-element.54), channel_id=1, source_target_pairs={{0,16},{1,17},{2,18},{3,19},{4,20},{5,21},{6,22},{7,23},{8,24},{9,... | collective-permute-start | bytes 196616 | tf_op jit(solution)/shard_map/ppermute | solution.py:394
  23.6 5.2 %collective-permute-start.8 = (f32[32,2,256]{2,1,0:T(2,128)S(1)}, f32[32,2,256]{2,1,0:T(2,128)S(1)}, u32[]{:S(2)}, u32[]{:S(2)}) collective-permute-start(f32[32,2,256]{2,1,0:T(2,128)S(1)} %get-tuple-element.51), channel_id=1, source_target_pairs={{0,16},{1,2},{2,1},{3,4},{4,3},{5,6},{6,5},{7,8},{8,7},{9,10},{10,... | collective-permute-start | bytes 196616 | tf_op jit(solution)/shard_map/ppermute | solution.py:394
  23.6 5.6 %collective-permute-start.9 = (f32[32,2,256]{2,1,0:T(2,128)S(1)}, f32[32,2,256]{2,1,0:T(2,128)S(1)}, u32[]{:S(2)}, u32[]{:S(2)}) collective-permute-start(f32[32,2,256]{2,1,0:T(2,128)S(1)} %get-tuple-element.52), channel_id=1, source_target_pairs={{0,1},{1,0},{2,3},{3,2},{4,5},{5,4},{6,7},{7,6},{8,9},{9,8},{10,11... | collective-permute-start | bytes 196616 | tf_op jit(solution)/shard_map/ppermute | solution.py:394
  29.6 8.4 %collective-permute-start.12 = (f32[32,2,256]{2,1,0:T(2,128)S(1)}, f32[32,2,256]{2,1,0:T(2,128)S(1)}, u32[]{:S(2)}, u32[]{:S(2)}) collective-permute-start(f32[32,2,256]{2,1,0:T(2,128)S(1)} %get-tuple-element.59), channel_id=1, source_target_pairs={{0,16},{1,2},{2,1},{3,4},{4,3},{5,6},{6,5},{7,8},{8,7},{9,10},{10,... | collective-permute-start | bytes 196616 | tf_op jit(solution)/shard_map/ppermute | solution.py:394
  29.7 8.3 %collective-permute-start.13 = (f32[32,2,256]{2,1,0:T(2,128)S(1)}, f32[32,2,256]{2,1,0:T(2,128)S(1)}, u32[]{:S(2)}, u32[]{:S(2)}) collective-permute-start(f32[32,2,256]{2,1,0:T(2,128)S(1)} %get-tuple-element.60), channel_id=1, source_target_pairs={{0,1},{1,0},{2,3},{3,2},{4,5},{5,4},{6,7},{7,6},{8,9},{9,8},{10,11... | collective-permute-start | bytes 196616 | tf_op jit(solution)/shard_map/ppermute | solution.py:394
  34.2 5.8 %collective-permute-start.14 = (f32[2,32,256]{2,1,0:T(8,128)S(1)}, f32[2,32,256]{2,1,0:T(8,128)S(1)}, u32[]{:S(2)}, u32[]{:S(2)}) collective-permute-start(f32[2,32,256]{2,1,0:T(8,128)S(1)} %get-tuple-element.61), channel_id=1, source_target_pairs={{0,1},{1,0},{2,3},{3,2},{4,5},{5,4},{6,7},{7,6},{8,9},{9,8},{10,11... | collective-permute-start | bytes 196616 | tf_op jit(solution)/shard_map/ppermute | solution.py:394
  34.3 5.8 %collective-permute-start.15 = (f32[2,32,256]{2,1,0:T(8,128)S(1)}, f32[2,32,256]{2,1,0:T(8,128)S(1)}, u32[]{:S(2)}, u32[]{:S(2)}) collective-permute-start(f32[2,32,256]{2,1,0:T(8,128)S(1)} %get-tuple-element.62), channel_id=1, source_target_pairs={{0,16},{1,17},{2,18},{3,19},{4,20},{5,21},{6,22},{7,23},{8,24},{9,... | collective-permute-start | bytes 196616 | tf_op jit(solution)/shard_map/ppermute | solution.py:394
  36.8 3.3 %copy-start.4 = (f32[64,256]{1,0:T(8,128)S(1)}, f32[64,256]{1,0:T(8,128)}, u32[]{:S(2)}) copy-start(f32[64,256]{1,0:T(8,128)} %constant.18.clone.refs_6_) | copy-start | bytes 196612
  40.1 23.5 %copy-start.2 = (f32[128,512]{1,0:T(8,128)S(1)}, f32[128,512]{1,0:T(8,128)}, u32[]{:S(2)}) copy-start(f32[128,512]{1,0:T(8,128)} %constant.19.clone.table_y.refs_5_) | copy-start | bytes 786436
  64.0 5.9 %collective-permute-start.17 = (f32[128,128]{1,0:T(8,128)S(1)}, f32[128,128]{1,0:T(8,128)S(1)}, u32[]{:S(2)}, u32[]{:S(2)}) collective-permute-start(f32[128,128]{1,0:T(8,128)S(1)} %shard_map.130.refs_0_), channel_id=1, source_target_pairs={{0,32},{16,48},{32,0},{48,16},{64,96},{80,112},{96,64},{112,80},{1... | collective-permute-start | bytes 196616 | tf_op jit(solution)/shard_map/ppermute | solution.py:444
  65.7 5.5 %copy-start.3 = (f32[7,128,128]{2,1,0:T(8,128)S(1)}, f32[7,128,128]{2,1,0:T(8,128)}, u32[]{:S(2)}) copy-start(f32[7,128,128]{2,1,0:T(8,128)} %constant.20.clone.refs_4_) | copy-start | bytes 1376260
  65.7 23.5 %copy-start.5 = (f32[64,256]{1,0:T(8,128)S(1)}, f32[64,256]{1,0:T(8,128)}, u32[]{:S(2)}) copy-start(f32[64,256]{1,0:T(8,128)} %constant.17.clone.table_z) | copy-start | bytes 196612
  67.6 2.2 %collective-permute-start.16 = (f32[128,128]{1,0:T(8,128)S(1)}, f32[128,128]{1,0:T(8,128)S(1)}, u32[]{:S(2)}, u32[]{:S(2)}) collective-permute-start(f32[128,128]{1,0:T(8,128)S(1)} %shard_map.130.refs_0_), channel_id=1, source_target_pairs={{0,16},{16,0},{32,48},{48,32},{64,80},{80,64},{96,112},{112,96},{1... | collective-permute-start | bytes 196616 | tf_op jit(solution)/shard_map/ppermute | solution.py:445
  69.9 1.3 %collective-permute-start.18 = (f32[128,128]{1,0:T(8,128)S(1)}, f32[128,128]{1,0:T(8,128)S(1)}, u32[]{:S(2)}, u32[]{:S(2)}) collective-permute-start(f32[128,128]{1,0:T(8,128)S(1)} %collective-permute-done.17.refs_2_), channel_id=1, source_target_pairs={{0,16},{16,0},{32,48},{48,32},{64,80},{80,64},{96,112},{112,96},{1... | collective-permute-start | bytes 196616 | tf_op jit(solution)/shard_map/ppermute | solution.py:447
